TPU v7x, 512 devices: a whole 4x8x8 slice. The times are simulated.
512 devices in a mesh: grp: 4 (over x), gx: 32 (over z, y_hi), gy: 4 (over y_lo, core).
Axes of the slice: x: 4, y: 8 (y_hi: 4, y_lo: 2; y = y_hi * 2 + y_lo), z: 8, core: 2. Of those that a mesh axis runs over, the one named last changes fastest.
Arguments:
- forcing: float32 [512, 64, 512], P('gx', 'gy', 'grp'), may hold values from -8 to 8
- kappa: float32 [512, 64, 512], P('gx', 'gy', 'grp'), may hold values from 0.5 to 8
Outputs:
- solution: float32 [512, 64, 512], P('gx', 'gy', 'grp')
- residual: float32 [512, 64, 512], P('gx', 'gy', 'grp')
All inputs are finite; a program needn't handle non-finite values.
Results may differ from a plain program's by a relative error of at most 0.0001.
Values sent between devices are 32-bit elements; how exact they have to be, the bound alone decides.
No kernel may reach another device: no remote copies, remote signals or barrier semaphores. Data moves between devices by JAX's collectives and lax.ppermute only.
A program may use at most 64 MiB of HBM per device.

v0:
```python
import jax
import jax.numpy as jnp
from jax import lax
from jax.sharding import PartitionSpec as P

ITERS = 2


def with_halo(value, sides, width):
    for axis, dim in sides:
        size, length = (lax.axis_size(axis), value.shape[dim])
        up = [(i, (i + 1) % size) for i in range(size - 1)]
        down = [(j, i) for i, j in up]
        last = lax.slice_in_dim(value, length - width, length, axis=dim)
        first = lax.slice_in_dim(value, 0, width, axis=dim)
        before = lax.ppermute(last, axis, up)
        after = lax.ppermute(first, axis, down)
        value = jnp.concatenate([before, value, after], axis=dim)
    return value


def smooth_sum(padded):
    first = 0.5 * padded[:-2] + padded[1:-1] + 0.5 * padded[2:]
    second = 0.5 * first[:, :-2] + first[:, 1:-1] + 0.5 * first[:, 2:]
    return 0.5 * second[:, :, :-2] + second[:, :, 1:-1] + 0.5 * second[:, :, 2:]


def stencil(padded, coef):
    inner = padded[1:-1, 1:-1, 1:-1]
    return coef * (16.0 * inner - 2.0 * smooth_sum(padded)) + inner


def sweeps(rhs, coef, border):
    diag = 14.0 * coef + 1.0
    error = 0.8 * rhs / diag
    for sweep in range(2):
        error = error + 0.8 * (rhs - stencil(border(error), coef)) / diag
    return error


def restrict(field):
    sx, sy, sz = field.shape
    return field.reshape(sx // 2, 2, sy // 2, 2, sz // 2, 2).mean(axis=(1, 3, 5))


def prolong(field):
    return jnp.repeat(jnp.repeat(jnp.repeat(field, 2, axis=0), 2, axis=1), 2, axis=2)


def fine_state(field):
    return with_halo(field, (("gx", 0), ("gy", 1), ("grp", 2)), 1)


def middle_border(field):
    return with_halo(field, (("gx", 0), ("gy", 1), ("grp", 2)), 1)


def shards(forcing, kappa):
    kappa2 = restrict(kappa)
    kappa3 = restrict(kappa2)
    coef2 = kappa2 * 0.25
    coef3 = kappa3 * 0.0625

    def fine_border(field):
        return with_halo(field, (("gx", 0), ("gy", 1), ("grp", 2)), 1)

    def bottom_border(field):
        return with_halo(field, (("gx", 0), ("gy", 1), ("grp", 2)), 1)

    solution = jnp.zeros_like(forcing)
    for step in range(ITERS):
        if step == 0:
            resid = forcing
        else:
            resid = forcing - stencil(fine_state(solution), kappa)
        second = restrict(resid)
        error1 = sweeps(resid, kappa, fine_border)
        coarse_third = restrict(second)
        error2 = sweeps(second, coef2, middle_border)
        error3 = sweeps(coarse_third, coef3, bottom_border)
        solution = solution + error1 + prolong(error2 + prolong(error3))
    residual = forcing - stencil(fine_state(solution), kappa)
    return (solution, residual)


def solution(mesh):
    placed = (P("gx", "gy", "grp"), P("gx", "gy", "grp"))
    return jax.shard_map(
        shards,
        mesh=mesh,
        in_specs=placed,
        out_specs=(P("gx", "gy", "grp"), P("gx", "gy", "grp")),
        check_vma=False,
    )
```

profile of v0, /device:TPU:262, one launch (start us, length us, event | category | flops | bytes accessed | tf_op | source)
XLA Modules:
  0.0 407.9 jit_solution(6993022681163228196)
XLA Ops:
  0.6 10.6 %reshape.61 = f32[8,2,8,2,64,2]{5,4,3,2,1,0:T(8,128)} reshape(f32[16,16,128]{2,1,0:T(8,128)} %param.2) | data formatting | bytes 262144 | tf_op jit(solution)/shard_map/reshape | solution.py:43
  11.2 9.7 %reshape.62 = f32[8,2,8,2,64,2]{5,4,3,2,1,0:T(8,128)} reshape(f32[16,16,128]{2,1,0:T(8,128)S(1)} %copy-done) | data formatting | bytes 262144 | tf_op jit(solution)/shard_map/reshape | solution.py:43
  20.9 4.0 reduce_sum.54
  25.0 4.0 reduce_sum.55
  29.1 5.3 %collective-permute-start.13 = (f32[1,8,64]{2,1,0:T(8,128)S(1)}, f32[1,8,64]{2,1,0:T(8,128)S(1)}, u32[]{:S(2)}, u32[]{:S(2)}) collective-permute-start(f32[1,8,64]{2,1,0:T(8,128)S(1)} %get-tuple-element.74), channel_id=1, source_target_pairs={{4,0},{8,4},{12,8},{16,12},{20,16},{24,20},{28,24},{32,28},{36,32}... | collective-permute-start | bytes 6152 | tf_op jit(solution)/shard_map/ppermute | solution.py:17
  36.3 7.8 %collective-permute-done.12 = f32[1,8,64]{2,1,0:T(8,128)S(1)} collective-permute-done((f32[1,8,64]{2,1,0:T(8,128)S(1)}, f32[1,8,64]{2,1,0:T(8,128)S(1)}, u32[]{:S(2)}, u32[]{:S(2)}) %collective-permute-start.12) | collective-permute-done | bytes 2080 | tf_op jit(solution)/shard_map/ppermute | solution.py:16
  54.2 4.1 %collective-permute-done.16 = f32[10,10,1]{2,1,0:T(8,128)S(1)} collective-permute-done((f32[10,10,1]{2,1,0:T(8,128)S(1)}, f32[10,10,1]{2,1,0:T(8,128)S(1)}, u32[]{:S(2)}, u32[]{:S(2)}) %collective-permute-start.16) | collective-permute-done | bytes 432 | tf_op jit(solution)/shard_map/ppermute | solution.py:16
  63.1 4.8 %collective-permute-start.24 = (f32[1,4,32]{2,1,0:T(4,128)S(1)}, f32[1,4,32]{2,1,0:T(4,128)S(1)}, u32[]{:S(2)}, u32[]{:S(2)}) collective-permute-start(f32[1,4,32]{2,1,0:T(4,128)S(1)} %get-tuple-element.97), channel_id=1, source_target_pairs={{0,4},{4,8},{8,12},{12,16},{16,20},{20,24},{24,28},{28,32},{32,36}... | collective-permute-start | bytes 1544 | tf_op jit(solution)/shard_map/ppermute | solution.py:16
  68.0 4.8 %collective-permute-done.24 = f32[1,4,32]{2,1,0:T(4,128)S(1)} collective-permute-done((f32[1,4,32]{2,1,0:T(4,128)S(1)}, f32[1,4,32]{2,1,0:T(4,128)S(1)}, u32[]{:S(2)}, u32[]{:S(2)}) %collective-permute-start.24) | collective-permute-done | bytes 544 | tf_op jit(solution)/shard_map/ppermute | solution.py:16
  83.0 4.8 %collective-permute-start = (f32[1,16,128]{2,1,0:T(8,128)S(1)}, f32[1,16,128]{2,1,0:T(8,128)S(1)}, u32[]{:S(2)}, u32[]{:S(2)}) collective-permute-start(f32[1,16,128]{2,1,0:T(8,128)S(1)} %get-tuple-element.44), channel_id=1, source_target_pairs={{0,4},{4,8},{8,12},{12,16},{16,20},{20,24},{24,28},{28,32},{32,36}... | collective-permute-start | bytes 24584 | tf_op jit(solution)/shard_map/ppermute | solution.py:16
  88.0 5.2 %collective-permute-start.31 = (f32[1,4,32]{2,1,0:T(4,128)S(1)}, f32[1,4,32]{2,1,0:T(4,128)S(1)}, u32[]{:S(2)}, u32[]{:S(2)}) collective-permute-start(f32[1,4,32]{2,1,0:T(4,128)S(1)} %get-tuple-element.96), channel_id=1, source_target_pairs={{4,0},{8,4},{12,8},{16,12},{20,16},{24,20},{28,24},{32,28},{36,32}... | collective-permute-start | bytes 1544 | tf_op jit(solution)/shard_map/ppermute | solution.py:17
  95.2 8.1 %collective-permute-start.19 = (f32[1,8,64]{2,1,0:T(8,128)S(1)}, f32[1,8,64]{2,1,0:T(8,128)S(1)}, u32[]{:S(2)}, u32[]{:S(2)}) collective-permute-start(f32[1,8,64]{2,1,0:T(8,128)S(1)} %get-tuple-element.69), channel_id=1, source_target_pairs={{4,0},{8,4},{12,8},{16,12},{20,16},{24,20},{28,24},{32,28},{36,32}... | collective-permute-start | bytes 6152 | tf_op jit(solution)/shard_map/ppermute | solution.py:17
  114.5 4.5 %collective-permute-start.35 = (f32[6,6,1]{2,1,0:T(8,128)S(1)}, f32[6,6,1]{2,1,0:T(8,128)S(1)}, u32[]{:S(2)}, u32[]{:S(2)}) collective-permute-start(f32[6,6,1]{2,1,0:T(8,128)S(1)} %get-tuple-element.80), channel_id=1, source_target_pairs={{128,0},{256,128},{384,256},{129,1},{257,129},{385,257},{130,2},{2... | collective-permute-start | bytes 440 | tf_op jit(solution)/shard_map/ppermute | solution.py:17
  126.8 3.8 collective-permute-start.2
  130.7 4.4 %collective-permute-start.23 = (f32[10,10,1]{2,1,0:T(8,128)S(1)}, f32[10,10,1]{2,1,0:T(8,128)S(1)}, u32[]{:S(2)}, u32[]{:S(2)}) collective-permute-start(f32[10,10,1]{2,1,0:T(8,128)S(1)} %get-tuple-element.51), channel_id=1, source_target_pairs={{128,0},{256,128},{384,256},{129,1},{257,129},{385,257},{130,2},{2... | collective-permute-start | bytes 1208 | tf_op jit(solution)/shard_map/ppermute | solution.py:17
  136.6 4.6 %collective-permute-start.5 = (f32[18,18,1]{2,1,0:T(8,128)S(1)}, f32[18,18,1]{2,1,0:T(8,128)S(1)}, u32[]{:S(2)}, u32[]{:S(2)}) collective-permute-start(f32[18,18,1]{2,1,0:T(8,128)S(1)} %get-tuple-element.21), channel_id=1, source_target_pairs={{128,0},{256,128},{384,256},{129,1},{257,129},{385,257},{130,2},{2... | collective-permute-start | bytes 3896 | tf_op jit(solution)/shard_map/ppermute | solution.py:17
  142.6 4.1 %collective-permute-done.5 = f32[18,18,1]{2,1,0:T(8,128)S(1)} collective-permute-done((f32[18,18,1]{2,1,0:T(8,128)S(1)}, f32[18,18,1]{2,1,0:T(8,128)S(1)}, u32[]{:S(2)}, u32[]{:S(2)}) %collective-permute-start.5) | collective-permute-done | bytes 1328 | tf_op jit(solution)/shard_map/ppermute | solution.py:17
  146.8 4.5 %collective-permute-done.4 = f32[18,18,1]{2,1,0:T(8,128)S(1)} collective-permute-done((f32[18,18,1]{2,1,0:T(8,128)S(1)}, f32[18,18,1]{2,1,0:T(8,128)S(1)}, u32[]{:S(2)}, u32[]{:S(2)}) %collective-permute-start.4) | collective-permute-done | bytes 1328 | tf_op jit(solution)/shard_map/ppermute | solution.py:16
  151.9 6.0 %collective-permute-start.7 = (f32[1,16,128]{2,1,0:T(8,128)S(1)}, f32[1,16,128]{2,1,0:T(8,128)S(1)}, u32[]{:S(2)}, u32[]{:S(2)}) collective-permute-start(f32[1,16,128]{2,1,0:T(8,128)S(1)} %get-tuple-element.43), channel_id=1, source_target_pairs={{4,0},{8,4},{12,8},{16,12},{20,16},{24,20},{28,24},{32,28},{36,32}... | collective-permute-start | bytes 24584 | tf_op jit(solution)/shard_map/ppermute | solution.py:17
  159.9 7.8 %collective-permute-done.6 = f32[1,16,128]{2,1,0:T(8,128)S(1)} collective-permute-done((f32[1,16,128]{2,1,0:T(8,128)S(1)}, f32[1,16,128]{2,1,0:T(8,128)S(1)}, u32[]{:S(2)}, u32[]{:S(2)}) %collective-permute-start.6) | collective-permute-done | bytes 8224 | tf_op jit(solution)/shard_map/ppermute | solution.py:16
  180.6 4.1 %collective-permute-done.10 = f32[18,18,1]{2,1,0:T(8,128)S(1)} collective-permute-done((f32[18,18,1]{2,1,0:T(8,128)S(1)}, f32[18,18,1]{2,1,0:T(8,128)S(1)}, u32[]{:S(2)}, u32[]{:S(2)}) %collective-permute-start.10) | collective-permute-done | bytes 1328 | tf_op jit(solution)/shard_map/ppermute | solution.py:16
  187.3 4.8 %collective-permute-start.36 = (f32[1,16,128]{2,1,0:T(8,128)S(1)}, f32[1,16,128]{2,1,0:T(8,128)S(1)}, u32[]{:S(2)}, u32[]{:S(2)}) collective-permute-start(f32[1,16,128]{2,1,0:T(8,128)S(1)} %get-tuple-element.40), channel_id=1, source_target_pairs={{0,4},{4,8},{8,12},{12,16},{16,20},{20,24},{24,28},{28,32},{32,36}... | collective-permute-start | bytes 24584 | tf_op jit(solution)/shard_map/ppermute | solution.py:16
  192.1 4.9 %collective-permute-done.36 = f32[1,16,128]{2,1,0:T(8,128)S(1)} collective-permute-done((f32[1,16,128]{2,1,0:T(8,128)S(1)}, f32[1,16,128]{2,1,0:T(8,128)S(1)}, u32[]{:S(2)}, u32[]{:S(2)}) %collective-permute-start.36) | collective-permute-done | bytes 8224 | tf_op jit(solution)/shard_map/ppermute | solution.py:16
  206.1 3.7 collective-permute-done.41
  209.8 4.1 %collective-permute-done.40 = f32[18,18,1]{2,1,0:T(8,128)S(1)} collective-permute-done((f32[18,18,1]{2,1,0:T(8,128)S(1)}, f32[18,18,1]{2,1,0:T(8,128)S(1)}, u32[]{:S(2)}, u32[]{:S(2)}) %collective-permute-start.40) | collective-permute-done | bytes 1328 | tf_op jit(solution)/shard_map/ppermute | solution.py:16
  214.5 9.8 %reshape.69 = f32[8,2,8,2,64,2]{5,4,3,2,1,0:T(8,128)} reshape(f32[16,16,128]{2,1,0:T(8,128)S(1)} %get-tuple-element.9) | data formatting | bytes 262144 | tf_op jit(solution)/shard_map/reshape | solution.py:43
  224.3 4.0 reduce_sum.58
  230.3 4.8 %collective-permute-start.54 = (f32[1,8,64]{2,1,0:T(8,128)S(1)}, f32[1,8,64]{2,1,0:T(8,128)S(1)}, u32[]{:S(2)}, u32[]{:S(2)}) collective-permute-start(f32[1,8,64]{2,1,0:T(8,128)S(1)} %get-tuple-element.66), channel_id=1, source_target_pairs={{0,4},{4,8},{8,12},{12,16},{16,20},{20,24},{24,28},{28,32},{32,36}... | collective-permute-start | bytes 6152 | tf_op jit(solution)/shard_map/ppermute | solution.py:16
  235.1 4.9 %collective-permute-done.54 = f32[1,8,64]{2,1,0:T(8,128)S(1)} collective-permute-done((f32[1,8,64]{2,1,0:T(8,128)S(1)}, f32[1,8,64]{2,1,0:T(8,128)S(1)}, u32[]{:S(2)}, u32[]{:S(2)}) %collective-permute-start.54) | collective-permute-done | bytes 2080 | tf_op jit(solution)/shard_map/ppermute | solution.py:16
  249.7 4.1 %collective-permute-done.58 = f32[10,10,1]{2,1,0:T(8,128)S(1)} collective-permute-done((f32[10,10,1]{2,1,0:T(8,128)S(1)}, f32[10,10,1]{2,1,0:T(8,128)S(1)}, u32[]{:S(2)}, u32[]{:S(2)}) %collective-permute-start.58) | collective-permute-done | bytes 432 | tf_op jit(solution)/shard_map/ppermute | solution.py:16
  257.3 4.8 %collective-permute-start.66 = (f32[1,4,32]{2,1,0:T(4,128)S(1)}, f32[1,4,32]{2,1,0:T(4,128)S(1)}, u32[]{:S(2)}, u32[]{:S(2)}) collective-permute-start(f32[1,4,32]{2,1,0:T(4,128)S(1)} %get-tuple-element.93), channel_id=1, source_target_pairs={{0,4},{4,8},{8,12},{12,16},{16,20},{20,24},{24,28},{28,32},{32,36}... | collective-permute-start | bytes 1544 | tf_op jit(solution)/shard_map/ppermute | solution.py:16
  262.1 4.9 %collective-permute-done.66 = f32[1,4,32]{2,1,0:T(4,128)S(1)} collective-permute-done((f32[1,4,32]{2,1,0:T(4,128)S(1)}, f32[1,4,32]{2,1,0:T(4,128)S(1)}, u32[]{:S(2)}, u32[]{:S(2)}) %collective-permute-start.66) | collective-permute-done | bytes 544 | tf_op jit(solution)/shard_map/ppermute | solution.py:16
  276.9 4.8 %collective-permute-start.42 = (f32[1,16,128]{2,1,0:T(8,128)S(1)}, f32[1,16,128]{2,1,0:T(8,128)S(1)}, u32[]{:S(2)}, u32[]{:S(2)}) collective-permute-start(f32[1,16,128]{2,1,0:T(8,128)S(1)} %get-tuple-element.38), channel_id=1, source_target_pairs={{0,4},{4,8},{8,12},{12,16},{16,20},{20,24},{24,28},{28,32},{32,36}... | collective-permute-start | bytes 24584 | tf_op jit(solution)/shard_map/ppermute | solution.py:16
  281.9 5.2 %collective-permute-start.73 = (f32[1,4,32]{2,1,0:T(4,128)S(1)}, f32[1,4,32]{2,1,0:T(4,128)S(1)}, u32[]{:S(2)}, u32[]{:S(2)}) collective-permute-start(f32[1,4,32]{2,1,0:T(4,128)S(1)} %get-tuple-element.92), channel_id=1, source_target_pairs={{4,0},{8,4},{12,8},{16,12},{20,16},{24,20},{28,24},{32,28},{36,32}... | collective-permute-start | bytes 1544 | tf_op jit(solution)/shard_map/ppermute | solution.py:17
  289.1 8.1 %collective-permute-start.61 = (f32[1,8,64]{2,1,0:T(8,128)S(1)}, f32[1,8,64]{2,1,0:T(8,128)S(1)}, u32[]{:S(2)}, u32[]{:S(2)}) collective-permute-start(f32[1,8,64]{2,1,0:T(8,128)S(1)} %get-tuple-element.63), channel_id=1, source_target_pairs={{4,0},{8,4},{12,8},{16,12},{20,16},{24,20},{28,24},{32,28},{36,32}... | collective-permute-start | bytes 6152 | tf_op jit(solution)/shard_map/ppermute | solution.py:17
  303.6 3.4 collective-permute-done.60
  308.4 4.5 %collective-permute-start.77 = (f32[6,6,1]{2,1,0:T(8,128)S(1)}, f32[6,6,1]{2,1,0:T(8,128)S(1)}, u32[]{:S(2)}, u32[]{:S(2)}) collective-permute-start(f32[6,6,1]{2,1,0:T(8,128)S(1)} %get-tuple-element.76), channel_id=1, source_target_pairs={{128,0},{256,128},{384,256},{129,1},{257,129},{385,257},{130,2},{2... | collective-permute-start | bytes 440 | tf_op jit(solution)/shard_map/ppermute | solution.py:17
  324.1 4.4 %collective-permute-start.65 = (f32[10,10,1]{2,1,0:T(8,128)S(1)}, f32[10,10,1]{2,1,0:T(8,128)S(1)}, u32[]{:S(2)}, u32[]{:S(2)}) collective-permute-start(f32[10,10,1]{2,1,0:T(8,128)S(1)} %get-tuple-element.47), channel_id=1, source_target_pairs={{128,0},{256,128},{384,256},{129,1},{257,129},{385,257},{130,2},{2... | collective-permute-start | bytes 1208 | tf_op jit(solution)/shard_map/ppermute | solution.py:17
  330.0 4.6 %collective-permute-start.47 = (f32[18,18,1]{2,1,0:T(8,128)S(1)}, f32[18,18,1]{2,1,0:T(8,128)S(1)}, u32[]{:S(2)}, u32[]{:S(2)}) collective-permute-start(f32[18,18,1]{2,1,0:T(8,128)S(1)} %get-tuple-element.15), channel_id=1, source_target_pairs={{128,0},{256,128},{384,256},{129,1},{257,129},{385,257},{130,2},{2... | collective-permute-start | bytes 3896 | tf_op jit(solution)/shard_map/ppermute | solution.py:17
  336.0 4.1 %collective-permute-done.47 = f32[18,18,1]{2,1,0:T(8,128)S(1)} collective-permute-done((f32[18,18,1]{2,1,0:T(8,128)S(1)}, f32[18,18,1]{2,1,0:T(8,128)S(1)}, u32[]{:S(2)}, u32[]{:S(2)}) %collective-permute-start.47) | collective-permute-done | bytes 1328 | tf_op jit(solution)/shard_map/ppermute | solution.py:17
  340.2 4.5 %collective-permute-done.46 = f32[18,18,1]{2,1,0:T(8,128)S(1)} collective-permute-done((f32[18,18,1]{2,1,0:T(8,128)S(1)}, f32[18,18,1]{2,1,0:T(8,128)S(1)}, u32[]{:S(2)}, u32[]{:S(2)}) %collective-permute-start.46) | collective-permute-done | bytes 1328 | tf_op jit(solution)/shard_map/ppermute | solution.py:16
  345.3 6.0 %collective-permute-start.49 = (f32[1,16,128]{2,1,0:T(8,128)S(1)}, f32[1,16,128]{2,1,0:T(8,128)S(1)}, u32[]{:S(2)}, u32[]{:S(2)}) collective-permute-start(f32[1,16,128]{2,1,0:T(8,128)S(1)} %get-tuple-element.37), channel_id=1, source_target_pairs={{4,0},{8,4},{12,8},{16,12},{20,16},{24,20},{28,24},{32,28},{36,32}... | collective-permute-start | bytes 24584 | tf_op jit(solution)/shard_map/ppermute | solution.py:17
  353.3 7.8 %collective-permute-done.48 = f32[1,16,128]{2,1,0:T(8,128)S(1)} collective-permute-done((f32[1,16,128]{2,1,0:T(8,128)S(1)}, f32[1,16,128]{2,1,0:T(8,128)S(1)}, u32[]{:S(2)}, u32[]{:S(2)}) %collective-permute-start.48) | collective-permute-done | bytes 8224 | tf_op jit(solution)/shard_map/ppermute | solution.py:16
  373.4 4.1 %collective-permute-done.52 = f32[18,18,1]{2,1,0:T(8,128)S(1)} collective-permute-done((f32[18,18,1]{2,1,0:T(8,128)S(1)}, f32[18,18,1]{2,1,0:T(8,128)S(1)}, u32[]{:S(2)}, u32[]{:S(2)}) %collective-permute-start.52) | collective-permute-done | bytes 1328 | tf_op jit(solution)/shard_map/ppermute | solution.py:16
  380.1 4.8 %collective-permute-start.78 = (f32[1,16,128]{2,1,0:T(8,128)S(1)}, f32[1,16,128]{2,1,0:T(8,128)S(1)}, u32[]{:S(2)}, u32[]{:S(2)}) collective-permute-start(f32[1,16,128]{2,1,0:T(8,128)S(1)} %get-tuple-element.34), channel_id=1, source_target_pairs={{0,4},{4,8},{8,12},{12,16},{16,20},{20,24},{24,28},{28,32},{32,36}... | collective-permute-start | bytes 24584 | tf_op jit(solution)/shard_map/ppermute | solution.py:16
  384.9 4.9 %collective-permute-done.78 = f32[1,16,128]{2,1,0:T(8,128)S(1)} collective-permute-done((f32[1,16,128]{2,1,0:T(8,128)S(1)}, f32[1,16,128]{2,1,0:T(8,128)S(1)}, u32[]{:S(2)}, u32[]{:S(2)}) %collective-permute-start.78) | collective-permute-done | bytes 8224 | tf_op jit(solution)/shard_map/ppermute | solution.py:16
  398.7 3.9 collective-permute-done.83
  402.5 4.1 %collective-permute-done.82 = f32[18,18,1]{2,1,0:T(8,128)S(1)} collective-permute-done((f32[18,18,1]{2,1,0:T(8,128)S(1)}, f32[18,18,1]{2,1,0:T(8,128)S(1)}, u32[]{:S(2)}, u32[]{:S(2)}) %collective-permute-start.82) | collective-permute-done | bytes 1328 | tf_op jit(solution)/shard_map/ppermute | solution.py:16
  (279 shorter events, 153.8 us)
Async XLA Ops:
  34.3 9.7 %collective-permute-start.12 = (f32[1,8,64]{2,1,0:T(8,128)S(1)}, f32[1,8,64]{2,1,0:T(8,128)S(1)}, u32[]{:S(2)}, u32[]{:S(2)}) collective-permute-start(f32[1,8,64]{2,1,0:T(8,128)S(1)} %get-tuple-element.73), channel_id=1, source_target_pairs={{0,4},{4,8},{8,12},{12,16},{16,20},{20,24},{24,28},{28,32},{32,36}... | collective-permute-start | bytes 6152 | tf_op jit(solution)/shard_map/ppermute | solution.py:16
  63.1 9.7 %collective-permute-start.24 = (f32[1,4,32]{2,1,0:T(4,128)S(1)}, f32[1,4,32]{2,1,0:T(4,128)S(1)}, u32[]{:S(2)}, u32[]{:S(2)}) collective-permute-start(f32[1,4,32]{2,1,0:T(4,128)S(1)} %get-tuple-element.97), channel_id=1, source_target_pairs={{0,4},{4,8},{8,12},{12,16},{16,20},{20,24},{24,28},{28,32},{32,36}... | collective-permute-start | bytes 1544 | tf_op jit(solution)/shard_map/ppermute | solution.py:16
  77.2 48.3 %collective-permute-start.1 = (f32[1,16,128]{2,1,0:T(8,128)S(1)}, f32[1,16,128]{2,1,0:T(8,128)S(1)}, u32[]{:S(2)}, u32[]{:S(2)}) collective-permute-start(f32[1,16,128]{2,1,0:T(8,128)S(1)} %get-tuple-element.45), channel_id=1, source_target_pairs={{4,0},{8,4},{12,8},{16,12},{20,16},{24,20},{28,24},{32,28},{36,32}... | collective-permute-start | bytes 24584 | tf_op jit(solution)/shard_map/ppermute | solution.py:17
  79.2 8.6 %collective-permute-start.29 = (f32[6,6,1]{2,1,0:T(8,128)S(1)}, f32[6,6,1]{2,1,0:T(8,128)S(1)}, u32[]{:S(2)}, u32[]{:S(2)}) collective-permute-start(f32[6,6,1]{2,1,0:T(8,128)S(1)} %get-tuple-element.82), channel_id=1, source_target_pairs={{128,0},{256,128},{384,256},{129,1},{257,129},{385,257},{130,2},{2... | collective-permute-start | bytes 440 | tf_op jit(solution)/shard_map/ppermute | solution.py:17
  83.0 42.5 %collective-permute-start = (f32[1,16,128]{2,1,0:T(8,128)S(1)}, f32[1,16,128]{2,1,0:T(8,128)S(1)}, u32[]{:S(2)}, u32[]{:S(2)}) collective-permute-start(f32[1,16,128]{2,1,0:T(8,128)S(1)} %get-tuple-element.44), channel_id=1, source_target_pairs={{0,4},{4,8},{8,12},{12,16},{16,20},{20,24},{24,28},{28,32},{32,36}... | collective-permute-start | bytes 24584 | tf_op jit(solution)/shard_map/ppermute | solution.py:16
  88.0 15.3 %collective-permute-start.31 = (f32[1,4,32]{2,1,0:T(4,128)S(1)}, f32[1,4,32]{2,1,0:T(4,128)S(1)}, u32[]{:S(2)}, u32[]{:S(2)}) collective-permute-start(f32[1,4,32]{2,1,0:T(4,128)S(1)} %get-tuple-element.96), channel_id=1, source_target_pairs={{4,0},{8,4},{12,8},{16,12},{20,16},{24,20},{28,24},{32,28},{36,32}... | collective-permute-start | bytes 1544 | tf_op jit(solution)/shard_map/ppermute | solution.py:17
  93.3 12.0 %collective-permute-start.30 = (f32[1,4,32]{2,1,0:T(4,128)S(1)}, f32[1,4,32]{2,1,0:T(4,128)S(1)}, u32[]{:S(2)}, u32[]{:S(2)}) collective-permute-start(f32[1,4,32]{2,1,0:T(4,128)S(1)} %get-tuple-element.95), channel_id=1, source_target_pairs={{0,4},{4,8},{8,12},{12,16},{16,20},{20,24},{24,28},{28,32},{32,36}... | collective-permute-start | bytes 1544 | tf_op jit(solution)/shard_map/ppermute | solution.py:16
  95.2 11.4 %collective-permute-start.19 = (f32[1,8,64]{2,1,0:T(8,128)S(1)}, f32[1,8,64]{2,1,0:T(8,128)S(1)}, u32[]{:S(2)}, u32[]{:S(2)}) collective-permute-start(f32[1,8,64]{2,1,0:T(8,128)S(1)} %get-tuple-element.69), channel_id=1, source_target_pairs={{4,0},{8,4},{12,8},{16,12},{20,16},{24,20},{28,24},{32,28},{36,32}... | collective-permute-start | bytes 6152 | tf_op jit(solution)/shard_map/ppermute | solution.py:17
  103.4 9.7 %collective-permute-start.18 = (f32[1,8,64]{2,1,0:T(8,128)S(1)}, f32[1,8,64]{2,1,0:T(8,128)S(1)}, u32[]{:S(2)}, u32[]{:S(2)}) collective-permute-start(f32[1,8,64]{2,1,0:T(8,128)S(1)} %get-tuple-element.68), channel_id=1, source_target_pairs={{0,4},{4,8},{8,12},{12,16},{16,20},{20,24},{24,28},{28,32},{32,36}... | collective-permute-start | bytes 6152 | tf_op jit(solution)/shard_map/ppermute | solution.py:16
  105.3 9.1 %collective-permute-start.33 = (f32[6,1,32]{2,1,0:T(1,128)S(1)}, f32[6,1,32]{2,1,0:T(1,128)S(1)}, u32[]{:S(2)}, u32[]{:S(2)}) collective-permute-start(f32[6,1,32]{2,1,0:T(1,128)S(1)} %get-tuple-element.88), channel_id=1, source_target_pairs={{1,0},{2,1},{3,2},{5,4},{6,5},{7,6},{9,8},{10,9},{11,10},{13,12},{... | collective-permute-start | bytes 2312 | tf_op jit(solution)/shard_map/ppermute | solution.py:17
  106.7 7.8 %collective-permute-start.32 = (f32[6,1,32]{2,1,0:T(1,128)S(1)}, f32[6,1,32]{2,1,0:T(1,128)S(1)}, u32[]{:S(2)}, u32[]{:S(2)}) collective-permute-start(f32[6,1,32]{2,1,0:T(1,128)S(1)} %get-tuple-element.87), channel_id=1, source_target_pairs={{0,1},{1,2},{2,3},{4,5},{5,6},{6,7},{8,9},{9,10},{10,11},{12,13},{... | collective-permute-start | bytes 2312 | tf_op jit(solution)/shard_map/ppermute | solution.py:16
  113.1 17.5 %collective-permute-start.21 = (f32[10,1,64]{2,1,0:T(1,128)S(1)}, f32[10,1,64]{2,1,0:T(1,128)S(1)}, u32[]{:S(2)}, u32[]{:S(2)}) collective-permute-start(f32[10,1,64]{2,1,0:T(1,128)S(1)} %get-tuple-element.59), channel_id=1, source_target_pairs={{1,0},{2,1},{3,2},{5,4},{6,5},{7,6},{9,8},{10,9},{11,10},{13,12},{... | collective-permute-start | bytes 7688 | tf_op jit(solution)/shard_map/ppermute | solution.py:17
  120.6 10.0 %collective-permute-start.20 = (f32[10,1,64]{2,1,0:T(1,128)S(1)}, f32[10,1,64]{2,1,0:T(1,128)S(1)}, u32[]{:S(2)}, u32[]{:S(2)}) collective-permute-start(f32[10,1,64]{2,1,0:T(1,128)S(1)} %get-tuple-element.58), channel_id=1, source_target_pairs={{0,1},{1,2},{2,3},{4,5},{5,6},{6,7},{8,9},{9,10},{10,11},{12,13},{... | collective-permute-start | bytes 7688 | tf_op jit(solution)/shard_map/ppermute | solution.py:16
  125.5 10.9 %collective-permute-start.3 = (f32[18,1,128]{2,1,0:T(1,128)S(1)}, f32[18,1,128]{2,1,0:T(1,128)S(1)}, u32[]{:S(2)}, u32[]{:S(2)}) collective-permute-start(f32[18,1,128]{2,1,0:T(1,128)S(1)} %get-tuple-element.33), channel_id=1, source_target_pairs={{1,0},{2,1},{3,2},{5,4},{6,5},{7,6},{9,8},{10,9},{11,10},{13,12},{... | collective-permute-start | bytes 27656 | tf_op jit(solution)/shard_map/ppermute | solution.py:17
  126.8 9.6 %collective-permute-start.2 = (f32[18,1,128]{2,1,0:T(1,128)S(1)}, f32[18,1,128]{2,1,0:T(1,128)S(1)}, u32[]{:S(2)}, u32[]{:S(2)}) collective-permute-start(f32[18,1,128]{2,1,0:T(1,128)S(1)} %get-tuple-element.32), channel_id=1, source_target_pairs={{0,1},{1,2},{2,3},{4,5},{5,6},{6,7},{8,9},{9,10},{10,11},{12,13},{... | collective-permute-start | bytes 27656 | tf_op jit(solution)/shard_map/ppermute | solution.py:16
  130.7 11.7 %collective-permute-start.23 = (f32[10,10,1]{2,1,0:T(8,128)S(1)}, f32[10,10,1]{2,1,0:T(8,128)S(1)}, u32[]{:S(2)}, u32[]{:S(2)}) collective-permute-start(f32[10,10,1]{2,1,0:T(8,128)S(1)} %get-tuple-element.51), channel_id=1, source_target_pairs={{128,0},{256,128},{384,256},{129,1},{257,129},{385,257},{130,2},{2... | collective-permute-start | bytes 1208 | tf_op jit(solution)/shard_map/ppermute | solution.py:17
  136.6 10.1 %collective-permute-start.5 = (f32[18,18,1]{2,1,0:T(8,128)S(1)}, f32[18,18,1]{2,1,0:T(8,128)S(1)}, u32[]{:S(2)}, u32[]{:S(2)}) collective-permute-start(f32[18,18,1]{2,1,0:T(8,128)S(1)} %get-tuple-element.21), channel_id=1, source_target_pairs={{128,0},{256,128},{384,256},{129,1},{257,129},{385,257},{130,2},{2... | collective-permute-start | bytes 3896 | tf_op jit(solution)/shard_map/ppermute | solution.py:17
  141.2 10.1 %collective-permute-start.4 = (f32[18,18,1]{2,1,0:T(8,128)S(1)}, f32[18,18,1]{2,1,0:T(8,128)S(1)}, u32[]{:S(2)}, u32[]{:S(2)}) collective-permute-start(f32[18,18,1]{2,1,0:T(8,128)S(1)} %get-tuple-element.20), channel_id=1, source_target_pairs={{0,128},{128,256},{256,384},{1,129},{129,257},{257,385},{2,130},{1... | collective-permute-start | bytes 3896 | tf_op jit(solution)/shard_map/ppermute | solution.py:16
  151.9 7.9 %collective-permute-start.7 = (f32[1,16,128]{2,1,0:T(8,128)S(1)}, f32[1,16,128]{2,1,0:T(8,128)S(1)}, u32[]{:S(2)}, u32[]{:S(2)}) collective-permute-start(f32[1,16,128]{2,1,0:T(8,128)S(1)} %get-tuple-element.43), channel_id=1, source_target_pairs={{4,0},{8,4},{12,8},{16,12},{20,16},{24,20},{28,24},{32,28},{36,32}... | collective-permute-start | bytes 24584 | tf_op jit(solution)/shard_map/ppermute | solution.py:17
  157.9 9.8 %collective-permute-start.6 = (f32[1,16,128]{2,1,0:T(8,128)S(1)}, f32[1,16,128]{2,1,0:T(8,128)S(1)}, u32[]{:S(2)}, u32[]{:S(2)}) collective-permute-start(f32[1,16,128]{2,1,0:T(8,128)S(1)} %get-tuple-element.42), channel_id=1, source_target_pairs={{0,4},{4,8},{8,12},{12,16},{16,20},{20,24},{24,28},{28,32},{32,36}... | collective-permute-start | bytes 24584 | tf_op jit(solution)/shard_map/ppermute | solution.py:16
  173.0 7.6 %collective-permute-start.11 = (f32[18,18,1]{2,1,0:T(8,128)S(1)}, f32[18,18,1]{2,1,0:T(8,128)S(1)}, u32[]{:S(2)}, u32[]{:S(2)}) collective-permute-start(f32[18,18,1]{2,1,0:T(8,128)S(1)} %get-tuple-element.19), channel_id=1, source_target_pairs={{128,0},{256,128},{384,256},{129,1},{257,129},{385,257},{130,2},{2... | collective-permute-start | bytes 3896 | tf_op jit(solution)/shard_map/ppermute | solution.py:17
  175.5 9.3 %collective-permute-start.10 = (f32[18,18,1]{2,1,0:T(8,128)S(1)}, f32[18,18,1]{2,1,0:T(8,128)S(1)}, u32[]{:S(2)}, u32[]{:S(2)}) collective-permute-start(f32[18,18,1]{2,1,0:T(8,128)S(1)} %get-tuple-element.18), channel_id=1, source_target_pairs={{0,128},{128,256},{256,384},{1,129},{129,257},{257,385},{2,130},{1... | collective-permute-start | bytes 3896 | tf_op jit(solution)/shard_map/ppermute | solution.py:16
  187.3 9.8 %collective-permute-start.36 = (f32[1,16,128]{2,1,0:T(8,128)S(1)}, f32[1,16,128]{2,1,0:T(8,128)S(1)}, u32[]{:S(2)}, u32[]{:S(2)}) collective-permute-start(f32[1,16,128]{2,1,0:T(8,128)S(1)} %get-tuple-element.40), channel_id=1, source_target_pairs={{0,4},{4,8},{8,12},{12,16},{16,20},{20,24},{24,28},{28,32},{32,36}... | collective-permute-start | bytes 24584 | tf_op jit(solution)/shard_map/ppermute | solution.py:16
  202.4 7.4 %collective-permute-start.41 = (f32[18,18,1]{2,1,0:T(8,128)S(1)}, f32[18,18,1]{2,1,0:T(8,128)S(1)}, u32[]{:S(2)}, u32[]{:S(2)}) collective-permute-start(f32[18,18,1]{2,1,0:T(8,128)S(1)} %get-tuple-element.17), channel_id=1, source_target_pairs={{128,0},{256,128},{384,256},{129,1},{257,129},{385,257},{130,2},{2... | collective-permute-start | bytes 3896 | tf_op jit(solution)/shard_map/ppermute | solution.py:17
  204.6 9.3 %collective-permute-start.40 = (f32[18,18,1]{2,1,0:T(8,128)S(1)}, f32[18,18,1]{2,1,0:T(8,128)S(1)}, u32[]{:S(2)}, u32[]{:S(2)}) collective-permute-start(f32[18,18,1]{2,1,0:T(8,128)S(1)} %get-tuple-element.16), channel_id=1, source_target_pairs={{0,128},{128,256},{256,384},{1,129},{129,257},{257,385},{2,130},{1... | collective-permute-start | bytes 3896 | tf_op jit(solution)/shard_map/ppermute | solution.py:16
  230.3 9.7 %collective-permute-start.54 = (f32[1,8,64]{2,1,0:T(8,128)S(1)}, f32[1,8,64]{2,1,0:T(8,128)S(1)}, u32[]{:S(2)}, u32[]{:S(2)}) collective-permute-start(f32[1,8,64]{2,1,0:T(8,128)S(1)} %get-tuple-element.66), channel_id=1, source_target_pairs={{0,4},{4,8},{8,12},{12,16},{16,20},{20,24},{24,28},{28,32},{32,36}... | collective-permute-start | bytes 6152 | tf_op jit(solution)/shard_map/ppermute | solution.py:16
  257.3 9.7 %collective-permute-start.66 = (f32[1,4,32]{2,1,0:T(4,128)S(1)}, f32[1,4,32]{2,1,0:T(4,128)S(1)}, u32[]{:S(2)}, u32[]{:S(2)}) collective-permute-start(f32[1,4,32]{2,1,0:T(4,128)S(1)} %get-tuple-element.93), channel_id=1, source_target_pairs={{0,4},{4,8},{8,12},{12,16},{16,20},{20,24},{24,28},{28,32},{32,36}... | collective-permute-start | bytes 1544 | tf_op jit(solution)/shard_map/ppermute | solution.py:16
  271.3 48.0 %collective-permute-start.43 = (f32[1,16,128]{2,1,0:T(8,128)S(1)}, f32[1,16,128]{2,1,0:T(8,128)S(1)}, u32[]{:S(2)}, u32[]{:S(2)}) collective-permute-start(f32[1,16,128]{2,1,0:T(8,128)S(1)} %get-tuple-element.39), channel_id=1, source_target_pairs={{4,0},{8,4},{12,8},{16,12},{20,16},{24,20},{28,24},{32,28},{36,32}... | collective-permute-start | bytes 24584 | tf_op jit(solution)/shard_map/ppermute | solution.py:17
  273.4 8.3 %collective-permute-start.71 = (f32[6,6,1]{2,1,0:T(8,128)S(1)}, f32[6,6,1]{2,1,0:T(8,128)S(1)}, u32[]{:S(2)}, u32[]{:S(2)}) collective-permute-start(f32[6,6,1]{2,1,0:T(8,128)S(1)} %get-tuple-element.78), channel_id=1, source_target_pairs={{128,0},{256,128},{384,256},{129,1},{257,129},{385,257},{130,2},{2... | collective-permute-start | bytes 440 | tf_op jit(solution)/shard_map/ppermute | solution.py:17
  276.9 42.5 %collective-permute-start.42 = (f32[1,16,128]{2,1,0:T(8,128)S(1)}, f32[1,16,128]{2,1,0:T(8,128)S(1)}, u32[]{:S(2)}, u32[]{:S(2)}) collective-permute-start(f32[1,16,128]{2,1,0:T(8,128)S(1)} %get-tuple-element.38), channel_id=1, source_target_pairs={{0,4},{4,8},{8,12},{12,16},{16,20},{20,24},{24,28},{28,32},{32,36}... | collective-permute-start | bytes 24584 | tf_op jit(solution)/shard_map/ppermute | solution.py:16
  281.9 15.3 %collective-permute-start.73 = (f32[1,4,32]{2,1,0:T(4,128)S(1)}, f32[1,4,32]{2,1,0:T(4,128)S(1)}, u32[]{:S(2)}, u32[]{:S(2)}) collective-permute-start(f32[1,4,32]{2,1,0:T(4,128)S(1)} %get-tuple-element.92), channel_id=1, source_target_pairs={{4,0},{8,4},{12,8},{16,12},{20,16},{24,20},{28,24},{32,28},{36,32}... | collective-permute-start | bytes 1544 | tf_op jit(solution)/shard_map/ppermute | solution.py:17
  287.2 12.0 %collective-permute-start.72 = (f32[1,4,32]{2,1,0:T(4,128)S(1)}, f32[1,4,32]{2,1,0:T(4,128)S(1)}, u32[]{:S(2)}, u32[]{:S(2)}) collective-permute-start(f32[1,4,32]{2,1,0:T(4,128)S(1)} %get-tuple-element.91), channel_id=1, source_target_pairs={{0,4},{4,8},{8,12},{12,16},{16,20},{20,24},{24,28},{28,32},{32,36}... | collective-permute-start | bytes 1544 | tf_op jit(solution)/shard_map/ppermute | solution.py:16
  289.1 11.4 %collective-permute-start.61 = (f32[1,8,64]{2,1,0:T(8,128)S(1)}, f32[1,8,64]{2,1,0:T(8,128)S(1)}, u32[]{:S(2)}, u32[]{:S(2)}) collective-permute-start(f32[1,8,64]{2,1,0:T(8,128)S(1)} %get-tuple-element.63), channel_id=1, source_target_pairs={{4,0},{8,4},{12,8},{16,12},{20,16},{24,20},{28,24},{32,28},{36,32}... | collective-permute-start | bytes 6152 | tf_op jit(solution)/shard_map/ppermute | solution.py:17
  297.3 9.7 %collective-permute-start.60 = (f32[1,8,64]{2,1,0:T(8,128)S(1)}, f32[1,8,64]{2,1,0:T(8,128)S(1)}, u32[]{:S(2)}, u32[]{:S(2)}) collective-permute-start(f32[1,8,64]{2,1,0:T(8,128)S(1)} %get-tuple-element.62), channel_id=1, source_target_pairs={{0,4},{4,8},{8,12},{12,16},{16,20},{20,24},{24,28},{28,32},{32,36}... | collective-permute-start | bytes 6152 | tf_op jit(solution)/shard_map/ppermute | solution.py:16
  299.2 9.1 %collective-permute-start.75 = (f32[6,1,32]{2,1,0:T(1,128)S(1)}, f32[6,1,32]{2,1,0:T(1,128)S(1)}, u32[]{:S(2)}, u32[]{:S(2)}) collective-permute-start(f32[6,1,32]{2,1,0:T(1,128)S(1)} %get-tuple-element.84), channel_id=1, source_target_pairs={{1,0},{2,1},{3,2},{5,4},{6,5},{7,6},{9,8},{10,9},{11,10},{13,12},{... | collective-permute-start | bytes 2312 | tf_op jit(solution)/shard_map/ppermute | solution.py:17
  300.6 7.8 %collective-permute-start.74 = (f32[6,1,32]{2,1,0:T(1,128)S(1)}, f32[6,1,32]{2,1,0:T(1,128)S(1)}, u32[]{:S(2)}, u32[]{:S(2)}) collective-permute-start(f32[6,1,32]{2,1,0:T(1,128)S(1)} %get-tuple-element.83), channel_id=1, source_target_pairs={{0,1},{1,2},{2,3},{4,5},{5,6},{6,7},{8,9},{9,10},{10,11},{12,13},{... | collective-permute-start | bytes 2312 | tf_op jit(solution)/shard_map/ppermute | solution.py:16
  307.0 17.0 %collective-permute-start.63 = (f32[10,1,64]{2,1,0:T(1,128)S(1)}, f32[10,1,64]{2,1,0:T(1,128)S(1)}, u32[]{:S(2)}, u32[]{:S(2)}) collective-permute-start(f32[10,1,64]{2,1,0:T(1,128)S(1)} %get-tuple-element.55), channel_id=1, source_target_pairs={{1,0},{2,1},{3,2},{5,4},{6,5},{7,6},{9,8},{10,9},{11,10},{13,12},{... | collective-permute-start | bytes 7688 | tf_op jit(solution)/shard_map/ppermute | solution.py:17
  314.5 9.5 %collective-permute-start.62 = (f32[10,1,64]{2,1,0:T(1,128)S(1)}, f32[10,1,64]{2,1,0:T(1,128)S(1)}, u32[]{:S(2)}, u32[]{:S(2)}) collective-permute-start(f32[10,1,64]{2,1,0:T(1,128)S(1)} %get-tuple-element.54), channel_id=1, source_target_pairs={{0,1},{1,2},{2,3},{4,5},{5,6},{6,7},{8,9},{9,10},{10,11},{12,13},{... | collective-permute-start | bytes 7688 | tf_op jit(solution)/shard_map/ppermute | solution.py:16
  319.4 10.4 %collective-permute-start.45 = (f32[18,1,128]{2,1,0:T(1,128)S(1)}, f32[18,1,128]{2,1,0:T(1,128)S(1)}, u32[]{:S(2)}, u32[]{:S(2)}) collective-permute-start(f32[18,1,128]{2,1,0:T(1,128)S(1)} %get-tuple-element.27), channel_id=1, source_target_pairs={{1,0},{2,1},{3,2},{5,4},{6,5},{7,6},{9,8},{10,9},{11,10},{13,12},{... | collective-permute-start | bytes 27656 | tf_op jit(solution)/shard_map/ppermute | solution.py:17
  320.7 9.1 %collective-permute-start.44 = (f32[18,1,128]{2,1,0:T(1,128)S(1)}, f32[18,1,128]{2,1,0:T(1,128)S(1)}, u32[]{:S(2)}, u32[]{:S(2)}) collective-permute-start(f32[18,1,128]{2,1,0:T(1,128)S(1)} %get-tuple-element.26), channel_id=1, source_target_pairs={{0,1},{1,2},{2,3},{4,5},{5,6},{6,7},{8,9},{9,10},{10,11},{12,13},{... | collective-permute-start | bytes 27656 | tf_op jit(solution)/shard_map/ppermute | solution.py:16
  324.1 11.7 %collective-permute-start.65 = (f32[10,10,1]{2,1,0:T(8,128)S(1)}, f32[10,10,1]{2,1,0:T(8,128)S(1)}, u32[]{:S(2)}, u32[]{:S(2)}) collective-permute-start(f32[10,10,1]{2,1,0:T(8,128)S(1)} %get-tuple-element.47), channel_id=1, source_target_pairs={{128,0},{256,128},{384,256},{129,1},{257,129},{385,257},{130,2},{2... | collective-permute-start | bytes 1208 | tf_op jit(solution)/shard_map/ppermute | solution.py:17
  330.0 10.1 %collective-permute-start.47 = (f32[18,18,1]{2,1,0:T(8,128)S(1)}, f32[18,18,1]{2,1,0:T(8,128)S(1)}, u32[]{:S(2)}, u32[]{:S(2)}) collective-permute-start(f32[18,18,1]{2,1,0:T(8,128)S(1)} %get-tuple-element.15), channel_id=1, source_target_pairs={{128,0},{256,128},{384,256},{129,1},{257,129},{385,257},{130,2},{2... | collective-permute-start | bytes 3896 | tf_op jit(solution)/shard_map/ppermute | solution.py:17
  334.6 10.1 %collective-permute-start.46 = (f32[18,18,1]{2,1,0:T(8,128)S(1)}, f32[18,18,1]{2,1,0:T(8,128)S(1)}, u32[]{:S(2)}, u32[]{:S(2)}) collective-permute-start(f32[18,18,1]{2,1,0:T(8,128)S(1)} %get-tuple-element.14), channel_id=1, source_target_pairs={{0,128},{128,256},{256,384},{1,129},{129,257},{257,385},{2,130},{1... | collective-permute-start | bytes 3896 | tf_op jit(solution)/shard_map/ppermute | solution.py:16
  345.3 7.9 %collective-permute-start.49 = (f32[1,16,128]{2,1,0:T(8,128)S(1)}, f32[1,16,128]{2,1,0:T(8,128)S(1)}, u32[]{:S(2)}, u32[]{:S(2)}) collective-permute-start(f32[1,16,128]{2,1,0:T(8,128)S(1)} %get-tuple-element.37), channel_id=1, source_target_pairs={{4,0},{8,4},{12,8},{16,12},{20,16},{24,20},{28,24},{32,28},{36,32}... | collective-permute-start | bytes 24584 | tf_op jit(solution)/shard_map/ppermute | solution.py:17
  351.3 9.8 %collective-permute-start.48 = (f32[1,16,128]{2,1,0:T(8,128)S(1)}, f32[1,16,128]{2,1,0:T(8,128)S(1)}, u32[]{:S(2)}, u32[]{:S(2)}) collective-permute-start(f32[1,16,128]{2,1,0:T(8,128)S(1)} %get-tuple-element.36), channel_id=1, source_target_pairs={{0,4},{4,8},{8,12},{12,16},{16,20},{20,24},{24,28},{28,32},{32,36}... | collective-permute-start | bytes 24584 | tf_op jit(solution)/shard_map/ppermute | solution.py:16
  368.2 9.3 %collective-permute-start.52 = (f32[18,18,1]{2,1,0:T(8,128)S(1)}, f32[18,18,1]{2,1,0:T(8,128)S(1)}, u32[]{:S(2)}, u32[]{:S(2)}) collective-permute-start(f32[18,18,1]{2,1,0:T(8,128)S(1)} %get-tuple-element.12), channel_id=1, source_target_pairs={{0,128},{128,256},{256,384},{1,129},{129,257},{257,385},{2,130},{1... | collective-permute-start | bytes 3896 | tf_op jit(solution)/shard_map/ppermute | solution.py:16
  380.1 9.8 %collective-permute-start.78 = (f32[1,16,128]{2,1,0:T(8,128)S(1)}, f32[1,16,128]{2,1,0:T(8,128)S(1)}, u32[]{:S(2)}, u32[]{:S(2)}) collective-permute-start(f32[1,16,128]{2,1,0:T(8,128)S(1)} %get-tuple-element.34), channel_id=1, source_target_pairs={{0,4},{4,8},{8,12},{12,16},{16,20},{20,24},{24,28},{28,32},{32,36}... | collective-permute-start | bytes 24584 | tf_op jit(solution)/shard_map/ppermute | solution.py:16
  397.4 9.3 %collective-permute-start.82 = (f32[18,18,1]{2,1,0:T(8,128)S(1)}, f32[18,18,1]{2,1,0:T(8,128)S(1)}, u32[]{:S(2)}, u32[]{:S(2)}) collective-permute-start(f32[18,18,1]{2,1,0:T(8,128)S(1)} %get-tuple-element.10), channel_id=1, source_target_pairs={{0,128},{128,256},{256,384},{1,129},{129,257},{257,385},{2,130},{1... | collective-permute-start | bytes 3896 | tf_op jit(solution)/shard_map/ppermute | solution.py:16
  (39 other events, 283.3 us)
where the time goes:
time: 410 us; the launch traced here: 408 us
  starting transfers between devices  229 us (56%)
  waiting for transfers between devices  121 us (30%)
  local copies, waits for them, and re-layouts  36.9 us (9%)
  other arithmetic  19.1 us (5%)
    ppermute x42, starting transfers between devices, with_halo(): after = lax.ppermute(first, axis, down)  121 us
    ppermute x42, starting transfers between devices, with_halo(): before = lax.ppermute(last, axis, up)  108 us
    ppermute x42, waiting for transfers between devices, with_halo(): before = lax.ppermute(last, axis, up)  96.8 us
    reshape x3, local copies, waits for them, and re-layouts, restrict(): field.reshape(sx // 2, 2, sy // 2, 2, sz // 2, 2).mean(axis=(1, 3, 5))  30.1 us
    ppermute x42, waiting for transfers between devices, with_halo(): after = lax.ppermute(first, axis, down)  23.8 us
    reduce_sum x6, other arithmetic, restrict(): field.reshape(sx // 2, 2, sy // 2, 2, sz // 2, 2).mean(axis=(1, 3, 5))  12.5 us
  transfers between devices with their start and end apart: 84, of which 36 were waited for; matrix products, arithmetic and copies ran while one was open for 1% of the time, Pallas kernels for 0%

commit v1 on v0

v1 whole, which is shorter than its diff:
```python
import jax
import jax.numpy as jnp
from jax import lax
from jax.experimental import pallas as pl
from jax.experimental.pallas import tpu as pltpu
from jax.sharding import PartitionSpec as P

F32 = jnp.float32
LANES = 128
HALO = 3
N = (16, 8, 4)
X = tuple(n + 2 * HALO for n in N)
RING = (24, 16, 16)
STEP = (1, 2, 4)
OWN = tuple(2 * n for n in N)
WIDE = tuple(2 * r for r in RING)
OBASE = (0, 512, 640)
OROWS = 672
XBASE = (0, 96, 144)
XROWS = 168
YBASE = (0, 132, 216)
YROWS = 280
WBASE = (0, 1056, 1504)
WROWS = 1824
SOLROWS = 18 * 48
VMEM_LIMIT = 48 * 1024 * 1024


def lanes_of(rows):
    return lax.broadcasted_iota(jnp.int32, (rows, LANES), 1)


def call(kernel, outs, scratch, *args):
    return pl.pallas_call(
        kernel,
        out_shape=[jax.ShapeDtypeStruct((rows, LANES), F32) for rows in outs],
        in_specs=[pl.BlockSpec(memory_space=pltpu.VMEM)] * len(args),
        out_specs=[pl.BlockSpec(memory_space=pltpu.VMEM)] * len(outs),
        scratch_shapes=[pltpu.VMEM((rows, LANES), F32) for rows in scratch],
        compiler_params=pltpu.CompilerParams(vmem_limit_bytes=VMEM_LIMIT),
    )(*args)


def z_faces(f_ref, k_ref, up_ref, down_ref):
    quarter = lanes_of(16) // 32
    for field, ref in enumerate((f_ref, k_ref)):
        for g in range(4):
            slabs = [ref[pl.ds(16 * (4 * g + m), 16), :] for m in range(4)]
            up = pltpu.roll(slabs[0], 32, 1)
            down = slabs[0]
            for m in range(1, 4):
                shift = 32 * (m + 1) % LANES
                moved = pltpu.roll(slabs[m], shift, 1) if shift else slabs[m]
                up = jnp.where(quarter == m, moved, up)
                down = jnp.where(quarter == m, pltpu.roll(slabs[m], 32 * m, 1), down)
            at = pl.ds(64 * field + 16 * g, 16)
            up_ref[at, :] = up
            down_ref[at, :] = down


def coarsen(ref, level, base, tmp, scale):
    rows = OWN[level]
    half = rows // 2
    bit = STEP[level]
    even = (lanes_of(half) // bit) % 2 == 0
    for a in range(N[level] // 2):
        at = base + OBASE[level] + 2 * a * rows
        tmp[pl.ds(a * rows, rows), :] = ref[pl.ds(at, rows), :] + ref[pl.ds(at + rows, rows), :]
    for a in range(N[level] // 2):
        pair = tmp[pl.ds(a * rows, half, 2), :] + tmp[pl.ds(a * rows + 1, half, 2), :]
        other = jnp.where(even, pltpu.roll(pair, LANES - bit, 1), pltpu.roll(pair, bit, 1))
        ref[pl.ds(base + OBASE[level + 1] + a * half, half), :] = (pair + other) * scale


def x_faces(own_ref, base, up_ref, down_ref, xbase):
    for level in range(3):
        rows = HALO * OWN[level]
        first = base + OBASE[level]
        last = first + (N[level] - HALO) * OWN[level]
        up_ref[pl.ds(xbase + XBASE[level], rows), :] = own_ref[pl.ds(last, rows), :]
        down_ref[pl.ds(xbase + XBASE[level], rows), :] = own_ref[pl.ds(first, rows), :]


def begin(f_ref, k_ref, zl_ref, zr_ref, own_ref, up_ref, down_ref, tmp):
    low = lanes_of(16) < 64
    for field, ref in enumerate((f_ref, k_ref)):
        base = field * OROWS
        for g in range(4):
            at = pl.ds(64 * field + 16 * g, 16)
            left, right = zl_ref[at, :], zr_ref[at, :]
            for m in range(4):
                slab = 4 * g + m
                shift_l, shift_r = (96 - 32 * m) % LANES, (-32 * m) % LANES
                from_l = pltpu.roll(left, shift_l, 1) if shift_l else left
                from_r = pltpu.roll(right, shift_r, 1) if shift_r else right
                own_ref[pl.ds(base + 32 * slab, 16), :] = ref[pl.ds(16 * slab, 16), :]
                own_ref[pl.ds(base + 32 * slab + 16, 16), :] = jnp.where(low, from_r, from_l)
        scale = 0.125 if field == 0 else 0.125 * 0.25
        coarsen(own_ref, 0, base, tmp, scale)
        coarsen(own_ref, 1, base, tmp, scale)
        x_faces(own_ref, base, up_ref, down_ref, field * XROWS)


def y_faces(fields, own_ref, xl_ref, xr_ref, up_ref, down_ref):
    for field in range(fields):
        ob, xb, yb = field * OROWS, field * XROWS, field * YROWS
        for dst, first in ((up_ref, False), (down_ref, True)):
            for level in range(3):
                n, rows = N[level], OWN[level]
                for h in range(2):
                    for j in range(HALO):
                        row = h * n + (j if first else n - HALO + j)
                        off = yb + YBASE[level] + (h * HALO + j) * X[level]
                        dst[pl.ds(off, HALO), :] = xl_ref[pl.ds(xb + XBASE[level] + row, HALO, rows), :]
                        dst[pl.ds(off + HALO, n), :] = own_ref[pl.ds(ob + OBASE[level] + row, n, rows), :]
                        dst[pl.ds(off + HALO + n, HALO), :] = xr_ref[pl.ds(xb + XBASE[level] + row, HALO, rows), :]
            dst[pl.ds(yb + 276, 4), :] = jnp.zeros((4, LANES), F32)


def widen(field, own_ref, xl_ref, xr_ref, yl_ref, yr_ref, wide_ref):
    ob, xb, yb = field * OROWS, field * XROWS, field * YROWS
    for level in range(3):
        n, ring, rows = N[level], RING[level], OWN[level]
        for i in range(X[level]):
            if i < HALO:
                ref, at = xl_ref, xb + XBASE[level] + i * rows
            elif i < HALO + n:
                ref, at = own_ref, ob + OBASE[level] + (i - HALO) * rows
            else:
                ref, at = xr_ref, xb + XBASE[level] + (i - HALO - n) * rows
            for h in range(2):
                to = WBASE[level] + i * WIDE[level] + h * ring
                wide_ref[pl.ds(to, n), :] = ref[pl.ds(at + h * n, n), :]
                wide_ref[pl.ds(to + n, ring - n), :] = jnp.zeros((ring - n, LANES), F32)
        for h in range(2):
            for j in range(HALO):
                off = yb + YBASE[level] + (h * HALO + j) * X[level]
                to = WBASE[level] + h * ring
                wide_ref[pl.ds(to + n + j, X[level], WIDE[level]), :] = yr_ref[pl.ds(off, X[level]), :]
                wide_ref[pl.ds(to + ring - HALO + j, X[level], WIDE[level]), :] = yl_ref[pl.ds(off, X[level]), :]


def slab(ref, base, i, rows):
    return ref[pl.ds(pl.multiple_of(base + i * rows, 8), rows), :]


def put(ref, base, i, rows, value):
    ref[pl.ds(pl.multiple_of(base + i * rows, 8), rows), :] = value


def loop(low, high, body, unroll):
    for lead in range(low, low + (high - low) % unroll):
        body(lead)
    low += (high - low) % unroll

    def step(k, carry):
        for u in range(unroll):
            body(low + k * unroll + u)
        return carry

    if high > low:
        lax.fori_loop(0, (high - low) // unroll, step, 0)


def ring_sum(ref, base, i, ring, step):
    rows = 2 * ring
    mid = slab(ref, base, i, rows)
    total = slab(ref, base, i - 1, rows) + slab(ref, base, i + 1, rows) + (mid + mid)
    halves = []
    for h in range(2):
        t = total[h * ring : (h + 1) * ring]
        t = t + pltpu.roll(t, 1, 0)
        halves.append(t + pltpu.roll(t, ring - 1, 0))
    lane = lanes_of(ring)
    a, b = halves
    ra, rb = pltpu.roll(a, step, 1), pltpu.roll(b, step, 1)
    edge = lane < step
    a, b = a + jnp.where(edge, rb, ra), b + jnp.where(edge, ra, rb)
    ra, rb = pltpu.roll(a, LANES - step, 1), pltpu.roll(b, LANES - step, 1)
    edge = lane >= LANES - step
    a, b = a + jnp.where(edge, rb, ra), b + jnp.where(edge, ra, rb)
    return mid, a, b


def join(a, b):
    return jnp.concatenate([a, b], axis=0)


def coefficients(wide_k, cw, ca, cg):
    for level in range(3):
        rows, base = WIDE[level], WBASE[level]

        def body(i):
            c = slab(wide_k, base, i, rows)
            w = 0.8 / (14.0 * c + 1.0)
            put(cw, base, i, rows, w)
            put(ca, base, i, rows, 1.0 - w * (16.0 * c + 1.0))
            put(cg, base, i, rows, 0.25 * (w * c))

        loop(0, X[level], body, 2)


def sweeps(wide_b, cw, ca, cg, first, second):
    for level in range(3):
        rows, base, ring, step = WIDE[level], WBASE[level], RING[level], STEP[level]

        def start(i):
            put(wide_b, base, i, rows, slab(cw, base, i, rows) * slab(wide_b, base, i, rows))

        loop(0, X[level], start, 2)

        def sweep(src, dst):
            def body(i):
                mid, a, b = ring_sum(src, base, i, ring, step)
                new = slab(ca, base, i, rows) * mid + slab(wide_b, base, i, rows) + slab(cg, base, i, rows) * join(a, b)
                put(dst, base, i, rows, new)

            return body

        loop(1, X[level] - 1, sweep(wide_b, first), 2)
        loop(2, X[level] - 2, sweep(first, second), 2)


def prolong(err, up3, up2):
    for q in range(6):
        for h in range(2):
            e3 = err[pl.ds(WBASE[2] + (q + 2) * 32 + h * 16, 16), :]
            to = q * 32 + h * 16
            up3[pl.ds(to, 5, 2), :] = e3[0:5]
            up3[pl.ds(to + 1, 5, 2), :] = e3[0:5]
            up3[pl.ds(to + 10, 4), :] = jnp.zeros((4, LANES), F32)
            up3[pl.ds(to + 14, 2), :] = jnp.broadcast_to(e3[15:16], (2, LANES))
    for a in range(10):
        for h in range(2):
            e2 = err[pl.ds(WBASE[1] + (a + 2) * 32 + h * 16, 16), :]
            e2 = e2 + up3[pl.ds(((a - 1) // 2 + 1) * 32 + h * 16, 16), :]
            to = a * 48 + h * 24
            up2[pl.ds(to, 9, 2), :] = e2[0:9]
            up2[pl.ds(to + 1, 9, 2), :] = e2[0:9]
            up2[pl.ds(to + 18, 4), :] = jnp.zeros((4, LANES), F32)
            up2[pl.ds(to + 22, 2), :] = jnp.broadcast_to(e2[15:16], (2, LANES))


def correct(err, up2, old_ref, sol_ref):
    for i in range(18):
        value = err[pl.ds((i + 2) * 48, 48), :] + up2[pl.ds(((i - 1) // 2 + 1) * 48, 48), :]
        if old_ref is not None:
            value = value + old_ref[pl.ds(i * 48, 48), :]
        sol_ref[pl.ds(i * 48, 48), :] = value


def first_round(
    own_ref, xl_ref, xr_ref, yl_ref, yr_ref,
    r_ref, up_ref, down_ref, sol_ref, cw, ca, cg,
    wide_b, wide_k, first, second, up3, up2, tmp,
):
    widen(0, own_ref, xl_ref, xr_ref, yl_ref, yr_ref, wide_b)
    widen(1, own_ref, xl_ref, xr_ref, yl_ref, yr_ref, wide_k)
    coefficients(wide_k, cw, ca, cg)
    sweeps(wide_b, cw, ca, cg, first, second)
    prolong(second, up3, up2)
    correct(second, up2, None, sol_ref)

    def resid(i):
        mid, a, b = ring_sum(sol_ref, 0, i + 1, 24, 1)
        for h, t in enumerate((a, b)):
            s = mid[h * 24 : h * 24 + 16]
            at = pl.ds(pl.multiple_of(i * 32 + h * 16, 16), 16)
            f = own_ref[at, :]
            k = own_ref[pl.ds(pl.multiple_of(OROWS + i * 32 + h * 16, 16), 16), :]
            r_ref[at, :] = f - (k * (16.0 * s - 0.25 * t[:16]) + s)

    loop(0, 16, resid, 2)
    coarsen(r_ref, 0, 0, tmp, 0.125)
    coarsen(r_ref, 1, 0, tmp, 0.125)
    x_faces(r_ref, 0, up_ref, down_ref, 0)


def second_round(
    f_ref, k_ref, own_ref, xl_ref, xr_ref, yl_ref, yr_ref, old_ref, cw, ca, cg,
    out_ref, resid_ref,
    wide_b, first, second, sol_ref, up3, up2,
):
    widen(0, own_ref, xl_ref, xr_ref, yl_ref, yr_ref, wide_b)
    sweeps(wide_b, cw, ca, cg, first, second)
    prolong(second, up3, up2)
    correct(second, up2, old_ref, sol_ref)

    def resid(i):
        mid, a, _ = ring_sum(sol_ref, 0, i + 1, 24, 1)
        s = mid[:16]
        at = pl.ds(pl.multiple_of(i * 16, 16), 16)
        out_ref[at, :] = s
        resid_ref[at, :] = f_ref[at, :] - (k_ref[at, :] * (16.0 * s - 0.25 * a[:16]) + s)

    loop(0, 16, resid, 2)


def swap(up, down, axis):
    size = lax.axis_size(axis)
    rising = [(i, i + 1) for i in range(size - 1)]
    falling = [(j, i) for i, j in rising]
    return lax.ppermute(up, axis, rising), lax.ppermute(down, axis, falling)


def shards(forcing, kappa):
    shape = forcing.shape
    f = forcing.reshape(256, LANES)
    k = kappa.reshape(256, LANES)
    zl, zr = swap(*call(z_faces, [128, 128], [], f, k), "grp")
    own, up, down = call(begin, [2 * OROWS, 2 * XROWS, 2 * XROWS], [256], f, k, zl, zr)
    xl, xr = swap(up, down, "gx")

    def faces(fields, own, xl, xr):
        def kernel(*refs):
            y_faces(fields, *refs)

        return call(kernel, [fields * YROWS] * 2, [], own, xl, xr)

    yl, yr = swap(*faces(2, own, xl, xr), "gy")
    r, up, down, sol, cw, ca, cg = call(
        first_round,
        [OROWS, XROWS, XROWS, SOLROWS, WROWS, WROWS, WROWS],
        [WROWS, WROWS, WROWS, WROWS, 192, 480, 256],
        own, xl, xr, yl, yr,
    )
    xl, xr = swap(up, down, "gx")
    yl, yr = swap(*faces(1, r, xl, xr), "gy")
    out, resid = call(
        second_round,
        [256, 256],
        [WROWS, WROWS, WROWS, SOLROWS, 192, 480],
        f, k, r, xl, xr, yl, yr, sol, cw, ca, cg,
    )
    return out.reshape(shape), resid.reshape(shape)


def solution(mesh):
    placed = (P("gx", "gy", "grp"), P("gx", "gy", "grp"))
    return jax.shard_map(shards, mesh=mesh, in_specs=placed, out_specs=placed, check_vma=False)
```

time: 410 us -> 82.4 us (0.20)
  the two profiles are of different devices: /device:TPU:262 before, /device:TPU:243 now
where the time goes in v1:
time: 82.4 us; the launch traced here: 82 us
  starting transfers between devices  31.2 us (38%)
  waiting for transfers between devices  30 us (36%)
  Pallas kernels  18.2 us (22%)
  local copies, waits for them, and re-layouts  1.8 us (2%)
    ppermute x10, starting transfers between devices, swap(): return (lax.ppermute(up, axis, rising), lax.ppermute(down, axis, falling))  31.2 us
    ppermute x10, waiting for transfers between devices, swap(): return (lax.ppermute(up, axis, rising), lax.ppermute(down, axis, falling))  30 us
    pallas_call x6, Pallas kernels, call(): pl.pallas_call(kernel, out_shape=[jax.ShapeDtypeStruct((rows, LANES), F32...  18.2 us
    unnamed x4, local copies, waits for them, and re-layouts  1.8 us
  transfers between devices with their start and end apart: 10, of which 9 were waited for; matrix products, arithmetic and copies ran while one was open for 0% of the time, Pallas kernels for 0%

profile of v1, /device:TPU:243, one launch (start us, length us, event | category | flops | bytes accessed | tf_op | source)
XLA Modules:
  0.0 82.0 jit_solution(16790128303904599449)
XLA Ops:
  0.6 0.0 copy-start
  0.6 0.9 %copy-done = f32[16,16,128]{2,1,0:T(8,128)S(1)} copy-done((f32[16,16,128]{2,1,0:T(8,128)S(1)}, f32[16,16,128]{2,1,0:T(8,128)}, u32[]{:S(2)}) %copy-start) | copy-done | bytes 131096
  1.5 0.0 copy-start.1
  1.5 0.9 %copy-done.1 = f32[16,16,128]{2,1,0:T(8,128)S(1)} copy-done((f32[16,16,128]{2,1,0:T(8,128)S(1)}, f32[16,16,128]{2,1,0:T(8,128)}, u32[]{:S(2)}) %copy-start.1) | copy-done | bytes 131096
  2.4 0.2 shard_map.41
  2.6 3.1 %collective-permute-start = (f32[128,128]{1,0:T(8,128)S(1)}, f32[128,128]{1,0:T(8,128)S(1)}, u32[]{:S(2)}, u32[]{:S(2)}) collective-permute-start(f32[128,128]{1,0:T(8,128)S(1)} %get-tuple-element.20), channel_id=1, source_target_pairs={{0,128},{128,256},{256,384},{1,129},{129,257},{257,385},{2,130},{1... | collective-permute-start | bytes 196616 | tf_op jit(solution)/shard_map/ppermute | solution.py:303
  5.7 2.2 %collective-permute-start.1 = (f32[128,128]{1,0:T(8,128)S(1)}, f32[128,128]{1,0:T(8,128)S(1)}, u32[]{:S(2)}, u32[]{:S(2)}) collective-permute-start(f32[128,128]{1,0:T(8,128)S(1)} %get-tuple-element.21), channel_id=1, source_target_pairs={{128,0},{256,128},{384,256},{129,1},{257,129},{385,257},{130,2},{2... | collective-permute-start | bytes 196616 | tf_op jit(solution)/shard_map/ppermute | solution.py:303
  7.9 0.0 collective-permute-done.zl_ref
  7.9 2.8 %collective-permute-done.1.zr_ref = f32[128,128]{1,0:T(8,128)S(1)} collective-permute-done((f32[128,128]{1,0:T(8,128)S(1)}, f32[128,128]{1,0:T(8,128)S(1)}, u32[]{:S(2)}, u32[]{:S(2)}) %collective-permute-start.1) | collective-permute-done | bytes 65568 | tf_op jit(solution)/shard_map/ppermute | solution.py:303
  10.7 0.4 shard_map.42
  11.2 4.5 %collective-permute-start.2 = (f32[336,128]{1,0:T(8,128)S(1)}, f32[336,128]{1,0:T(8,128)S(1)}, u32[]{:S(2)}, u32[]{:S(2)}) collective-permute-start(f32[336,128]{1,0:T(8,128)S(1)} %get-tuple-element.23), channel_id=1, source_target_pairs={{0,4},{4,8},{8,12},{12,16},{16,20},{20,24},{24,28},{28,32},{32,36}... | collective-permute-start | bytes 516104 | tf_op jit(solution)/shard_map/ppermute | solution.py:303
  15.7 1.9 %collective-permute-start.3 = (f32[336,128]{1,0:T(8,128)S(1)}, f32[336,128]{1,0:T(8,128)S(1)}, u32[]{:S(2)}, u32[]{:S(2)}) collective-permute-start(f32[336,128]{1,0:T(8,128)S(1)} %get-tuple-element.24), channel_id=1, source_target_pairs={{4,0},{8,4},{12,8},{16,12},{20,16},{24,20},{28,24},{32,28},{36,32}... | collective-permute-start | bytes 516104 | tf_op jit(solution)/shard_map/ppermute | solution.py:303
  17.6 1.5 %collective-permute-done.2.refs_1_.xl_ref = f32[336,128]{1,0:T(8,128)S(1)} collective-permute-done((f32[336,128]{1,0:T(8,128)S(1)}, f32[336,128]{1,0:T(8,128)S(1)}, u32[]{:S(2)}, u32[]{:S(2)}) %collective-permute-start.2) | collective-permute-done | bytes 172064 | tf_op jit(solution)/shard_map/ppermute | solution.py:303
  19.2 9.1 %collective-permute-done.3.refs_2_.xr_ref = f32[336,128]{1,0:T(8,128)S(1)} collective-permute-done((f32[336,128]{1,0:T(8,128)S(1)}, f32[336,128]{1,0:T(8,128)S(1)}, u32[]{:S(2)}, u32[]{:S(2)}) %collective-permute-start.3) | collective-permute-done | bytes 172064 | tf_op jit(solution)/shard_map/ppermute | solution.py:303
  28.3 0.3 shard_map.43
  28.5 7.1 %collective-permute-start.4 = (f32[560,128]{1,0:T(8,128)S(1)}, f32[560,128]{1,0:T(8,128)S(1)}, u32[]{:S(2)}, u32[]{:S(2)}) collective-permute-start(f32[560,128]{1,0:T(8,128)S(1)} %get-tuple-element.25), channel_id=1, source_target_pairs={{0,1},{1,2},{2,3},{4,5},{5,6},{6,7},{8,9},{9,10},{10,11},{12,13},{... | collective-permute-start | bytes 860168 | tf_op jit(solution)/shard_map/ppermute | solution.py:303
  35.6 1.9 %collective-permute-start.5 = (f32[560,128]{1,0:T(8,128)S(1)}, f32[560,128]{1,0:T(8,128)S(1)}, u32[]{:S(2)}, u32[]{:S(2)}) collective-permute-start(f32[560,128]{1,0:T(8,128)S(1)} %get-tuple-element.26), channel_id=1, source_target_pairs={{1,0},{2,1},{3,2},{5,4},{6,5},{7,6},{9,8},{10,9},{11,10},{13,12},{... | collective-permute-start | bytes 860168 | tf_op jit(solution)/shard_map/ppermute | solution.py:303
  37.5 1.6 %collective-permute-done.4.yl_ref = f32[560,128]{1,0:T(8,128)S(1)} collective-permute-done((f32[560,128]{1,0:T(8,128)S(1)}, f32[560,128]{1,0:T(8,128)S(1)}, u32[]{:S(2)}, u32[]{:S(2)}) %collective-permute-start.4) | collective-permute-done | bytes 286752 | tf_op jit(solution)/shard_map/ppermute | solution.py:303
  39.2 4.4 %collective-permute-done.5.yr_ref = f32[560,128]{1,0:T(8,128)S(1)} collective-permute-done((f32[560,128]{1,0:T(8,128)S(1)}, f32[560,128]{1,0:T(8,128)S(1)}, u32[]{:S(2)}, u32[]{:S(2)}) %collective-permute-start.5) | collective-permute-done | bytes 286752 | tf_op jit(solution)/shard_map/ppermute | solution.py:303
  43.6 8.7 %shard_map.44 = (f32[672,128]{1,0:T(8,128)S(1)}, f32[168,128]{1,0:T(8,128)S(1)}, f32[168,128]{1,0:T(8,128)S(1)}, f32[864,128]{1,0:T(8,128)S(1)}, f32[1824,128]{1...) custom-call(f32[1344,128]{1,0:T(8,128)S(1)} %get-tuple-element.22.refs_0_.own_ref, ...), custom_call_target="tpu_custom_call" | custom-call | tf_op jit(solution)/shard_map/pallas_call | solution.py:34
  52.3 1.9 %collective-permute-start.6 = (f32[168,128]{1,0:T(8,128)S(1)}, f32[168,128]{1,0:T(8,128)S(1)}, u32[]{:S(2)}, u32[]{:S(2)}) collective-permute-start(f32[168,128]{1,0:T(8,128)S(1)} %get-tuple-element.28), channel_id=1, source_target_pairs={{0,4},{4,8},{8,12},{12,16},{16,20},{20,24},{24,28},{28,32},{32,36}... | collective-permute-start | bytes 258056 | tf_op jit(solution)/shard_map/ppermute | solution.py:303
  54.2 4.3 %collective-permute-start.7 = (f32[168,128]{1,0:T(8,128)S(1)}, f32[168,128]{1,0:T(8,128)S(1)}, u32[]{:S(2)}, u32[]{:S(2)}) collective-permute-start(f32[168,128]{1,0:T(8,128)S(1)} %get-tuple-element.29), channel_id=1, source_target_pairs={{4,0},{8,4},{12,8},{16,12},{20,16},{24,20},{28,24},{32,28},{36,32}... | collective-permute-start | bytes 258056 | tf_op jit(solution)/shard_map/ppermute | solution.py:303
  58.4 0.2 collective-permute-done.6.refs_1_.xl_ref
  58.7 5.9 %collective-permute-done.7.refs_2_.xr_ref = f32[168,128]{1,0:T(8,128)S(1)} collective-permute-done((f32[168,128]{1,0:T(8,128)S(1)}, f32[168,128]{1,0:T(8,128)S(1)}, u32[]{:S(2)}, u32[]{:S(2)}) %collective-permute-start.7) | collective-permute-done | bytes 86048 | tf_op jit(solution)/shard_map/ppermute | solution.py:303
  64.5 0.1 shard_map.45
  64.7 2.4 %collective-permute-start.8 = (f32[280,128]{1,0:T(8,128)S(1)}, f32[280,128]{1,0:T(8,128)S(1)}, u32[]{:S(2)}, u32[]{:S(2)}) collective-permute-start(f32[280,128]{1,0:T(8,128)S(1)} %get-tuple-element.30), channel_id=1, source_target_pairs={{0,1},{1,2},{2,3},{4,5},{5,6},{6,7},{8,9},{9,10},{10,11},{12,13},{... | collective-permute-start | bytes 430088 | tf_op jit(solution)/shard_map/ppermute | solution.py:303
  67.1 1.9 %collective-permute-start.9 = (f32[280,128]{1,0:T(8,128)S(1)}, f32[280,128]{1,0:T(8,128)S(1)}, u32[]{:S(2)}, u32[]{:S(2)}) collective-permute-start(f32[280,128]{1,0:T(8,128)S(1)} %get-tuple-element.31), channel_id=1, source_target_pairs={{1,0},{2,1},{3,2},{5,4},{6,5},{7,6},{9,8},{10,9},{11,10},{13,12},{... | collective-permute-start | bytes 430088 | tf_op jit(solution)/shard_map/ppermute | solution.py:303
  69.0 0.1 collective-permute-done.8.yl_ref
  69.1 4.4 %collective-permute-done.9.yr_ref = f32[280,128]{1,0:T(8,128)S(1)} collective-permute-done((f32[280,128]{1,0:T(8,128)S(1)}, f32[280,128]{1,0:T(8,128)S(1)}, u32[]{:S(2)}, u32[]{:S(2)}) %collective-permute-start.9) | collective-permute-done | bytes 143392 | tf_op jit(solution)/shard_map/ppermute | solution.py:303
  73.5 8.5 %shard_map.46 = (f32[256,128]{1,0:T(8,128)}, f32[256,128]{1,0:T(8,128)}) custom-call(f32[256,128]{1,0:T(8,128)S(1)} %bitcast.6, f32[256,128]{1,0:T(8,128)S(1)} %bitcast.9, f32[672,128]{1,0:T(8,128)S(1)} %get-tuple-element.27.refs_0_.own_ref, f32[168,128]{1,0:T(8,128)S(1)} %collective-permute-done.6.refs_1_.xl_ref, ...), custom_call_target="tpu_custom_call" | custom-call | tf_op jit(solution)/shard_map/pallas_call | solution.py:34
Async XLA Ops:
  0.6 0.9 %copy-start = (f32[16,16,128]{2,1,0:T(8,128)S(1)}, f32[16,16,128]{2,1,0:T(8,128)}, u32[]{:S(2)}) copy-start(f32[16,16,128]{2,1,0:T(8,128)} %param.2) | copy-start | bytes 393220
  1.5 0.9 %copy-start.1 = (f32[16,16,128]{2,1,0:T(8,128)S(1)}, f32[16,16,128]{2,1,0:T(8,128)}, u32[]{:S(2)}) copy-start(f32[16,16,128]{2,1,0:T(8,128)} %param.3) | copy-start | bytes 393220
  2.6 5.3 %collective-permute-start = (f32[128,128]{1,0:T(8,128)S(1)}, f32[128,128]{1,0:T(8,128)S(1)}, u32[]{:S(2)}, u32[]{:S(2)}) collective-permute-start(f32[128,128]{1,0:T(8,128)S(1)} %get-tuple-element.20), channel_id=1, source_target_pairs={{0,128},{128,256},{256,384},{1,129},{129,257},{257,385},{2,130},{1... | collective-permute-start | bytes 196616 | tf_op jit(solution)/shard_map/ppermute | solution.py:303
  5.7 5.0 %collective-permute-start.1 = (f32[128,128]{1,0:T(8,128)S(1)}, f32[128,128]{1,0:T(8,128)S(1)}, u32[]{:S(2)}, u32[]{:S(2)}) collective-permute-start(f32[128,128]{1,0:T(8,128)S(1)} %get-tuple-element.21), channel_id=1, source_target_pairs={{128,0},{256,128},{384,256},{129,1},{257,129},{385,257},{130,2},{2... | collective-permute-start | bytes 196616 | tf_op jit(solution)/shard_map/ppermute | solution.py:303
  11.2 8.0 %collective-permute-start.2 = (f32[336,128]{1,0:T(8,128)S(1)}, f32[336,128]{1,0:T(8,128)S(1)}, u32[]{:S(2)}, u32[]{:S(2)}) collective-permute-start(f32[336,128]{1,0:T(8,128)S(1)} %get-tuple-element.23), channel_id=1, source_target_pairs={{0,4},{4,8},{8,12},{12,16},{16,20},{20,24},{24,28},{28,32},{32,36}... | collective-permute-start | bytes 516104 | tf_op jit(solution)/shard_map/ppermute | solution.py:303
  15.7 12.5 %collective-permute-start.3 = (f32[336,128]{1,0:T(8,128)S(1)}, f32[336,128]{1,0:T(8,128)S(1)}, u32[]{:S(2)}, u32[]{:S(2)}) collective-permute-start(f32[336,128]{1,0:T(8,128)S(1)} %get-tuple-element.24), channel_id=1, source_target_pairs={{4,0},{8,4},{12,8},{16,12},{20,16},{24,20},{28,24},{32,28},{36,32}... | collective-permute-start | bytes 516104 | tf_op jit(solution)/shard_map/ppermute | solution.py:303
  28.5 10.6 %collective-permute-start.4 = (f32[560,128]{1,0:T(8,128)S(1)}, f32[560,128]{1,0:T(8,128)S(1)}, u32[]{:S(2)}, u32[]{:S(2)}) collective-permute-start(f32[560,128]{1,0:T(8,128)S(1)} %get-tuple-element.25), channel_id=1, source_target_pairs={{0,1},{1,2},{2,3},{4,5},{5,6},{6,7},{8,9},{9,10},{10,11},{12,13},{... | collective-permute-start | bytes 860168 | tf_op jit(solution)/shard_map/ppermute | solution.py:303
  35.6 8.0 %collective-permute-start.5 = (f32[560,128]{1,0:T(8,128)S(1)}, f32[560,128]{1,0:T(8,128)S(1)}, u32[]{:S(2)}, u32[]{:S(2)}) collective-permute-start(f32[560,128]{1,0:T(8,128)S(1)} %get-tuple-element.26), channel_id=1, source_target_pairs={{1,0},{2,1},{3,2},{5,4},{6,5},{7,6},{9,8},{10,9},{11,10},{13,12},{... | collective-permute-start | bytes 860168 | tf_op jit(solution)/shard_map/ppermute | solution.py:303
  52.3 6.4 %collective-permute-start.6 = (f32[168,128]{1,0:T(8,128)S(1)}, f32[168,128]{1,0:T(8,128)S(1)}, u32[]{:S(2)}, u32[]{:S(2)}) collective-permute-start(f32[168,128]{1,0:T(8,128)S(1)} %get-tuple-element.28), channel_id=1, source_target_pairs={{0,4},{4,8},{8,12},{12,16},{16,20},{20,24},{24,28},{28,32},{32,36}... | collective-permute-start | bytes 258056 | tf_op jit(solution)/shard_map/ppermute | solution.py:303
  54.2 10.4 %collective-permute-start.7 = (f32[168,128]{1,0:T(8,128)S(1)}, f32[168,128]{1,0:T(8,128)S(1)}, u32[]{:S(2)}, u32[]{:S(2)}) collective-permute-start(f32[168,128]{1,0:T(8,128)S(1)} %get-tuple-element.29), channel_id=1, source_target_pairs={{4,0},{8,4},{12,8},{16,12},{20,16},{24,20},{28,24},{32,28},{36,32}... | collective-permute-start | bytes 258056 | tf_op jit(solution)/shard_map/ppermute | solution.py:303
  64.7 4.4 %collective-permute-start.8 = (f32[280,128]{1,0:T(8,128)S(1)}, f32[280,128]{1,0:T(8,128)S(1)}, u32[]{:S(2)}, u32[]{:S(2)}) collective-permute-start(f32[280,128]{1,0:T(8,128)S(1)} %get-tuple-element.30), channel_id=1, source_target_pairs={{0,1},{1,2},{2,3},{4,5},{5,6},{6,7},{8,9},{9,10},{10,11},{12,13},{... | collective-permute-start | bytes 430088 | tf_op jit(solution)/shard_map/ppermute | solution.py:303
  67.1 6.4 %collective-permute-start.9 = (f32[280,128]{1,0:T(8,128)S(1)}, f32[280,128]{1,0:T(8,128)S(1)}, u32[]{:S(2)}, u32[]{:S(2)}) collective-permute-start(f32[280,128]{1,0:T(8,128)S(1)} %get-tuple-element.31), channel_id=1, source_target_pairs={{1,0},{2,1},{3,2},{5,4},{6,5},{7,6},{9,8},{10,9},{11,10},{13,12},{... | collective-permute-start | bytes 430088 | tf_op jit(solution)/shard_map/ppermute | solution.py:303

commit v2 on v1

--- a/solution.py
+++ b/solution.py
@@ -20,6 +20,8 @@
 XROWS = 168
 YBASE = (0, 132, 216)
 YROWS = 280
+PACKED = 112
+UNROLL = 8
 WBASE = (0, 1056, 1504)
 WROWS = 1824
 SOLROWS = 18 * 48
@@ -30,20 +32,25 @@
     return lax.broadcasted_iota(jnp.int32, (rows, LANES), 1)
 
 
-def call(kernel, outs, scratch, *args):
+VM = pl.BlockSpec(memory_space=pltpu.VMEM)
+HBM = pl.BlockSpec(memory_space=pl.ANY)
+
+
+def call(kernel, outs, scratch, *args, out_specs=None, copies=0):
     return pl.pallas_call(
         kernel,
         out_shape=[jax.ShapeDtypeStruct((rows, LANES), F32) for rows in outs],
-        in_specs=[pl.BlockSpec(memory_space=pltpu.VMEM)] * len(args),
-        out_specs=[pl.BlockSpec(memory_space=pltpu.VMEM)] * len(outs),
-        scratch_shapes=[pltpu.VMEM((rows, LANES), F32) for rows in scratch],
+        in_specs=[VM] * len(args),
+        out_specs=out_specs or [VM] * len(outs),
+        scratch_shapes=[pltpu.VMEM((rows, LANES), F32) for rows in scratch]
+        + ([pltpu.SemaphoreType.DMA((copies,))] if copies else []),
         compiler_params=pltpu.CompilerParams(vmem_limit_bytes=VMEM_LIMIT),
     )(*args)
 
 
-def z_faces(f_ref, k_ref, up_ref, down_ref):
+def z_faces(fk_ref, up_ref, down_ref):
     quarter = lanes_of(16) // 32
-    for field, ref in enumerate((f_ref, k_ref)):
+    for field, ref in enumerate((fk_ref.at[pl.ds(0, 256), :], fk_ref.at[pl.ds(256, 256), :])):
         for g in range(4):
             slabs = [ref[pl.ds(16 * (4 * g + m), 16), :] for m in range(4)]
             up = pltpu.roll(slabs[0], 32, 1)
@@ -73,17 +80,54 @@
 
 
 def x_faces(own_ref, base, up_ref, down_ref, xbase):
-    for level in range(3):
-        rows = HALO * OWN[level]
-        first = base + OBASE[level]
-        last = first + (N[level] - HALO) * OWN[level]
-        up_ref[pl.ds(xbase + XBASE[level], rows), :] = own_ref[pl.ds(last, rows), :]
-        down_ref[pl.ds(xbase + XBASE[level], rows), :] = own_ref[pl.ds(first, rows), :]
-
-
-def begin(f_ref, k_ref, zl_ref, zr_ref, own_ref, up_ref, down_ref, tmp):
+    centre = abs(lanes_of(16) - 63.5) < 32
+    odd = lanes_of(16) % 2 == 1
+    turn = lanes_of(8) % 4
+    for dst, end in ((up_ref, 1), (down_ref, 0)):
+        at = [base + OBASE[level] + end * (N[level] - HALO) * OWN[level] for level in range(3)]
+        for i in range(HALO):
+            dst[pl.ds(xbase + 16 * i, 16), :] = own_ref[pl.ds(at[0] + 32 * i, 16), :]
+        z = [own_ref[pl.ds(at[0] + 32 * i + 16, 16), :] for i in range(HALO)]
+        dst[pl.ds(xbase + 48, 16), :] = jnp.where(centre, pltpu.roll(z[1], 64, 1), z[0])
+        dst[pl.ds(xbase + 64, 16), :] = z[2]
+        c = [own_ref[pl.ds(at[1] + 16 * i, 16), :] for i in range(HALO)]
+        dst[pl.ds(xbase + 80, 16), :] = jnp.where(odd, c[1], c[0])
+        dst[pl.ds(xbase + 96, 8), :] = jnp.where(odd[:8], c[2][8:], c[2][:8])
+        c = [own_ref[pl.ds(at[2] + 8 * i, 8), :] for i in range(HALO)]
+        dst[pl.ds(xbase + 104, 8), :] = jnp.where(turn == 0, c[0], jnp.where(turn == 1, c[1], c[2]))
+
+
+def unpack(src, at, dst, to):
+    odd = lanes_of(16) % 2 == 1
+    turn = lanes_of(8) % 4
+    for i in range(HALO):
+        dst[pl.ds(to + 32 * i, 16), :] = src[pl.ds(at + 16 * i, 16), :]
+    z = src[pl.ds(at + 48, 16), :]
+    for i, value in enumerate((z, pltpu.roll(z, 64, 1), src[pl.ds(at + 64, 16), :])):
+        dst[pl.ds(to + 32 * i + 16, 16), :] = value
+
+    def two(value):
+        mask = odd[: value.shape[0]]
+        return jnp.where(mask, pltpu.roll(value, 1, 1), value), jnp.where(mask, value, pltpu.roll(value, LANES - 1, 1))
+
+    first = two(src[pl.ds(at + 80, 16), :])
+    dst[pl.ds(to + 96, 16), :] = first[0]
+    dst[pl.ds(to + 112, 16), :] = first[1]
+    last = two(src[pl.ds(at + 96, 8), :])
+    dst[pl.ds(to + 128, 8), :] = last[0]
+    dst[pl.ds(to + 136, 8), :] = last[1]
+    c = src[pl.ds(at + 104, 8), :]
+    moved = {d: pltpu.roll(c, d % LANES, 1) if d else c for d in range(-2, 4)}
+    for i in range(HALO):
+        value = moved[-i]
+        for lane in range(1, 4):
+            value = jnp.where(turn == lane, moved[lane - i], value)
+        dst[pl.ds(to + 144 + 8 * i, 8), :] = value
+
+
+def begin(fk_ref, zl_ref, zr_ref, raw_ref, own_ref, w_ref, up_ref, down_ref, tmp):
     low = lanes_of(16) < 64
-    for field, ref in enumerate((f_ref, k_ref)):
+    for field, ref in enumerate((fk_ref.at[pl.ds(0, 256), :], fk_ref.at[pl.ds(256, 256), :])):
         base = field * OROWS
         for g in range(4):
             at = pl.ds(64 * field + 16 * g, 16)
@@ -93,17 +137,26 @@
                 shift_l, shift_r = (96 - 32 * m) % LANES, (-32 * m) % LANES
                 from_l = pltpu.roll(left, shift_l, 1) if shift_l else left
                 from_r = pltpu.roll(right, shift_r, 1) if shift_r else right
-                own_ref[pl.ds(base + 32 * slab, 16), :] = ref[pl.ds(16 * slab, 16), :]
-                own_ref[pl.ds(base + 32 * slab + 16, 16), :] = jnp.where(low, from_r, from_l)
+                raw_ref[pl.ds(base + 32 * slab, 16), :] = ref[pl.ds(16 * slab, 16), :]
+                raw_ref[pl.ds(base + 32 * slab + 16, 16), :] = jnp.where(low, from_r, from_l)
         scale = 0.125 if field == 0 else 0.125 * 0.25
-        coarsen(own_ref, 0, base, tmp, scale)
-        coarsen(own_ref, 1, base, tmp, scale)
-        x_faces(own_ref, base, up_ref, down_ref, field * XROWS)
-
-
-def y_faces(fields, own_ref, xl_ref, xr_ref, up_ref, down_ref):
+        coarsen(raw_ref, 0, base, tmp, scale)
+        coarsen(raw_ref, 1, base, tmp, scale)
+    for at in range(0, OROWS, 32):
+        c = raw_ref[pl.ds(OROWS + at, 32), :]
+        w = 0.8 / (14.0 * c + 1.0)
+        w_ref[pl.ds(at, 32), :] = w
+        own_ref[pl.ds(at, 32), :] = w * raw_ref[pl.ds(at, 32), :]
+        own_ref[pl.ds(OROWS + at, 32), :] = 0.25 * (w * c)
+    for field in range(2):
+        x_faces(own_ref, field * OROWS, up_ref, down_ref, field * PACKED)
+
+
+def y_faces(fields, own_ref, xl_packed, xr_packed, up_ref, down_ref, xl_ref, xr_ref):
     for field in range(fields):
         ob, xb, yb = field * OROWS, field * XROWS, field * YROWS
+        unpack(xl_packed, field * PACKED, xl_ref, xb)
+        unpack(xr_packed, field * PACKED, xr_ref, xb)
         for dst, first in ((up_ref, False), (down_ref, True)):
             for level in range(3):
                 n, rows = N[level], OWN[level]
@@ -148,18 +201,23 @@
     ref[pl.ds(pl.multiple_of(base + i * rows, 8), rows), :] = value
 
 
-def loop(low, high, body, unroll):
-    for lead in range(low, low + (high - low) % unroll):
-        body(lead)
-    low += (high - low) % unroll
-
-    def step(k, carry):
-        for u in range(unroll):
-            body(low + k * unroll + u)
+def loop(low, high, value, store):
+    groups = -(-(high - low) // UNROLL)
+    size = -(-(high - low) // groups)
+    lead = (high - low) - (groups - 1) * size
+
+    def group(first, count):
+        values = [value(first + u) for u in range(count)]
+        for u in range(count):
+            store(first + u, values[u])
+
+    def step(g, carry):
+        group(low + lead + g * size, size)
         return carry
 
-    if high > low:
-        lax.fori_loop(0, (high - low) // unroll, step, 0)
+    group(low, lead)
+    if groups > 1:
+        lax.fori_loop(0, groups - 1, step, 0)
 
 
 def ring_sum(ref, base, i, ring, step):
@@ -186,39 +244,20 @@
     return jnp.concatenate([a, b], axis=0)
 
 
-def coefficients(wide_k, cw, ca, cg):
-    for level in range(3):
-        rows, base = WIDE[level], WBASE[level]
-
-        def body(i):
-            c = slab(wide_k, base, i, rows)
-            w = 0.8 / (14.0 * c + 1.0)
-            put(cw, base, i, rows, w)
-            put(ca, base, i, rows, 1.0 - w * (16.0 * c + 1.0))
-            put(cg, base, i, rows, 0.25 * (w * c))
-
-        loop(0, X[level], body, 2)
-
-
-def sweeps(wide_b, cw, ca, cg, first, second):
+def sweeps(wide_b, wide_u, first, second):
     for level in range(3):
         rows, base, ring, step = WIDE[level], WBASE[level], RING[level], STEP[level]
 
-        def start(i):
-            put(wide_b, base, i, rows, slab(cw, base, i, rows) * slab(wide_b, base, i, rows))
-
-        loop(0, X[level], start, 2)
-
-        def sweep(src, dst):
-            def body(i):
+        def sweep(low, high, src, dst):
+            def value(i):
                 mid, a, b = ring_sum(src, base, i, ring, step)
-                new = slab(ca, base, i, rows) * mid + slab(wide_b, base, i, rows) + slab(cg, base, i, rows) * join(a, b)
-                put(dst, base, i, rows, new)
-
-            return body
-
-        loop(1, X[level] - 1, sweep(wide_b, first), 2)
-        loop(2, X[level] - 2, sweep(first, second), 2)
+                around = slab(wide_u, base, i, rows) * (join(a, b) - 8.0 * mid)
+                return 0.2 * mid + slab(wide_b, base, i, rows) + around
+
+            loop(low, high, value, lambda i, new: put(dst, base, i, rows, new))
+
+        sweep(1, X[level] - 1, wide_b, first)
+        sweep(2, X[level] - 2, first, second)
 
 
 def prolong(err, up3, up2):
@@ -250,87 +289,115 @@
 
 
 def first_round(
-    own_ref, xl_ref, xr_ref, yl_ref, yr_ref,
-    r_ref, up_ref, down_ref, sol_ref, cw, ca, cg,
-    wide_b, wide_k, first, second, up3, up2, tmp,
+    raw_ref, own_ref, w_ref, xl_ref, xr_ref, yl_ref, yr_ref,
+    next_ref, up_ref, down_ref, sol_ref, wide_u,
+    wide_b, first, second, up3, up2, r_ref, tmp,
 ):
     widen(0, own_ref, xl_ref, xr_ref, yl_ref, yr_ref, wide_b)
-    widen(1, own_ref, xl_ref, xr_ref, yl_ref, yr_ref, wide_k)
-    coefficients(wide_k, cw, ca, cg)
-    sweeps(wide_b, cw, ca, cg, first, second)
+    widen(1, own_ref, xl_ref, xr_ref, yl_ref, yr_ref, wide_u)
+    sweeps(wide_b, wide_u, first, second)
     prolong(second, up3, up2)
     correct(second, up2, None, sol_ref)
 
     def resid(i):
         mid, a, b = ring_sum(sol_ref, 0, i + 1, 24, 1)
+        halves = []
         for h, t in enumerate((a, b)):
             s = mid[h * 24 : h * 24 + 16]
-            at = pl.ds(pl.multiple_of(i * 32 + h * 16, 16), 16)
-            f = own_ref[at, :]
-            k = own_ref[pl.ds(pl.multiple_of(OROWS + i * 32 + h * 16, 16), 16), :]
-            r_ref[at, :] = f - (k * (16.0 * s - 0.25 * t[:16]) + s)
-
-    loop(0, 16, resid, 2)
+            f = raw_ref[pl.ds(pl.multiple_of(i * 32 + h * 16, 16), 16), :]
+            k = raw_ref[pl.ds(pl.multiple_of(OROWS + i * 32 + h * 16, 16), 16), :]
+            halves.append(f - (k * (16.0 * s - 0.25 * t[:16]) + s))
+        return join(*halves)
+
+    loop(0, 16, resid, lambda i, new: put(r_ref, 0, i, 32, new))
     coarsen(r_ref, 0, 0, tmp, 0.125)
     coarsen(r_ref, 1, 0, tmp, 0.125)
-    x_faces(r_ref, 0, up_ref, down_ref, 0)
+    for at in range(0, OROWS, 32):
+        next_ref[pl.ds(at, 32), :] = w_ref[pl.ds(at, 32), :] * r_ref[pl.ds(at, 32), :]
+    x_faces(next_ref, 0, up_ref, down_ref, 0)
 
 
 def second_round(
-    f_ref, k_ref, own_ref, xl_ref, xr_ref, yl_ref, yr_ref, old_ref, cw, ca, cg,
-    out_ref, resid_ref,
-    wide_b, first, second, sol_ref, up3, up2,
+    fk_ref, own_ref, xl_ref, xr_ref, yl_ref, yr_ref, old_ref, wide_u,
+    out_hbm, resid_hbm,
+    wide_b, first, second, sol_ref, up3, up2, out_ref, resid_ref, sems,
 ):
     widen(0, own_ref, xl_ref, xr_ref, yl_ref, yr_ref, wide_b)
-    sweeps(wide_b, cw, ca, cg, first, second)
+    sweeps(wide_b, wide_u, first, second)
     prolong(second, up3, up2)
     correct(second, up2, old_ref, sol_ref)
+    for i in range(16):
+        out_ref[pl.ds(16 * i, 16), :] = sol_ref[pl.ds(48 * (i + 1), 16), :]
+    copies = [pltpu.make_async_copy(out_ref, out_hbm, sems.at[0])]
+    copies[0].start()
 
     def resid(i):
         mid, a, _ = ring_sum(sol_ref, 0, i + 1, 24, 1)
         s = mid[:16]
-        at = pl.ds(pl.multiple_of(i * 16, 16), 16)
-        out_ref[at, :] = s
-        resid_ref[at, :] = f_ref[at, :] - (k_ref[at, :] * (16.0 * s - 0.25 * a[:16]) + s)
-
-    loop(0, 16, resid, 2)
-
-
-def swap(up, down, axis):
+        return slab(fk_ref, 0, i, 16) - (slab(fk_ref, 256, i, 16) * (16.0 * s - 0.25 * a[:16]) + s)
+
+    for half in range(2):
+        loop(8 * half, 8 * half + 8, resid, lambda i, new: put(resid_ref, 0, i, 16, new))
+        at = pl.ds(128 * half, 128)
+        copies.append(pltpu.make_async_copy(resid_ref.at[at, :], resid_hbm.at[at, :], sems.at[1 + half]))
+        copies[-1].start()
+    for copy in copies:
+        copy.wait()
+
+
+def shift(up, down, axis):
     size = lax.axis_size(axis)
     rising = [(i, i + 1) for i in range(size - 1)]
     falling = [(j, i) for i, j in rising]
     return lax.ppermute(up, axis, rising), lax.ppermute(down, axis, falling)
 
 
+def swap(up, down, axis):
+    size = lax.axis_size(axis)
+    odd = lax.axis_index(axis) % 2 == 1
+    inner = [(i, i ^ 1) for i in range(size)]
+    outer = [(i, i + 1) for i in range(1, size - 1, 2)]
+    outer = outer + [(j, i) for i, j in outer]
+    one = lax.ppermute(jnp.where(odd, down, up), axis, inner)
+    two = lax.ppermute(jnp.where(odd, up, down), axis, outer)
+    return jnp.where(odd, one, two), jnp.where(odd, two, one)
+
+
 def shards(forcing, kappa):
     shape = forcing.shape
     f = forcing.reshape(256, LANES)
     k = kappa.reshape(256, LANES)
-    zl, zr = swap(*call(z_faces, [128, 128], [], f, k), "grp")
-    own, up, down = call(begin, [2 * OROWS, 2 * XROWS, 2 * XROWS], [256], f, k, zl, zr)
-    xl, xr = swap(up, down, "gx")
+    fk = lax.optimization_barrier(jnp.concatenate([f, k]))
+    up, down = call(z_faces, [128, 128], [], fk)
+    zl, zr = shift(up, down, "grp")
+    raw, own, w, up, down = call(
+        begin, [2 * OROWS, 2 * OROWS, OROWS, 2 * PACKED, 2 * PACKED], [256], fk, zl, zr
+    )
+    xl, xr = shift(up, down, "gx")
 
     def faces(fields, own, xl, xr):
         def kernel(*refs):
             y_faces(fields, *refs)
 
-        return call(kernel, [fields * YROWS] * 2, [], own, xl, xr)
-
-    yl, yr = swap(*faces(2, own, xl, xr), "gy")
-    r, up, down, sol, cw, ca, cg = call(
+        return call(kernel, [fields * YROWS] * 2 + [fields * XROWS] * 2, [], own, xl, xr)
+
+    up, down, xl, xr = faces(2, own, xl, xr)
+    yl, yr = swap(up, down, "gy")
+    own, up, down, sol, wide_u = call(
         first_round,
-        [OROWS, XROWS, XROWS, SOLROWS, WROWS, WROWS, WROWS],
-        [WROWS, WROWS, WROWS, WROWS, 192, 480, 256],
-        own, xl, xr, yl, yr,
+        [OROWS, PACKED, PACKED, SOLROWS, WROWS],
+        [WROWS, WROWS, WROWS, 192, 480, OROWS, 256],
+        raw, own, w, xl, xr, yl, yr,
     )
-    xl, xr = swap(up, down, "gx")
-    yl, yr = swap(*faces(1, r, xl, xr), "gy")
+    xl, xr = shift(up, down, "gx")
+    up, down, xl, xr = faces(1, own, xl, xr)
+    yl, yr = swap(up, down, "gy")
     out, resid = call(
         second_round,
         [256, 256],
-        [WROWS, WROWS, WROWS, SOLROWS, 192, 480],
-        f, k, r, xl, xr, yl, yr, sol, cw, ca, cg,
+        [WROWS, WROWS, WROWS, SOLROWS, 192, 480, 256, 256],
+        fk, own, xl, xr, yl, yr, sol, wide_u,
+        out_specs=[HBM, HBM], copies=3,
     )
     return out.reshape(shape), resid.reshape(shape)
 

time: 82.4 us -> 62.8 us (0.76)
  the two profiles are of different devices: /device:TPU:243 before, /device:TPU:250 now
where the time goes in v2:
time: 62.8 us; the launch traced here: 62.4 us
  starting transfers between devices  27.9 us (44%)
  waiting for transfers between devices  25.7 us (41%)
  Pallas kernels  7 us (11%)
  other arithmetic  1.11 us (2%)
  between operations  0.78 us (1%)
    ppermute x6, starting transfers between devices, shift(): return (lax.ppermute(up, axis, rising), lax.ppermute(down, axis, falling))  20.2 us
    ppermute x6, waiting for transfers between devices, shift(): return (lax.ppermute(up, axis, rising), lax.ppermute(down, axis, falling))  19 us
    pallas_call x6, Pallas kernels, call(): pl.pallas_call(kernel, out_shape=[jax.ShapeDtypeStruct((rows, LANES), F32...  7 us
    ppermute x2, waiting for transfers between devices, swap(): two = lax.ppermute(jnp.where(odd, up, down), axis, outer)  6.66 us
    ppermute x2, starting transfers between devices, swap(): two = lax.ppermute(jnp.where(odd, up, down), axis, outer)  3.84 us
    ppermute x2, starting transfers between devices, swap(): one = lax.ppermute(jnp.where(odd, down, up), axis, inner)  3.84 us
  transfers between devices with their start and end apart: 10, of which 8 were waited for; matrix products, arithmetic and copies ran while one was open for 0% of the time, Pallas kernels for 0%

profile of v2, /device:TPU:250, one launch (start us, length us, event | category | flops | bytes accessed | tf_op | source)
XLA Modules:
  0.0 62.4 jit_solution(6872513465990561172)
XLA Ops:
  0.6 1.0 %pad_maximum_fusion.fk_ref = f32[512,128]{1,0:T(8,128)S(1)} fusion(f32[256,128]{1,0:T(8,128)} %bitcast.4, f32[256,128]{1,0:T(8,128)} %bitcast.5), kind=kLoop, calls=%fused_computation | loop fusion | flops 65536 | bytes 524288 | tf_op jit(solution)/shard_map/concatenate | solution.py:370
  1.6 0.2 shard_map.41
  1.8 3.4 %collective-permute-start = (f32[128,128]{1,0:T(8,128)S(1)}, f32[128,128]{1,0:T(8,128)S(1)}, u32[]{:S(2)}, u32[]{:S(2)}) collective-permute-start(f32[128,128]{1,0:T(8,128)S(1)} %get-tuple-element.24), channel_id=1, source_target_pairs={{0,128},{128,256},{256,384},{1,129},{129,257},{257,385},{2,130},{1... | collective-permute-start | bytes 196616 | tf_op jit(solution)/shard_map/ppermute | solution.py:352
  5.2 2.4 %collective-permute-start.1 = (f32[128,128]{1,0:T(8,128)S(1)}, f32[128,128]{1,0:T(8,128)S(1)}, u32[]{:S(2)}, u32[]{:S(2)}) collective-permute-start(f32[128,128]{1,0:T(8,128)S(1)} %get-tuple-element.25), channel_id=1, source_target_pairs={{128,0},{256,128},{384,256},{129,1},{257,129},{385,257},{130,2},{2... | collective-permute-start | bytes 196616 | tf_op jit(solution)/shard_map/ppermute | solution.py:352
  7.6 0.3 collective-permute-done.zl_ref
  7.9 3.4 %collective-permute-done.1.zr_ref = f32[128,128]{1,0:T(8,128)S(1)} collective-permute-done((f32[128,128]{1,0:T(8,128)S(1)}, f32[128,128]{1,0:T(8,128)S(1)}, u32[]{:S(2)}, u32[]{:S(2)}) %collective-permute-start.1) | collective-permute-done | bytes 65568 | tf_op jit(solution)/shard_map/ppermute | solution.py:352
  11.4 0.5 shard_map.42
  11.8 5.7 %collective-permute-start.2 = (f32[224,128]{1,0:T(8,128)S(1)}, f32[224,128]{1,0:T(8,128)S(1)}, u32[]{:S(2)}, u32[]{:S(2)}) collective-permute-start(f32[224,128]{1,0:T(8,128)S(1)} %get-tuple-element.29), channel_id=1, source_target_pairs={{0,4},{4,8},{8,12},{12,16},{16,20},{20,24},{24,28},{28,32},{32,36}... | collective-permute-start | bytes 344072 | tf_op jit(solution)/shard_map/ppermute | solution.py:352
  17.5 1.9 %collective-permute-start.3 = (f32[224,128]{1,0:T(8,128)S(1)}, f32[224,128]{1,0:T(8,128)S(1)}, u32[]{:S(2)}, u32[]{:S(2)}) collective-permute-start(f32[224,128]{1,0:T(8,128)S(1)} %get-tuple-element.30), channel_id=1, source_target_pairs={{4,0},{8,4},{12,8},{16,12},{20,16},{24,20},{28,24},{32,28},{36,32}... | collective-permute-start | bytes 344072 | tf_op jit(solution)/shard_map/ppermute | solution.py:352
  19.5 1.7 %collective-permute-done.2.refs_1_ = f32[224,128]{1,0:T(8,128)S(1)} collective-permute-done((f32[224,128]{1,0:T(8,128)S(1)}, f32[224,128]{1,0:T(8,128)S(1)}, u32[]{:S(2)}, u32[]{:S(2)}) %collective-permute-start.2) | collective-permute-done | bytes 114720 | tf_op jit(solution)/shard_map/ppermute | solution.py:352
  21.2 8.1 %collective-permute-done.3.refs_2_ = f32[224,128]{1,0:T(8,128)S(1)} collective-permute-done((f32[224,128]{1,0:T(8,128)S(1)}, f32[224,128]{1,0:T(8,128)S(1)}, u32[]{:S(2)}, u32[]{:S(2)}) %collective-permute-start.3) | collective-permute-done | bytes 114720 | tf_op jit(solution)/shard_map/ppermute | solution.py:352
  29.3 0.3 shard_map.43
  29.7 1.9 %collective-permute-start.5 = (f32[560,128]{1,0:T(8,128)S(1)}, f32[560,128]{1,0:T(8,128)S(1)}, u32[]{:S(2)}, u32[]{:S(2)}) collective-permute-start(f32[560,128]{1,0:T(8,128)S(1)} %get-tuple-element.48), channel_id=1, source_target_pairs={{1,2},{2,1},{5,6},{6,5},{9,10},{10,9},{13,14},{14,13},{17,18},{18,... | collective-permute-start | bytes 860168 | tf_op jit(solution)/shard_map/ppermute | solution.py:362
  31.6 1.9 %collective-permute-start.4 = (f32[560,128]{1,0:T(8,128)S(1)}, f32[560,128]{1,0:T(8,128)S(1)}, u32[]{:S(2)}, u32[]{:S(2)}) collective-permute-start(f32[560,128]{1,0:T(8,128)S(1)} %get-tuple-element.49), channel_id=1, source_target_pairs={{0,1},{1,0},{2,3},{3,2},{4,5},{5,4},{6,7},{7,6},{8,9},{9,8},{10,11... | collective-permute-start | bytes 860168 | tf_op jit(solution)/shard_map/ppermute | solution.py:361
  33.5 4.1 %collective-permute-done.5 = f32[560,128]{1,0:T(8,128)S(1)} collective-permute-done((f32[560,128]{1,0:T(8,128)S(1)}, f32[560,128]{1,0:T(8,128)S(1)}, u32[]{:S(2)}, u32[]{:S(2)}) %collective-permute-start.5) | collective-permute-done | bytes 286752 | tf_op jit(solution)/shard_map/ppermute | solution.py:362
  37.6 0.0 collective-permute-done.4
  37.7 2.7 %shard_map.44 = (f32[672,128]{1,0:T(8,128)S(1)}, f32[112,128]{1,0:T(8,128)S(1)}, f32[112,128]{1,0:T(8,128)S(1)}, f32[864,128]{1,0:T(8,128)S(1)}, f32[1824,128]{1,0:T(8,128)S(1)}) custom-call(f32[1344,128]{1,0:T(8,128)S(1)} %get-tuple-element.26.raw_ref, f32[1344,128]{1,0:T(8,128)S(1)} %get-tuple-element.27.refs_0_.own_ref, ...), custom_call_target="tpu_custom_call" | custom-call | tf_op jit(solution)/shard_map/pallas_call | solution.py:40
  40.4 1.9 %collective-permute-start.6 = (f32[112,128]{1,0:T(8,128)S(1)}, f32[112,128]{1,0:T(8,128)S(1)}, u32[]{:S(2)}, u32[]{:S(2)}) collective-permute-start(f32[112,128]{1,0:T(8,128)S(1)} %get-tuple-element.36), channel_id=1, source_target_pairs={{0,4},{4,8},{8,12},{12,16},{16,20},{20,24},{24,28},{28,32},{32,36}... | collective-permute-start | bytes 172040 | tf_op jit(solution)/shard_map/ppermute | solution.py:352
  42.3 4.8 %collective-permute-start.7 = (f32[112,128]{1,0:T(8,128)S(1)}, f32[112,128]{1,0:T(8,128)S(1)}, u32[]{:S(2)}, u32[]{:S(2)}) collective-permute-start(f32[112,128]{1,0:T(8,128)S(1)} %get-tuple-element.37), channel_id=1, source_target_pairs={{4,0},{8,4},{12,8},{16,12},{20,16},{24,20},{28,24},{32,28},{36,32}... | collective-permute-start | bytes 172040 | tf_op jit(solution)/shard_map/ppermute | solution.py:352
  47.2 0.2 collective-permute-done.6.refs_1_
  47.4 5.2 %collective-permute-done.7.refs_2_ = f32[112,128]{1,0:T(8,128)S(1)} collective-permute-done((f32[112,128]{1,0:T(8,128)S(1)}, f32[112,128]{1,0:T(8,128)S(1)}, u32[]{:S(2)}, u32[]{:S(2)}) %collective-permute-start.7) | collective-permute-done | bytes 57376 | tf_op jit(solution)/shard_map/ppermute | solution.py:352
  52.6 0.1 shard_map.45
  52.8 1.9 %collective-permute-start.9 = (f32[280,128]{1,0:T(8,128)S(1)}, f32[280,128]{1,0:T(8,128)S(1)}, u32[]{:S(2)}, u32[]{:S(2)}) collective-permute-start(f32[280,128]{1,0:T(8,128)S(1)} %get-tuple-element.52), channel_id=1, source_target_pairs={{1,2},{2,1},{5,6},{6,5},{9,10},{10,9},{13,14},{14,13},{17,18},{18,... | collective-permute-start | bytes 430088 | tf_op jit(solution)/shard_map/ppermute | solution.py:362
  54.7 1.9 %collective-permute-start.8 = (f32[280,128]{1,0:T(8,128)S(1)}, f32[280,128]{1,0:T(8,128)S(1)}, u32[]{:S(2)}, u32[]{:S(2)}) collective-permute-start(f32[280,128]{1,0:T(8,128)S(1)} %get-tuple-element.53), channel_id=1, source_target_pairs={{0,1},{1,0},{2,3},{3,2},{4,5},{5,4},{6,7},{7,6},{8,9},{9,8},{10,11... | collective-permute-start | bytes 430088 | tf_op jit(solution)/shard_map/ppermute | solution.py:361
  56.7 2.6 %collective-permute-done.9 = f32[280,128]{1,0:T(8,128)S(1)} collective-permute-done((f32[280,128]{1,0:T(8,128)S(1)}, f32[280,128]{1,0:T(8,128)S(1)}, u32[]{:S(2)}, u32[]{:S(2)}) %collective-permute-start.9) | collective-permute-done | bytes 143392 | tf_op jit(solution)/shard_map/ppermute | solution.py:362
  59.2 0.0 collective-permute-done.8
  59.2 3.2 %shard_map.46 = (f32[256,128]{1,0:T(8,128)}, f32[256,128]{1,0:T(8,128)}) custom-call(f32[512,128]{1,0:T(8,128)S(1)} %pad_maximum_fusion.fk_ref, f32[672,128]{1,0:T(8,128)S(1)} %get-tuple-element.35.refs_0_.own_ref, f32[168,128]{1,0:T(8,128)S(1)} %get-tuple-element.38.xl_ref, f32[168,128]{1,0:T(8,128)S(1)} %get-tuple-element.39.xr_ref, ...), custom_call_target="tpu_custom_call" | custom-call | tf_op jit(solution)/shard_map/pallas_call | solution.py:40
  (4 shorter events, 0.1 us)
Async XLA Ops:
  1.8 6.2 %collective-permute-start = (f32[128,128]{1,0:T(8,128)S(1)}, f32[128,128]{1,0:T(8,128)S(1)}, u32[]{:S(2)}, u32[]{:S(2)}) collective-permute-start(f32[128,128]{1,0:T(8,128)S(1)} %get-tuple-element.24), channel_id=1, source_target_pairs={{0,128},{128,256},{256,384},{1,129},{129,257},{257,385},{2,130},{1... | collective-permute-start | bytes 196616 | tf_op jit(solution)/shard_map/ppermute | solution.py:352
  5.2 6.2 %collective-permute-start.1 = (f32[128,128]{1,0:T(8,128)S(1)}, f32[128,128]{1,0:T(8,128)S(1)}, u32[]{:S(2)}, u32[]{:S(2)}) collective-permute-start(f32[128,128]{1,0:T(8,128)S(1)} %get-tuple-element.25), channel_id=1, source_target_pairs={{128,0},{256,128},{384,256},{129,1},{257,129},{385,257},{130,2},{2... | collective-permute-start | bytes 196616 | tf_op jit(solution)/shard_map/ppermute | solution.py:352
  11.8 9.4 %collective-permute-start.2 = (f32[224,128]{1,0:T(8,128)S(1)}, f32[224,128]{1,0:T(8,128)S(1)}, u32[]{:S(2)}, u32[]{:S(2)}) collective-permute-start(f32[224,128]{1,0:T(8,128)S(1)} %get-tuple-element.29), channel_id=1, source_target_pairs={{0,4},{4,8},{8,12},{12,16},{16,20},{20,24},{24,28},{28,32},{32,36}... | collective-permute-start | bytes 344072 | tf_op jit(solution)/shard_map/ppermute | solution.py:352
  17.5 11.8 %collective-permute-start.3 = (f32[224,128]{1,0:T(8,128)S(1)}, f32[224,128]{1,0:T(8,128)S(1)}, u32[]{:S(2)}, u32[]{:S(2)}) collective-permute-start(f32[224,128]{1,0:T(8,128)S(1)} %get-tuple-element.30), channel_id=1, source_target_pairs={{4,0},{8,4},{12,8},{16,12},{20,16},{24,20},{28,24},{32,28},{36,32}... | collective-permute-start | bytes 344072 | tf_op jit(solution)/shard_map/ppermute | solution.py:352
  29.7 8.0 %collective-permute-start.5 = (f32[560,128]{1,0:T(8,128)S(1)}, f32[560,128]{1,0:T(8,128)S(1)}, u32[]{:S(2)}, u32[]{:S(2)}) collective-permute-start(f32[560,128]{1,0:T(8,128)S(1)} %get-tuple-element.48), channel_id=1, source_target_pairs={{1,2},{2,1},{5,6},{6,5},{9,10},{10,9},{13,14},{14,13},{17,18},{18,... | collective-permute-start | bytes 860168 | tf_op jit(solution)/shard_map/ppermute | solution.py:362
  31.6 6.0 %collective-permute-start.4 = (f32[560,128]{1,0:T(8,128)S(1)}, f32[560,128]{1,0:T(8,128)S(1)}, u32[]{:S(2)}, u32[]{:S(2)}) collective-permute-start(f32[560,128]{1,0:T(8,128)S(1)} %get-tuple-element.49), channel_id=1, source_target_pairs={{0,1},{1,0},{2,3},{3,2},{4,5},{5,4},{6,7},{7,6},{8,9},{9,8},{10,11... | collective-permute-start | bytes 860168 | tf_op jit(solution)/shard_map/ppermute | solution.py:361
  40.4 7.0 %collective-permute-start.6 = (f32[112,128]{1,0:T(8,128)S(1)}, f32[112,128]{1,0:T(8,128)S(1)}, u32[]{:S(2)}, u32[]{:S(2)}) collective-permute-start(f32[112,128]{1,0:T(8,128)S(1)} %get-tuple-element.36), channel_id=1, source_target_pairs={{0,4},{4,8},{8,12},{12,16},{16,20},{20,24},{24,28},{28,32},{32,36}... | collective-permute-start | bytes 172040 | tf_op jit(solution)/shard_map/ppermute | solution.py:352
  42.3 10.3 %collective-permute-start.7 = (f32[112,128]{1,0:T(8,128)S(1)}, f32[112,128]{1,0:T(8,128)S(1)}, u32[]{:S(2)}, u32[]{:S(2)}) collective-permute-start(f32[112,128]{1,0:T(8,128)S(1)} %get-tuple-element.37), channel_id=1, source_target_pairs={{4,0},{8,4},{12,8},{16,12},{20,16},{24,20},{28,24},{32,28},{36,32}... | collective-permute-start | bytes 172040 | tf_op jit(solution)/shard_map/ppermute | solution.py:352
  52.8 6.4 %collective-permute-start.9 = (f32[280,128]{1,0:T(8,128)S(1)}, f32[280,128]{1,0:T(8,128)S(1)}, u32[]{:S(2)}, u32[]{:S(2)}) collective-permute-start(f32[280,128]{1,0:T(8,128)S(1)} %get-tuple-element.52), channel_id=1, source_target_pairs={{1,2},{2,1},{5,6},{6,5},{9,10},{10,9},{13,14},{14,13},{17,18},{18,... | collective-permute-start | bytes 430088 | tf_op jit(solution)/shard_map/ppermute | solution.py:362
  54.7 4.5 %collective-permute-start.8 = (f32[280,128]{1,0:T(8,128)S(1)}, f32[280,128]{1,0:T(8,128)S(1)}, u32[]{:S(2)}, u32[]{:S(2)}) collective-permute-start(f32[280,128]{1,0:T(8,128)S(1)} %get-tuple-element.53), channel_id=1, source_target_pairs={{0,1},{1,0},{2,3},{3,2},{4,5},{5,4},{6,7},{7,6},{8,9},{9,8},{10,11... | collective-permute-start | bytes 430088 | tf_op jit(solution)/shard_map/ppermute | solution.py:361

commit v3 on v2

--- a/solution.py
+++ b/solution.py
@@ -345,11 +345,15 @@
         copy.wait()
 
 
-def shift(up, down, axis):
+def exchange(up, down, axis):
     size = lax.axis_size(axis)
-    rising = [(i, i + 1) for i in range(size - 1)]
-    falling = [(j, i) for i, j in rising]
-    return lax.ppermute(up, axis, rising), lax.ppermute(down, axis, falling)
+    odd = lax.axis_index(axis) % 2 == 1
+    outer = [(i, i + 1) for i in range(1, size - 1, 2)]
+    outer = outer + [(j, i) for i, j in outer]
+    inner = [[i, i + 1] for i in range(0, size, 2)]
+    two = lax.ppermute(jnp.where(odd, up, down), axis, outer)
+    one = lax.all_gather(jnp.where(odd, down, up), axis, axis_index_groups=inner)
+    return jnp.where(odd, one[0], two), jnp.where(odd, two, one[1])
 
 
 def swap(up, down, axis):
@@ -369,11 +373,11 @@
     k = kappa.reshape(256, LANES)
     fk = lax.optimization_barrier(jnp.concatenate([f, k]))
     up, down = call(z_faces, [128, 128], [], fk)
-    zl, zr = shift(up, down, "grp")
+    zl, zr = exchange(up, down, "grp")
     raw, own, w, up, down = call(
         begin, [2 * OROWS, 2 * OROWS, OROWS, 2 * PACKED, 2 * PACKED], [256], fk, zl, zr
     )
-    xl, xr = shift(up, down, "gx")
+    xl, xr = exchange(up, down, "gx")
 
     def faces(fields, own, xl, xr):
         def kernel(*refs):
@@ -389,7 +393,7 @@
         [WROWS, WROWS, WROWS, 192, 480, OROWS, 256],
         raw, own, w, xl, xr, yl, yr,
     )
-    xl, xr = shift(up, down, "gx")
+    xl, xr = exchange(up, down, "gx")
     up, down, xl, xr = faces(1, own, xl, xr)
     yl, yr = swap(up, down, "gy")
     out, resid = call(

time: 62.8 us -> 56 us (0.89)
  the two profiles are of different devices: /device:TPU:250 before, /device:TPU:259 now
where the time goes in v3:
time: 56 us; the launch traced here: 55.6 us
  starting transfers between devices  26.5 us (47%)
  blocking collectives  16.4 us (29%)
  Pallas kernels  7.01 us (13%)
  waiting for transfers between devices  3.72 us (7%)
  other arithmetic  1.21 us (2%)
  between operations  0.82 us (1%)
    all_gather x3, blocking collectives, exchange(): lax.all_gather(jnp.where(odd, down, up), axis, axis_index_groups=inner)  16.4 us
    ppermute x3, starting transfers between devices, exchange(): two = lax.ppermute(jnp.where(odd, up, down), axis, outer)  13.4 us
    ppermute x2, starting transfers between devices, swap(): two = lax.ppermute(jnp.where(odd, up, down), axis, outer)  9.28 us
    pallas_call x6, Pallas kernels, call(): pl.pallas_call(kernel, out_shape=[jax.ShapeDtypeStruct((rows, LANES), F32...  7.01 us
    ppermute x2, starting transfers between devices, swap(): one = lax.ppermute(jnp.where(odd, down, up), axis, inner)  3.84 us
    ppermute x2, waiting for transfers between devices, swap(): two = lax.ppermute(jnp.where(odd, up, down), axis, outer)  3.22 us
  transfers between devices with their start and end apart: 7, of which 3 were waited for; matrix products, arithmetic and copies ran while one was open for 0% of the time, Pallas kernels for 0%

profile of v3, /device:TPU:259, one launch (start us, length us, event | category | flops | bytes accessed | tf_op | source)
XLA Modules:
  0.0 55.6 jit_solution(5445648830674290026)
XLA Ops:
  0.6 1.0 %pad_maximum_fusion.fk_ref = f32[512,128]{1,0:T(8,128)S(1)} fusion(f32[256,128]{1,0:T(8,128)} %bitcast.4, f32[256,128]{1,0:T(8,128)} %bitcast.5), kind=kLoop, calls=%fused_computation | loop fusion | flops 65536 | bytes 524288 | tf_op jit(solution)/shard_map/concatenate | solution.py:374
  1.6 0.2 shard_map.41
  1.8 3.1 %collective-permute-start = (f32[128,128]{1,0:T(8,128)S(1)}, f32[128,128]{1,0:T(8,128)S(1)}, u32[]{:S(2)}, u32[]{:S(2)}) collective-permute-start(f32[128,128]{1,0:T(8,128)S(1)} %get-tuple-element.63), channel_id=1, source_target_pairs={{128,256},{256,128},{129,257},{257,129},{130,258},{258,130},{131,2... | collective-permute-start | bytes 196616 | tf_op jit(solution)/shard_map/ppermute | solution.py:354
  5.0 3.8 %all-gather = f32[256,128]{1,0:T(8,128)S(1)} all-gather(f32[128,128]{1,0:T(8,128)S(1)} %get-tuple-element.62), channel_id=2, replica_groups={{0,128},{256,384},{1,129},{257,385},{2,130},{258,386},{3,131},{259,387}..., dimensions={0}, use_global_device_ids=true | all-gather | bytes 196608 | tf_op jit(solution)/shard_map/all_gather | solution.py:355
  8.8 0.0 collective-permute-done
  8.8 0.5 shard_map.42
  9.3 5.0 %collective-permute-start.1 = (f32[224,128]{1,0:T(8,128)S(1)}, f32[224,128]{1,0:T(8,128)S(1)}, u32[]{:S(2)}, u32[]{:S(2)}) collective-permute-start(f32[224,128]{1,0:T(8,128)S(1)} %get-tuple-element.57), channel_id=1, source_target_pairs={{4,8},{12,16},{20,24},{28,32},{36,40},{44,48},{52,56},{60,64},{68,... | collective-permute-start | bytes 344072 | tf_op jit(solution)/shard_map/ppermute | solution.py:354
  14.3 7.1 %all-gather.1 = f32[448,128]{1,0:T(8,128)S(1)} all-gather(f32[224,128]{1,0:T(8,128)S(1)} %get-tuple-element.56), channel_id=3, replica_groups={{0,4},{8,12},{16,20},{24,28},{32,36},{40,44},{48,52},{56,60},{64,68},{7..., dimensions={0}, use_global_device_ids=true | all-gather | bytes 344064 | tf_op jit(solution)/shard_map/all_gather | solution.py:355
  21.4 0.0 collective-permute-done.1
  21.4 0.3 shard_map.43
  21.8 5.1 %collective-permute-start.3 = (f32[560,128]{1,0:T(8,128)S(1)}, f32[560,128]{1,0:T(8,128)S(1)}, u32[]{:S(2)}, u32[]{:S(2)}) collective-permute-start(f32[560,128]{1,0:T(8,128)S(1)} %get-tuple-element.48), channel_id=1, source_target_pairs={{1,2},{2,1},{5,6},{6,5},{9,10},{10,9},{13,14},{14,13},{17,18},{18,... | collective-permute-start | bytes 860168 | tf_op jit(solution)/shard_map/ppermute | solution.py:366
  26.9 1.9 %collective-permute-start.2 = (f32[560,128]{1,0:T(8,128)S(1)}, f32[560,128]{1,0:T(8,128)S(1)}, u32[]{:S(2)}, u32[]{:S(2)}) collective-permute-start(f32[560,128]{1,0:T(8,128)S(1)} %get-tuple-element.49), channel_id=1, source_target_pairs={{0,1},{1,0},{2,3},{3,2},{4,5},{5,4},{6,7},{7,6},{8,9},{9,8},{10,11... | collective-permute-start | bytes 860168 | tf_op jit(solution)/shard_map/ppermute | solution.py:365
  28.8 2.4 %collective-permute-done.3 = f32[560,128]{1,0:T(8,128)S(1)} collective-permute-done((f32[560,128]{1,0:T(8,128)S(1)}, f32[560,128]{1,0:T(8,128)S(1)}, u32[]{:S(2)}, u32[]{:S(2)}) %collective-permute-start.3) | collective-permute-done | bytes 286752 | tf_op jit(solution)/shard_map/ppermute | solution.py:366
  31.2 0.0 collective-permute-done.2
  31.2 2.7 %shard_map.44 = (f32[672,128]{1,0:T(8,128)S(1)}, f32[112,128]{1,0:T(8,128)S(1)}, f32[112,128]{1,0:T(8,128)S(1)}, f32[864,128]{1,0:T(8,128)S(1)}, f32[1824,128]{1,0:T(8,128)S(1)}) custom-call(f32[1344,128]{1,0:T(8,128)S(1)} %get-tuple-element.26.raw_ref, f32[1344,128]{1,0:T(8,128)S(1)} %get-tuple-element.27.refs_0_.own_ref, ...), custom_call_target="tpu_custom_call" | custom-call | tf_op jit(solution)/shard_map/pallas_call | solution.py:40
  34.0 5.3 %collective-permute-start.4 = (f32[112,128]{1,0:T(8,128)S(1)}, f32[112,128]{1,0:T(8,128)S(1)}, u32[]{:S(2)}, u32[]{:S(2)}) collective-permute-start(f32[112,128]{1,0:T(8,128)S(1)} %get-tuple-element.65), channel_id=1, source_target_pairs={{4,8},{12,16},{20,24},{28,32},{36,40},{44,48},{52,56},{60,64},{68,... | collective-permute-start | bytes 172040 | tf_op jit(solution)/shard_map/ppermute | solution.py:354
  39.3 5.5 %all-gather.2 = f32[224,128]{1,0:T(8,128)S(1)} all-gather(f32[112,128]{1,0:T(8,128)S(1)} %get-tuple-element.64), channel_id=4, replica_groups={{0,4},{8,12},{16,20},{24,28},{32,36},{40,44},{48,52},{56,60},{64,68},{7..., dimensions={0}, use_global_device_ids=true | all-gather | bytes 172032 | tf_op jit(solution)/shard_map/all_gather | solution.py:355
  44.8 0.0 collective-permute-done.4
  44.8 0.1 shard_map.45
  45.0 4.2 %collective-permute-start.6 = (f32[280,128]{1,0:T(8,128)S(1)}, f32[280,128]{1,0:T(8,128)S(1)}, u32[]{:S(2)}, u32[]{:S(2)}) collective-permute-start(f32[280,128]{1,0:T(8,128)S(1)} %get-tuple-element.54), channel_id=1, source_target_pairs={{1,2},{2,1},{5,6},{6,5},{9,10},{10,9},{13,14},{14,13},{17,18},{18,... | collective-permute-start | bytes 430088 | tf_op jit(solution)/shard_map/ppermute | solution.py:366
  49.2 1.9 %collective-permute-start.5 = (f32[280,128]{1,0:T(8,128)S(1)}, f32[280,128]{1,0:T(8,128)S(1)}, u32[]{:S(2)}, u32[]{:S(2)}) collective-permute-start(f32[280,128]{1,0:T(8,128)S(1)} %get-tuple-element.55), channel_id=1, source_target_pairs={{0,1},{1,0},{2,3},{3,2},{4,5},{5,4},{6,7},{7,6},{8,9},{9,8},{10,11... | collective-permute-start | bytes 430088 | tf_op jit(solution)/shard_map/ppermute | solution.py:365
  51.1 0.8 %collective-permute-done.6 = f32[280,128]{1,0:T(8,128)S(1)} collective-permute-done((f32[280,128]{1,0:T(8,128)S(1)}, f32[280,128]{1,0:T(8,128)S(1)}, u32[]{:S(2)}, u32[]{:S(2)}) %collective-permute-start.6) | collective-permute-done | bytes 143392 | tf_op jit(solution)/shard_map/ppermute | solution.py:366
  51.9 0.5 collective-permute-done.5
  52.5 3.2 %shard_map.46 = (f32[256,128]{1,0:T(8,128)}, f32[256,128]{1,0:T(8,128)}) custom-call(f32[512,128]{1,0:T(8,128)S(1)} %pad_maximum_fusion.fk_ref, f32[672,128]{1,0:T(8,128)S(1)} %get-tuple-element.35.refs_0_.own_ref, f32[168,128]{1,0:T(8,128)S(1)} %get-tuple-element.38.xl_ref, f32[168,128]{1,0:T(8,128)S(1)} %get-tuple-element.39.xr_ref, ...), custom_call_target="tpu_custom_call" | custom-call | tf_op jit(solution)/shard_map/pallas_call | solution.py:40
  (10 shorter events, 0.2 us)
Async XLA Ops:
  1.8 6.9 %collective-permute-start = (f32[128,128]{1,0:T(8,128)S(1)}, f32[128,128]{1,0:T(8,128)S(1)}, u32[]{:S(2)}, u32[]{:S(2)}) collective-permute-start(f32[128,128]{1,0:T(8,128)S(1)} %get-tuple-element.63), channel_id=1, source_target_pairs={{128,256},{256,128},{129,257},{257,129},{130,258},{258,130},{131,2... | collective-permute-start | bytes 196616 | tf_op jit(solution)/shard_map/ppermute | solution.py:354
  9.3 12.1 %collective-permute-start.1 = (f32[224,128]{1,0:T(8,128)S(1)}, f32[224,128]{1,0:T(8,128)S(1)}, u32[]{:S(2)}, u32[]{:S(2)}) collective-permute-start(f32[224,128]{1,0:T(8,128)S(1)} %get-tuple-element.57), channel_id=1, source_target_pairs={{4,8},{12,16},{20,24},{28,32},{36,40},{44,48},{52,56},{60,64},{68,... | collective-permute-start | bytes 344072 | tf_op jit(solution)/shard_map/ppermute | solution.py:354
  21.8 9.4 %collective-permute-start.3 = (f32[560,128]{1,0:T(8,128)S(1)}, f32[560,128]{1,0:T(8,128)S(1)}, u32[]{:S(2)}, u32[]{:S(2)}) collective-permute-start(f32[560,128]{1,0:T(8,128)S(1)} %get-tuple-element.48), channel_id=1, source_target_pairs={{1,2},{2,1},{5,6},{6,5},{9,10},{10,9},{13,14},{14,13},{17,18},{18,... | collective-permute-start | bytes 860168 | tf_op jit(solution)/shard_map/ppermute | solution.py:366
  26.9 4.3 %collective-permute-start.2 = (f32[560,128]{1,0:T(8,128)S(1)}, f32[560,128]{1,0:T(8,128)S(1)}, u32[]{:S(2)}, u32[]{:S(2)}) collective-permute-start(f32[560,128]{1,0:T(8,128)S(1)} %get-tuple-element.49), channel_id=1, source_target_pairs={{0,1},{1,0},{2,3},{3,2},{4,5},{5,4},{6,7},{7,6},{8,9},{9,8},{10,11... | collective-permute-start | bytes 860168 | tf_op jit(solution)/shard_map/ppermute | solution.py:365
  34.0 10.8 %collective-permute-start.4 = (f32[112,128]{1,0:T(8,128)S(1)}, f32[112,128]{1,0:T(8,128)S(1)}, u32[]{:S(2)}, u32[]{:S(2)}) collective-permute-start(f32[112,128]{1,0:T(8,128)S(1)} %get-tuple-element.65), channel_id=1, source_target_pairs={{4,8},{12,16},{20,24},{28,32},{36,40},{44,48},{52,56},{60,64},{68,... | collective-permute-start | bytes 172040 | tf_op jit(solution)/shard_map/ppermute | solution.py:354
  45.0 7.0 %collective-permute-start.6 = (f32[280,128]{1,0:T(8,128)S(1)}, f32[280,128]{1,0:T(8,128)S(1)}, u32[]{:S(2)}, u32[]{:S(2)}) collective-permute-start(f32[280,128]{1,0:T(8,128)S(1)} %get-tuple-element.54), channel_id=1, source_target_pairs={{1,2},{2,1},{5,6},{6,5},{9,10},{10,9},{13,14},{14,13},{17,18},{18,... | collective-permute-start | bytes 430088 | tf_op jit(solution)/shard_map/ppermute | solution.py:366
  49.2 3.3 %collective-permute-start.5 = (f32[280,128]{1,0:T(8,128)S(1)}, f32[280,128]{1,0:T(8,128)S(1)}, u32[]{:S(2)}, u32[]{:S(2)}) collective-permute-start(f32[280,128]{1,0:T(8,128)S(1)} %get-tuple-element.55), channel_id=1, source_target_pairs={{0,1},{1,0},{2,3},{3,2},{4,5},{5,4},{6,7},{7,6},{8,9},{9,8},{10,11... | collective-permute-start | bytes 430088 | tf_op jit(solution)/shard_map/ppermute | solution.py:365

commit v4 on v3

--- a/solution.py
+++ b/solution.py
@@ -20,8 +20,10 @@
 XROWS = 168
 YBASE = (0, 132, 216)
 YROWS = 280
-PACKED = 112
+PACKED = (0, 96, 168)
+LAYERS = (3, 2)
 UNROLL = 8
+GROUPS = (4, 3)
 WBASE = (0, 1056, 1504)
 WROWS = 1824
 SOLROWS = 18 * 48
@@ -79,50 +81,70 @@
         ref[pl.ds(base + OBASE[level + 1] + a * half, half), :] = (pair + other) * scale
 
 
-def x_faces(own_ref, base, up_ref, down_ref, xbase):
-    centre = abs(lanes_of(16) - 63.5) < 32
+def x_faces(own_ref, base, up_ref, down_ref, xbase, count):
+    lane = lanes_of(16)
+    odd = lane % 2 == 1
+    turn = lanes_of(8) % 4
+    for dst, end in ((up_ref, 1), (down_ref, 0)):
+        at = [base + OBASE[level] + end * (N[level] - count) * OWN[level] for level in range(3)]
+        to = xbase
+        for i in range(count):
+            dst[pl.ds(to, 16), :] = own_ref[pl.ds(at[0] + 32 * i, 16), :]
+            to += 16
+        shared = own_ref[pl.ds(at[0] + 16, 16), :]
+        for i in range(1, count):
+            moved = pltpu.roll(own_ref[pl.ds(at[0] + 32 * i + 16, 16), :], 32 * i, 1)
+            shared = jnp.where((lane + 16) // 32 == i, moved, shared)
+        dst[pl.ds(to, 16), :] = shared
+        c = [own_ref[pl.ds(at[1] + 16 * i, 16), :] for i in range(count)]
+        dst[pl.ds(to + 16, 16), :] = jnp.where(odd, c[1], c[0])
+        to += 32
+        if count == 3:
+            dst[pl.ds(to, 8), :] = jnp.where(odd[:8], c[2][8:], c[2][:8])
+            to += 8
+        c = [own_ref[pl.ds(at[2] + 8 * i, 8), :] for i in range(count)]
+        shared = c[0]
+        for i in range(1, count):
+            shared = jnp.where(turn == i, c[i], shared)
+        dst[pl.ds(to, 8), :] = shared
+
+
+def unpack(src, at, dst, to, count, skip):
     odd = lanes_of(16) % 2 == 1
     turn = lanes_of(8) % 4
-    for dst, end in ((up_ref, 1), (down_ref, 0)):
-        at = [base + OBASE[level] + end * (N[level] - HALO) * OWN[level] for level in range(3)]
+    for level in range(3):
+        rows = OWN[level]
         for i in range(HALO):
-            dst[pl.ds(xbase + 16 * i, 16), :] = own_ref[pl.ds(at[0] + 32 * i, 16), :]
-        z = [own_ref[pl.ds(at[0] + 32 * i + 16, 16), :] for i in range(HALO)]
-        dst[pl.ds(xbase + 48, 16), :] = jnp.where(centre, pltpu.roll(z[1], 64, 1), z[0])
-        dst[pl.ds(xbase + 64, 16), :] = z[2]
-        c = [own_ref[pl.ds(at[1] + 16 * i, 16), :] for i in range(HALO)]
-        dst[pl.ds(xbase + 80, 16), :] = jnp.where(odd, c[1], c[0])
-        dst[pl.ds(xbase + 96, 8), :] = jnp.where(odd[:8], c[2][8:], c[2][:8])
-        c = [own_ref[pl.ds(at[2] + 8 * i, 8), :] for i in range(HALO)]
-        dst[pl.ds(xbase + 104, 8), :] = jnp.where(turn == 0, c[0], jnp.where(turn == 1, c[1], c[2]))
-
-
-def unpack(src, at, dst, to):
-    odd = lanes_of(16) % 2 == 1
-    turn = lanes_of(8) % 4
-    for i in range(HALO):
-        dst[pl.ds(to + 32 * i, 16), :] = src[pl.ds(at + 16 * i, 16), :]
-    z = src[pl.ds(at + 48, 16), :]
-    for i, value in enumerate((z, pltpu.roll(z, 64, 1), src[pl.ds(at + 64, 16), :])):
-        dst[pl.ds(to + 32 * i + 16, 16), :] = value
+            if not skip <= i < skip + count:
+                dst[pl.ds(to + XBASE[level] + rows * i, rows), :] = jnp.zeros((rows, LANES), F32)
+    to1, to2, to3 = (to + XBASE[level] + skip * OWN[level] for level in range(3))
+    for i in range(count):
+        dst[pl.ds(to1 + 32 * i, 16), :] = src[pl.ds(at, 16), :]
+        at += 16
+    shared = src[pl.ds(at, 16), :]
+    for i in range(count):
+        dst[pl.ds(to1 + 32 * i + 16, 16), :] = pltpu.roll(shared, LANES - 32 * i, 1) if i else shared
 
     def two(value):
         mask = odd[: value.shape[0]]
         return jnp.where(mask, pltpu.roll(value, 1, 1), value), jnp.where(mask, value, pltpu.roll(value, LANES - 1, 1))
 
-    first = two(src[pl.ds(at + 80, 16), :])
-    dst[pl.ds(to + 96, 16), :] = first[0]
-    dst[pl.ds(to + 112, 16), :] = first[1]
-    last = two(src[pl.ds(at + 96, 8), :])
-    dst[pl.ds(to + 128, 8), :] = last[0]
-    dst[pl.ds(to + 136, 8), :] = last[1]
-    c = src[pl.ds(at + 104, 8), :]
-    moved = {d: pltpu.roll(c, d % LANES, 1) if d else c for d in range(-2, 4)}
-    for i in range(HALO):
+    first = two(src[pl.ds(at + 16, 16), :])
+    dst[pl.ds(to2, 16), :] = first[0]
+    dst[pl.ds(to2 + 16, 16), :] = first[1]
+    at += 32
+    if count == 3:
+        last = two(src[pl.ds(at, 8), :])
+        dst[pl.ds(to2 + 32, 8), :] = last[0]
+        dst[pl.ds(to2 + 40, 8), :] = last[1]
+        at += 8
+    c = src[pl.ds(at, 8), :]
+    moved = {d: pltpu.roll(c, d % LANES, 1) if d else c for d in range(1 - count, 4)}
+    for i in range(count):
         value = moved[-i]
         for lane in range(1, 4):
             value = jnp.where(turn == lane, moved[lane - i], value)
-        dst[pl.ds(to + 144 + 8 * i, 8), :] = value
+        dst[pl.ds(to3 + 8 * i, 8), :] = value
 
 
 def begin(fk_ref, zl_ref, zr_ref, raw_ref, own_ref, w_ref, up_ref, down_ref, tmp):
@@ -149,14 +171,15 @@
         own_ref[pl.ds(at, 32), :] = w * raw_ref[pl.ds(at, 32), :]
         own_ref[pl.ds(OROWS + at, 32), :] = 0.25 * (w * c)
     for field in range(2):
-        x_faces(own_ref, field * OROWS, up_ref, down_ref, field * PACKED)
+        x_faces(own_ref, field * OROWS, up_ref, down_ref, PACKED[field], LAYERS[field])
 
 
 def y_faces(fields, own_ref, xl_packed, xr_packed, up_ref, down_ref, xl_ref, xr_ref):
     for field in range(fields):
         ob, xb, yb = field * OROWS, field * XROWS, field * YROWS
-        unpack(xl_packed, field * PACKED, xl_ref, xb)
-        unpack(xr_packed, field * PACKED, xr_ref, xb)
+        count = LAYERS[field]
+        unpack(xl_packed, PACKED[field], xl_ref, xb, count, HALO - count)
+        unpack(xr_packed, PACKED[field], xr_ref, xb, count, 0)
         for dst, first in ((up_ref, False), (down_ref, True)):
             for level in range(3):
                 n, rows = N[level], OWN[level]
@@ -245,19 +268,27 @@
 
 
 def sweeps(wide_b, wide_u, first, second):
-    for level in range(3):
-        rows, base, ring, step = WIDE[level], WBASE[level], RING[level], STEP[level]
-
-        def sweep(low, high, src, dst):
-            def value(i):
-                mid, a, b = ring_sum(src, base, i, ring, step)
-                around = slab(wide_u, base, i, rows) * (join(a, b) - 8.0 * mid)
-                return 0.2 * mid + slab(wide_b, base, i, rows) + around
-
-            loop(low, high, value, lambda i, new: put(dst, base, i, rows, new))
-
-        sweep(1, X[level] - 1, wide_b, first)
-        sweep(2, X[level] - 2, first, second)
+    def sweep(edge, groups, src, dst):
+        def value(level, i):
+            rows, base = WIDE[level], WBASE[level]
+            mid, a, b = ring_sum(src, base, i, RING[level], STEP[level])
+            around = slab(wide_u, base, i, rows) * (join(a, b) - 8.0 * mid)
+            return 0.2 * mid + slab(wide_b, base, i, rows) + around
+
+        def group(g):
+            done = []
+            for level in range(3):
+                high = X[level] - edge
+                size = -(-(high - edge) // groups)
+                start = jnp.minimum(edge + g * size, high - size)
+                done += [(level, start + u, value(level, start + u)) for u in range(size)]
+            for level, i, new in done:
+                put(dst, WBASE[level], i, WIDE[level], new)
+
+        pl.loop(0, groups)(group)
+
+    sweep(1, GROUPS[0], wide_b, first)
+    sweep(2, GROUPS[1], first, second)
 
 
 def prolong(err, up3, up2):
@@ -314,7 +345,7 @@
     coarsen(r_ref, 1, 0, tmp, 0.125)
     for at in range(0, OROWS, 32):
         next_ref[pl.ds(at, 32), :] = w_ref[pl.ds(at, 32), :] * r_ref[pl.ds(at, 32), :]
-    x_faces(next_ref, 0, up_ref, down_ref, 0)
+    x_faces(next_ref, 0, up_ref, down_ref, 0, LAYERS[0])
 
 
 def second_round(
@@ -356,17 +387,6 @@
     return jnp.where(odd, one[0], two), jnp.where(odd, two, one[1])
 
 
-def swap(up, down, axis):
-    size = lax.axis_size(axis)
-    odd = lax.axis_index(axis) % 2 == 1
-    inner = [(i, i ^ 1) for i in range(size)]
-    outer = [(i, i + 1) for i in range(1, size - 1, 2)]
-    outer = outer + [(j, i) for i, j in outer]
-    one = lax.ppermute(jnp.where(odd, down, up), axis, inner)
-    two = lax.ppermute(jnp.where(odd, up, down), axis, outer)
-    return jnp.where(odd, one, two), jnp.where(odd, two, one)
-
-
 def shards(forcing, kappa):
     shape = forcing.shape
     f = forcing.reshape(256, LANES)
@@ -375,7 +395,7 @@
     up, down = call(z_faces, [128, 128], [], fk)
     zl, zr = exchange(up, down, "grp")
     raw, own, w, up, down = call(
-        begin, [2 * OROWS, 2 * OROWS, OROWS, 2 * PACKED, 2 * PACKED], [256], fk, zl, zr
+        begin, [2 * OROWS, 2 * OROWS, OROWS, PACKED[2], PACKED[2]], [256], fk, zl, zr
     )
     xl, xr = exchange(up, down, "gx")
 
@@ -386,16 +406,16 @@
         return call(kernel, [fields * YROWS] * 2 + [fields * XROWS] * 2, [], own, xl, xr)
 
     up, down, xl, xr = faces(2, own, xl, xr)
-    yl, yr = swap(up, down, "gy")
+    yl, yr = exchange(up, down, "gy")
     own, up, down, sol, wide_u = call(
         first_round,
-        [OROWS, PACKED, PACKED, SOLROWS, WROWS],
+        [OROWS, PACKED[1], PACKED[1], SOLROWS, WROWS],
         [WROWS, WROWS, WROWS, 192, 480, OROWS, 256],
         raw, own, w, xl, xr, yl, yr,
     )
     xl, xr = exchange(up, down, "gx")
     up, down, xl, xr = faces(1, own, xl, xr)
-    yl, yr = swap(up, down, "gy")
+    yl, yr = exchange(up, down, "gy")
     out, resid = call(
         second_round,
         [256, 256],

time: 56 us -> 54.4 us (0.971)
  the two profiles are of different devices: /device:TPU:259 before, /device:TPU:250 now
where the time goes in v4:
time: 54.4 us; the launch traced here: 54.1 us
  blocking collectives  21.7 us (40%)
  starting transfers between devices  17.6 us (32%)
  Pallas kernels  6.52 us (12%)
  waiting for transfers between devices  6.29 us (12%)
  other arithmetic  1.22 us (2%)
  between operations  0.8 us (1%)
    all_gather x5, blocking collectives, exchange(): lax.all_gather(jnp.where(odd, down, up), axis, axis_index_groups=inner)  21.7 us
    ppermute x5, starting transfers between devices, exchange(): two = lax.ppermute(jnp.where(odd, up, down), axis, outer)  17.6 us
    pallas_call x6, Pallas kernels, call(): pl.pallas_call(kernel, out_shape=[jax.ShapeDtypeStruct((rows, LANES), F32...  6.52 us
    ppermute x5, waiting for transfers between devices, exchange(): two = lax.ppermute(jnp.where(odd, up, down), axis, outer)  6.29 us
  transfers between devices with their start and end apart: 5, of which 2 were waited for; matrix products, arithmetic and copies ran while one was open for 0% of the time, Pallas kernels for 0%

profile of v4, /device:TPU:250, one launch (start us, length us, event | category | flops | bytes accessed | tf_op | source)
XLA Modules:
  0.0 54.1 jit_solution(8393679702491517826)
XLA Ops:
  0.6 1.0 %pad_maximum_fusion.fk_ref = f32[512,128]{1,0:T(8,128)S(1)} fusion(f32[256,128]{1,0:T(8,128)} %bitcast.4, f32[256,128]{1,0:T(8,128)} %bitcast.5), kind=kLoop, calls=%fused_computation.2 | loop fusion | flops 65536 | bytes 524288 | tf_op jit(solution)/shard_map/concatenate | solution.py:394
  1.6 0.2 shard_map.41
  1.8 3.4 %collective-permute-start = (f32[128,128]{1,0:T(8,128)S(1)}, f32[128,128]{1,0:T(8,128)S(1)}, u32[]{:S(2)}, u32[]{:S(2)}) collective-permute-start(f32[128,128]{1,0:T(8,128)S(1)} %get-tuple-element.63), channel_id=1, source_target_pairs={{128,256},{256,128},{129,257},{257,129},{130,258},{258,130},{131,2... | collective-permute-start | bytes 196616 | tf_op jit(solution)/shard_map/ppermute | solution.py:385
  5.2 4.9 %all-gather = f32[256,128]{1,0:T(8,128)S(1)} all-gather(f32[128,128]{1,0:T(8,128)S(1)} %get-tuple-element.62), channel_id=2, replica_groups={{0,128},{256,384},{1,129},{257,385},{2,130},{258,386},{3,131},{259,387}..., dimensions={0}, use_global_device_ids=true | all-gather | bytes 196608 | tf_op jit(solution)/shard_map/all_gather | solution.py:386
  10.2 0.0 collective-permute-done
  10.2 0.5 shard_map.42
  10.7 5.7 %collective-permute-start.1 = (f32[168,128]{1,0:T(8,128)S(1)}, f32[168,128]{1,0:T(8,128)S(1)}, u32[]{:S(2)}, u32[]{:S(2)}) collective-permute-start(f32[168,128]{1,0:T(8,128)S(1)} %get-tuple-element.59), channel_id=1, source_target_pairs={{4,8},{12,16},{20,24},{28,32},{36,40},{44,48},{52,56},{60,64},{68,... | collective-permute-start | bytes 258056 | tf_op jit(solution)/shard_map/ppermute | solution.py:385
  16.4 6.9 %all-gather.1 = f32[336,128]{1,0:T(8,128)S(1)} all-gather(f32[168,128]{1,0:T(8,128)S(1)} %get-tuple-element.58), channel_id=3, replica_groups={{0,4},{8,12},{16,20},{24,28},{32,36},{40,44},{48,52},{56,60},{64,68},{7..., dimensions={0}, use_global_device_ids=true | all-gather | bytes 258048 | tf_op jit(solution)/shard_map/all_gather | solution.py:386
  23.3 0.0 collective-permute-done.1
  23.3 0.3 shard_map.43
  23.7 1.9 %collective-permute-start.2 = (f32[560,128]{1,0:T(8,128)S(1)}, f32[560,128]{1,0:T(8,128)S(1)}, u32[]{:S(2)}, u32[]{:S(2)}) collective-permute-start(f32[560,128]{1,0:T(8,128)S(1)} %get-tuple-element.49), channel_id=1, source_target_pairs={{1,2},{2,1},{5,6},{6,5},{9,10},{10,9},{13,14},{14,13},{17,18},{18,... | collective-permute-start | bytes 860168 | tf_op jit(solution)/shard_map/ppermute | solution.py:385
  25.6 2.2 %all-gather.2 = f32[1120,128]{1,0:T(8,128)S(1)} all-gather(f32[560,128]{1,0:T(8,128)S(1)} %get-tuple-element.48), channel_id=4, replica_groups={{0,1},{2,3},{4,5},{6,7},{8,9},{10,11},{12,13},{14,15},{16,17},{18,19},{..., dimensions={0}, use_global_device_ids=true | all-gather | bytes 860160 | tf_op jit(solution)/shard_map/all_gather | solution.py:386
  27.8 3.8 %collective-permute-done.2 = f32[560,128]{1,0:T(8,128)S(1)} collective-permute-done((f32[560,128]{1,0:T(8,128)S(1)}, f32[560,128]{1,0:T(8,128)S(1)}, u32[]{:S(2)}, u32[]{:S(2)}) %collective-permute-start.2) | collective-permute-done | bytes 286752 | tf_op jit(solution)/shard_map/ppermute | solution.py:385
  31.7 2.6 %shard_map.44 = (f32[672,128]{1,0:T(8,128)S(1)}, f32[96,128]{1,0:T(8,128)S(1)}, f32[96,128]{1,0:T(8,128)S(1)}, f32[864,128]{1,0:T(8,128)S(1)}, f32[1824,128]{1,0:T(8,128)S(1)}) custom-call(f32[1344,128]{1,0:T(8,128)S(1)} %get-tuple-element.26.raw_ref, f32[1344,128]{1,0:T(8,128)S(1)} %get-tuple-element.27.refs_0_.own_ref, ...), custom_call_target="tpu_custom_call" | custom-call | tf_op jit(solution)/shard_map/pallas_call | solution.py:42
  34.3 4.6 %collective-permute-start.3 = (f32[96,128]{1,0:T(8,128)S(1)}, f32[96,128]{1,0:T(8,128)S(1)}, u32[]{:S(2)}, u32[]{:S(2)}) collective-permute-start(f32[96,128]{1,0:T(8,128)S(1)} %get-tuple-element.65), channel_id=1, source_target_pairs={{4,8},{12,16},{20,24},{28,32},{36,40},{44,48},{52,56},{60,64},{68,... | collective-permute-start | bytes 147464 | tf_op jit(solution)/shard_map/ppermute | solution.py:385
  38.9 5.7 %all-gather.3 = f32[192,128]{1,0:T(8,128)S(1)} all-gather(f32[96,128]{1,0:T(8,128)S(1)} %get-tuple-element.64), channel_id=5, replica_groups={{0,4},{8,12},{16,20},{24,28},{32,36},{40,44},{48,52},{56,60},{64,68},{7..., dimensions={0}, use_global_device_ids=true | all-gather | bytes 147456 | tf_op jit(solution)/shard_map/all_gather | solution.py:386
  44.6 0.0 collective-permute-done.3
  44.6 0.2 shard_map.45
  44.8 1.9 %collective-permute-start.4 = (f32[280,128]{1,0:T(8,128)S(1)}, f32[280,128]{1,0:T(8,128)S(1)}, u32[]{:S(2)}, u32[]{:S(2)}) collective-permute-start(f32[280,128]{1,0:T(8,128)S(1)} %get-tuple-element.53), channel_id=1, source_target_pairs={{1,2},{2,1},{5,6},{6,5},{9,10},{10,9},{13,14},{14,13},{17,18},{18,... | collective-permute-start | bytes 430088 | tf_op jit(solution)/shard_map/ppermute | solution.py:385
  46.7 2.0 %all-gather.4 = f32[560,128]{1,0:T(8,128)S(1)} all-gather(f32[280,128]{1,0:T(8,128)S(1)} %get-tuple-element.52), channel_id=6, replica_groups={{0,1},{2,3},{4,5},{6,7},{8,9},{10,11},{12,13},{14,15},{16,17},{18,19},{..., dimensions={0}, use_global_device_ids=true | all-gather | bytes 430080 | tf_op jit(solution)/shard_map/all_gather | solution.py:386
  48.7 2.5 %collective-permute-done.4 = f32[280,128]{1,0:T(8,128)S(1)} collective-permute-done((f32[280,128]{1,0:T(8,128)S(1)}, f32[280,128]{1,0:T(8,128)S(1)}, u32[]{:S(2)}, u32[]{:S(2)}) %collective-permute-start.4) | collective-permute-done | bytes 143392 | tf_op jit(solution)/shard_map/ppermute | solution.py:385
  51.2 2.9 %shard_map.46 = (f32[256,128]{1,0:T(8,128)}, f32[256,128]{1,0:T(8,128)}) custom-call(f32[512,128]{1,0:T(8,128)S(1)} %pad_maximum_fusion.fk_ref, f32[672,128]{1,0:T(8,128)S(1)} %get-tuple-element.35.refs_0_.own_ref, f32[168,128]{1,0:T(8,128)S(1)} %get-tuple-element.38.xl_ref, f32[168,128]{1,0:T(8,128)S(1)} %get-tuple-element.39.xr_ref, ...), custom_call_target="tpu_custom_call" | custom-call | tf_op jit(solution)/shard_map/pallas_call | solution.py:42
  (10 shorter events, 0.2 us)
Async XLA Ops:
  1.8 8.4 %collective-permute-start = (f32[128,128]{1,0:T(8,128)S(1)}, f32[128,128]{1,0:T(8,128)S(1)}, u32[]{:S(2)}, u32[]{:S(2)}) collective-permute-start(f32[128,128]{1,0:T(8,128)S(1)} %get-tuple-element.63), channel_id=1, source_target_pairs={{128,256},{256,128},{129,257},{257,129},{130,258},{258,130},{131,2... | collective-permute-start | bytes 196616 | tf_op jit(solution)/shard_map/ppermute | solution.py:385
  10.7 12.6 %collective-permute-start.1 = (f32[168,128]{1,0:T(8,128)S(1)}, f32[168,128]{1,0:T(8,128)S(1)}, u32[]{:S(2)}, u32[]{:S(2)}) collective-permute-start(f32[168,128]{1,0:T(8,128)S(1)} %get-tuple-element.59), channel_id=1, source_target_pairs={{4,8},{12,16},{20,24},{28,32},{36,40},{44,48},{52,56},{60,64},{68,... | collective-permute-start | bytes 258056 | tf_op jit(solution)/shard_map/ppermute | solution.py:385
  23.7 8.0 %collective-permute-start.2 = (f32[560,128]{1,0:T(8,128)S(1)}, f32[560,128]{1,0:T(8,128)S(1)}, u32[]{:S(2)}, u32[]{:S(2)}) collective-permute-start(f32[560,128]{1,0:T(8,128)S(1)} %get-tuple-element.49), channel_id=1, source_target_pairs={{1,2},{2,1},{5,6},{6,5},{9,10},{10,9},{13,14},{14,13},{17,18},{18,... | collective-permute-start | bytes 860168 | tf_op jit(solution)/shard_map/ppermute | solution.py:385
  34.3 10.3 %collective-permute-start.3 = (f32[96,128]{1,0:T(8,128)S(1)}, f32[96,128]{1,0:T(8,128)S(1)}, u32[]{:S(2)}, u32[]{:S(2)}) collective-permute-start(f32[96,128]{1,0:T(8,128)S(1)} %get-tuple-element.65), channel_id=1, source_target_pairs={{4,8},{12,16},{20,24},{28,32},{36,40},{44,48},{52,56},{60,64},{68,... | collective-permute-start | bytes 147464 | tf_op jit(solution)/shard_map/ppermute | solution.py:385
  44.8 6.4 %collective-permute-start.4 = (f32[280,128]{1,0:T(8,128)S(1)}, f32[280,128]{1,0:T(8,128)S(1)}, u32[]{:S(2)}, u32[]{:S(2)}) collective-permute-start(f32[280,128]{1,0:T(8,128)S(1)} %get-tuple-element.53), channel_id=1, source_target_pairs={{1,2},{2,1},{5,6},{6,5},{9,10},{10,9},{13,14},{14,13},{17,18},{18,... | collective-permute-start | bytes 430088 | tf_op jit(solution)/shard_map/ppermute | solution.py:385

commit v5 on v4

--- a/solution.py
+++ b/solution.py
@@ -18,8 +18,7 @@
 OROWS = 672
 XBASE = (0, 96, 144)
 XROWS = 168
-YBASE = (0, 132, 216)
-YROWS = 280
+YROWS = (0, 152, 256)
 PACKED = (0, 96, 168)
 LAYERS = (3, 2)
 UNROLL = 8
@@ -174,27 +173,77 @@
         x_faces(own_ref, field * OROWS, up_ref, down_ref, PACKED[field], LAYERS[field])
 
 
-def y_faces(fields, own_ref, xl_packed, xr_packed, up_ref, down_ref, xl_ref, xr_ref):
+def y_parts(count):
+    parts, at = [], 0
+    for j in range(count):
+        parts.append((at, 0, ((0, j),), None))
+        at += X[0]
+    parts.append((at, 0, tuple((1, j) for j in range(count)), "lanes"))
+    at += X[0]
+    for j in range(count):
+        parts.append((at, 1, ((0, j), (1, j)), "turns"))
+        at += X[1]
+    for j in range(0, count, 2):
+        members = tuple((h, k) for k in range(j, min(j + 2, count)) for h in range(2))
+        parts.append((at, 2, members, "turns"))
+        at += X[2]
+    return parts
+
+
+def share(vectors, how):
+    shared = vectors[0]
+    lane = lanes_of(shared.shape[0])
+    for i in range(1, len(vectors)):
+        if how == "lanes":
+            shared = jnp.where((lane + 16) // 32 == i, pltpu.roll(vectors[i], 32 * i, 1), shared)
+        else:
+            shared = jnp.where(lane % len(vectors) == i, vectors[i], shared)
+    return shared
+
+
+def unshare(shared, number, how):
+    if how != "turns":
+        return [pltpu.roll(shared, LANES - 32 * i, 1) if i else shared for i in range(number)]
+    turn = lanes_of(shared.shape[0]) % number
+    moved = {d: pltpu.roll(shared, d % LANES, 1) if d else shared for d in range(1 - number, number)}
+    vectors = []
+    for i in range(number):
+        value = moved[-i]
+        for lane in range(1, number):
+            value = jnp.where(turn == lane, moved[lane - i], value)
+        vectors.append(value)
+    return vectors
+
+
+def y_faces(fields, own_ref, xl_packed, xr_packed, up_ref, down_ref, xl_ref, xr_ref, rows_ref):
+    for ref in (up_ref, down_ref):
+        ref[pl.ds(150, 2), :] = jnp.zeros((2, LANES), F32)
     for field in range(fields):
-        ob, xb, yb = field * OROWS, field * XROWS, field * YROWS
-        count = LAYERS[field]
+        ob, xb, yb, count = field * OROWS, field * XROWS, YROWS[field], LAYERS[field]
         unpack(xl_packed, PACKED[field], xl_ref, xb, count, HALO - count)
         unpack(xr_packed, PACKED[field], xr_ref, xb, count, 0)
-        for dst, first in ((up_ref, False), (down_ref, True)):
-            for level in range(3):
-                n, rows = N[level], OWN[level]
-                for h in range(2):
-                    for j in range(HALO):
-                        row = h * n + (j if first else n - HALO + j)
-                        off = yb + YBASE[level] + (h * HALO + j) * X[level]
-                        dst[pl.ds(off, HALO), :] = xl_ref[pl.ds(xb + XBASE[level] + row, HALO, rows), :]
-                        dst[pl.ds(off + HALO, n), :] = own_ref[pl.ds(ob + OBASE[level] + row, n, rows), :]
-                        dst[pl.ds(off + HALO + n, HALO), :] = xr_ref[pl.ds(xb + XBASE[level] + row, HALO, rows), :]
-            dst[pl.ds(yb + 276, 4), :] = jnp.zeros((4, LANES), F32)
+        for side, (dst, first) in enumerate(((up_ref, False), (down_ref, True))):
+            for at, level, members, how in y_parts(count):
+                n, rows, size = N[level], OWN[level], X[level]
+                vectors = []
+                for m, (h, j) in enumerate(members):
+                    row = h * n + (j if first else n - count + j)
+                    to = 24 * (m + 4 * (side + 2 * field))
+                    if len(members) == 1:
+                        ref, to = dst, yb + at
+                    else:
+                        ref = rows_ref
+                    ref[pl.ds(to, HALO), :] = xl_ref[pl.ds(xb + XBASE[level] + row, HALO, rows), :]
+                    ref[pl.ds(to + HALO, n), :] = own_ref[pl.ds(ob + OBASE[level] + row, n, rows), :]
+                    ref[pl.ds(to + HALO + n, HALO), :] = xr_ref[pl.ds(xb + XBASE[level] + row, HALO, rows), :]
+                    if len(members) > 1:
+                        vectors.append(ref[pl.ds(to, size), :])
+                if vectors:
+                    dst[pl.ds(yb + at, size), :] = share(vectors, how)
 
 
 def widen(field, own_ref, xl_ref, xr_ref, yl_ref, yr_ref, wide_ref):
-    ob, xb, yb = field * OROWS, field * XROWS, field * YROWS
+    ob, xb, yb, count = field * OROWS, field * XROWS, YROWS[field], LAYERS[field]
     for level in range(3):
         n, ring, rows = N[level], RING[level], OWN[level]
         for i in range(X[level]):
@@ -208,12 +257,12 @@
                 to = WBASE[level] + i * WIDE[level] + h * ring
                 wide_ref[pl.ds(to, n), :] = ref[pl.ds(at + h * n, n), :]
                 wide_ref[pl.ds(to + n, ring - n), :] = jnp.zeros((ring - n, LANES), F32)
-        for h in range(2):
-            for j in range(HALO):
-                off = yb + YBASE[level] + (h * HALO + j) * X[level]
-                to = WBASE[level] + h * ring
-                wide_ref[pl.ds(to + n + j, X[level], WIDE[level]), :] = yr_ref[pl.ds(off, X[level]), :]
-                wide_ref[pl.ds(to + ring - HALO + j, X[level], WIDE[level]), :] = yl_ref[pl.ds(off, X[level]), :]
+    for at, level, members, how in y_parts(count):
+        n, ring, size = N[level], RING[level], X[level]
+        for ref, start in ((yr_ref, n), (yl_ref, ring - count)):
+            shared = ref[pl.ds(yb + at, size), :]
+            for (h, j), vector in zip(members, unshare(shared, len(members), how)):
+                wide_ref[pl.ds(WBASE[level] + h * ring + start + j, size, WIDE[level]), :] = vector
 
 
 def slab(ref, base, i, rows):
@@ -403,7 +452,7 @@
         def kernel(*refs):
             y_faces(fields, *refs)
 
-        return call(kernel, [fields * YROWS] * 2 + [fields * XROWS] * 2, [], own, xl, xr)
+        return call(kernel, [YROWS[fields]] * 2 + [fields * XROWS] * 2, [24 * 16], own, xl, xr)
 
     up, down, xl, xr = faces(2, own, xl, xr)
     yl, yr = exchange(up, down, "gy")

time: 54.4 us -> 51.9 us (0.954)
  waiting for transfers between devices: 6.29 us -> 4.24 us
    ppermute x5, waiting for transfers between devices: 6.29 us -> 4.24 us  [exchange(): two = lax.ppermute(jnp.where(odd, up, down), axis, outer)]
where the time goes in v5:
time: 51.9 us; the launch traced here: 51.6 us
  blocking collectives  21.4 us (41%)
  starting transfers between devices  17.6 us (34%)
  Pallas kernels  6.49 us (13%)
  waiting for transfers between devices  4.24 us (8%)
  other arithmetic  1.16 us (2%)
  between operations  0.79 us (2%)
    all_gather x5, blocking collectives, exchange(): lax.all_gather(jnp.where(odd, down, up), axis, axis_index_groups=inner)  21.4 us
    ppermute x5, starting transfers between devices, exchange(): two = lax.ppermute(jnp.where(odd, up, down), axis, outer)  17.6 us
    pallas_call x6, Pallas kernels, call(): pl.pallas_call(kernel, out_shape=[jax.ShapeDtypeStruct((rows, LANES), F32...  6.49 us
    ppermute x5, waiting for transfers between devices, exchange(): two = lax.ppermute(jnp.where(odd, up, down), axis, outer)  4.24 us
  transfers between devices with their start and end apart: 5, of which 2 were waited for; matrix products, arithmetic and copies ran while one was open for 0% of the time, Pallas kernels for 0%

profile of v5, /device:TPU:250, one launch (start us, length us, event | category | flops | bytes accessed | tf_op | source)
XLA Modules:
  0.0 51.6 jit_solution(17620190042811243093)
XLA Ops:
  0.6 1.0 %pad_maximum_fusion.fk_ref = f32[512,128]{1,0:T(8,128)S(1)} fusion(f32[256,128]{1,0:T(8,128)} %bitcast.4, f32[256,128]{1,0:T(8,128)} %bitcast.5), kind=kLoop, calls=%fused_computation | loop fusion | flops 65536 | bytes 524288 | tf_op jit(solution)/shard_map/concatenate | solution.py:443
  1.6 0.2 shard_map.41
  1.8 3.4 %collective-permute-start = (f32[128,128]{1,0:T(8,128)S(1)}, f32[128,128]{1,0:T(8,128)S(1)}, u32[]{:S(2)}, u32[]{:S(2)}) collective-permute-start(f32[128,128]{1,0:T(8,128)S(1)} %get-tuple-element.63), channel_id=1, source_target_pairs={{128,256},{256,128},{129,257},{257,129},{130,258},{258,130},{131,2... | collective-permute-start | bytes 196616 | tf_op jit(solution)/shard_map/ppermute | solution.py:434
  5.2 4.9 %all-gather = f32[256,128]{1,0:T(8,128)S(1)} all-gather(f32[128,128]{1,0:T(8,128)S(1)} %get-tuple-element.62), channel_id=2, replica_groups={{0,128},{256,384},{1,129},{257,385},{2,130},{258,386},{3,131},{259,387}..., dimensions={0}, use_global_device_ids=true | all-gather | bytes 196608 | tf_op jit(solution)/shard_map/all_gather | solution.py:435
  10.2 0.0 collective-permute-done
  10.2 0.5 shard_map.42
  10.7 5.7 %collective-permute-start.1 = (f32[168,128]{1,0:T(8,128)S(1)}, f32[168,128]{1,0:T(8,128)S(1)}, u32[]{:S(2)}, u32[]{:S(2)}) collective-permute-start(f32[168,128]{1,0:T(8,128)S(1)} %get-tuple-element.57), channel_id=1, source_target_pairs={{4,8},{12,16},{20,24},{28,32},{36,40},{44,48},{52,56},{60,64},{68,... | collective-permute-start | bytes 258056 | tf_op jit(solution)/shard_map/ppermute | solution.py:434
  16.4 6.9 %all-gather.1 = f32[336,128]{1,0:T(8,128)S(1)} all-gather(f32[168,128]{1,0:T(8,128)S(1)} %get-tuple-element.56), channel_id=3, replica_groups={{0,4},{8,12},{16,20},{24,28},{32,36},{40,44},{48,52},{56,60},{64,68},{7..., dimensions={0}, use_global_device_ids=true | all-gather | bytes 258048 | tf_op jit(solution)/shard_map/all_gather | solution.py:435
  23.3 0.0 collective-permute-done.1
  23.3 0.3 shard_map.43
  23.7 1.9 %collective-permute-start.2 = (f32[256,128]{1,0:T(8,128)S(1)}, f32[256,128]{1,0:T(8,128)S(1)}, u32[]{:S(2)}, u32[]{:S(2)}) collective-permute-start(f32[256,128]{1,0:T(8,128)S(1)} %get-tuple-element.49), channel_id=1, source_target_pairs={{1,2},{2,1},{5,6},{6,5},{9,10},{10,9},{13,14},{14,13},{17,18},{18,... | collective-permute-start | bytes 393224 | tf_op jit(solution)/shard_map/ppermute | solution.py:434
  25.6 2.0 %all-gather.2 = f32[512,128]{1,0:T(8,128)S(1)} all-gather(f32[256,128]{1,0:T(8,128)S(1)} %get-tuple-element.48), channel_id=4, replica_groups={{0,1},{2,3},{4,5},{6,7},{8,9},{10,11},{12,13},{14,15},{16,17},{18,19},{..., dimensions={0}, use_global_device_ids=true | all-gather | bytes 393216 | tf_op jit(solution)/shard_map/all_gather | solution.py:435
  27.6 2.4 %collective-permute-done.2 = f32[256,128]{1,0:T(8,128)S(1)} collective-permute-done((f32[256,128]{1,0:T(8,128)S(1)}, f32[256,128]{1,0:T(8,128)S(1)}, u32[]{:S(2)}, u32[]{:S(2)}) %collective-permute-start.2) | collective-permute-done | bytes 131104 | tf_op jit(solution)/shard_map/ppermute | solution.py:434
  30.0 2.5 %shard_map.44 = (f32[672,128]{1,0:T(8,128)S(1)}, f32[96,128]{1,0:T(8,128)S(1)}, f32[96,128]{1,0:T(8,128)S(1)}, f32[864,128]{1,0:T(8,128)S(1)}, f32[1824,128]{1,0:T(8,128)S(1)}) custom-call(f32[1344,128]{1,0:T(8,128)S(1)} %get-tuple-element.26.raw_ref, f32[1344,128]{1,0:T(8,128)S(1)} %get-tuple-element.27.refs_0_.own_ref, ...), custom_call_target="tpu_custom_call" | custom-call | tf_op jit(solution)/shard_map/pallas_call | solution.py:41
  32.5 4.6 %collective-permute-start.3 = (f32[96,128]{1,0:T(8,128)S(1)}, f32[96,128]{1,0:T(8,128)S(1)}, u32[]{:S(2)}, u32[]{:S(2)}) collective-permute-start(f32[96,128]{1,0:T(8,128)S(1)} %get-tuple-element.65), channel_id=1, source_target_pairs={{4,8},{12,16},{20,24},{28,32},{36,40},{44,48},{52,56},{60,64},{68,... | collective-permute-start | bytes 147464 | tf_op jit(solution)/shard_map/ppermute | solution.py:434
  37.1 5.7 %all-gather.3 = f32[192,128]{1,0:T(8,128)S(1)} all-gather(f32[96,128]{1,0:T(8,128)S(1)} %get-tuple-element.64), channel_id=5, replica_groups={{0,4},{8,12},{16,20},{24,28},{32,36},{40,44},{48,52},{56,60},{64,68},{7..., dimensions={0}, use_global_device_ids=true | all-gather | bytes 147456 | tf_op jit(solution)/shard_map/all_gather | solution.py:435
  42.8 0.0 collective-permute-done.3
  42.8 0.2 shard_map.45
  43.1 1.9 %collective-permute-start.4 = (f32[152,128]{1,0:T(8,128)S(1)}, f32[152,128]{1,0:T(8,128)S(1)}, u32[]{:S(2)}, u32[]{:S(2)}) collective-permute-start(f32[152,128]{1,0:T(8,128)S(1)} %get-tuple-element.59), channel_id=1, source_target_pairs={{1,2},{2,1},{5,6},{6,5},{9,10},{10,9},{13,14},{14,13},{17,18},{18,... | collective-permute-start | bytes 233480 | tf_op jit(solution)/shard_map/ppermute | solution.py:434
  45.0 1.9 %all-gather.4 = f32[304,128]{1,0:T(8,128)S(1)} all-gather(f32[152,128]{1,0:T(8,128)S(1)} %get-tuple-element.58), channel_id=6, replica_groups={{0,1},{2,3},{4,5},{6,7},{8,9},{10,11},{12,13},{14,15},{16,17},{18,19},{..., dimensions={0}, use_global_device_ids=true | all-gather | bytes 233472 | tf_op jit(solution)/shard_map/all_gather | solution.py:435
  46.9 1.9 %collective-permute-done.4 = f32[152,128]{1,0:T(8,128)S(1)} collective-permute-done((f32[152,128]{1,0:T(8,128)S(1)}, f32[152,128]{1,0:T(8,128)S(1)}, u32[]{:S(2)}, u32[]{:S(2)}) %collective-permute-start.4) | collective-permute-done | bytes 77856 | tf_op jit(solution)/shard_map/ppermute | solution.py:434
  48.8 2.8 %shard_map.46 = (f32[256,128]{1,0:T(8,128)}, f32[256,128]{1,0:T(8,128)}) custom-call(f32[512,128]{1,0:T(8,128)S(1)} %pad_maximum_fusion.fk_ref, f32[672,128]{1,0:T(8,128)S(1)} %get-tuple-element.35.refs_0_.own_ref, f32[168,128]{1,0:T(8,128)S(1)} %get-tuple-element.38.xl_ref, f32[168,128]{1,0:T(8,128)S(1)} %get-tuple-element.39.xr_ref, ...), custom_call_target="tpu_custom_call" | custom-call | tf_op jit(solution)/shard_map/pallas_call | solution.py:41
  (10 shorter events, 0.2 us)
Async XLA Ops:
  1.8 8.4 %collective-permute-start = (f32[128,128]{1,0:T(8,128)S(1)}, f32[128,128]{1,0:T(8,128)S(1)}, u32[]{:S(2)}, u32[]{:S(2)}) collective-permute-start(f32[128,128]{1,0:T(8,128)S(1)} %get-tuple-element.63), channel_id=1, source_target_pairs={{128,256},{256,128},{129,257},{257,129},{130,258},{258,130},{131,2... | collective-permute-start | bytes 196616 | tf_op jit(solution)/shard_map/ppermute | solution.py:434
  10.7 12.6 %collective-permute-start.1 = (f32[168,128]{1,0:T(8,128)S(1)}, f32[168,128]{1,0:T(8,128)S(1)}, u32[]{:S(2)}, u32[]{:S(2)}) collective-permute-start(f32[168,128]{1,0:T(8,128)S(1)} %get-tuple-element.57), channel_id=1, source_target_pairs={{4,8},{12,16},{20,24},{28,32},{36,40},{44,48},{52,56},{60,64},{68,... | collective-permute-start | bytes 258056 | tf_op jit(solution)/shard_map/ppermute | solution.py:434
  23.7 6.3 %collective-permute-start.2 = (f32[256,128]{1,0:T(8,128)S(1)}, f32[256,128]{1,0:T(8,128)S(1)}, u32[]{:S(2)}, u32[]{:S(2)}) collective-permute-start(f32[256,128]{1,0:T(8,128)S(1)} %get-tuple-element.49), channel_id=1, source_target_pairs={{1,2},{2,1},{5,6},{6,5},{9,10},{10,9},{13,14},{14,13},{17,18},{18,... | collective-permute-start | bytes 393224 | tf_op jit(solution)/shard_map/ppermute | solution.py:434
  32.5 10.3 %collective-permute-start.3 = (f32[96,128]{1,0:T(8,128)S(1)}, f32[96,128]{1,0:T(8,128)S(1)}, u32[]{:S(2)}, u32[]{:S(2)}) collective-permute-start(f32[96,128]{1,0:T(8,128)S(1)} %get-tuple-element.65), channel_id=1, source_target_pairs={{4,8},{12,16},{20,24},{28,32},{36,40},{44,48},{52,56},{60,64},{68,... | collective-permute-start | bytes 147464 | tf_op jit(solution)/shard_map/ppermute | solution.py:434
  43.1 5.7 %collective-permute-start.4 = (f32[152,128]{1,0:T(8,128)S(1)}, f32[152,128]{1,0:T(8,128)S(1)}, u32[]{:S(2)}, u32[]{:S(2)}) collective-permute-start(f32[152,128]{1,0:T(8,128)S(1)} %get-tuple-element.59), channel_id=1, source_target_pairs={{1,2},{2,1},{5,6},{6,5},{9,10},{10,9},{13,14},{14,13},{17,18},{18,... | collective-permute-start | bytes 233480 | tf_op jit(solution)/shard_map/ppermute | solution.py:434

commit v6 on v5

--- a/solution.py
+++ b/solution.py
@@ -22,7 +22,7 @@
 PACKED = (0, 96, 168)
 LAYERS = (3, 2)
 UNROLL = 8
-GROUPS = (4, 3)
+GROUPS = (3, 3)
 WBASE = (0, 1056, 1504)
 WROWS = 1824
 SOLROWS = 18 * 48
@@ -256,7 +256,6 @@
             for h in range(2):
                 to = WBASE[level] + i * WIDE[level] + h * ring
                 wide_ref[pl.ds(to, n), :] = ref[pl.ds(at + h * n, n), :]
-                wide_ref[pl.ds(to + n, ring - n), :] = jnp.zeros((ring - n, LANES), F32)
     for at, level, members, how in y_parts(count):
         n, ring, size = N[level], RING[level], X[level]
         for ref, start in ((yr_ref, n), (yl_ref, ring - count)):
@@ -299,17 +298,15 @@
     halves = []
     for h in range(2):
         t = total[h * ring : (h + 1) * ring]
-        t = t + pltpu.roll(t, 1, 0)
-        halves.append(t + pltpu.roll(t, ring - 1, 0))
+        halves.append(pltpu.roll(t, 1, 0) + pltpu.roll(t, ring - 1, 0) + (t + t))
     lane = lanes_of(ring)
     a, b = halves
     ra, rb = pltpu.roll(a, step, 1), pltpu.roll(b, step, 1)
-    edge = lane < step
-    a, b = a + jnp.where(edge, rb, ra), b + jnp.where(edge, ra, rb)
-    ra, rb = pltpu.roll(a, LANES - step, 1), pltpu.roll(b, LANES - step, 1)
-    edge = lane >= LANES - step
-    a, b = a + jnp.where(edge, rb, ra), b + jnp.where(edge, ra, rb)
-    return mid, a, b
+    sa, sb = pltpu.roll(a, LANES - step, 1), pltpu.roll(b, LANES - step, 1)
+    low, high = lane < step, lane >= LANES - step
+    new_a = a + a + jnp.where(low, rb, ra) + jnp.where(high, sb, sa)
+    new_b = b + b + jnp.where(low, ra, rb) + jnp.where(high, sa, sb)
+    return mid, new_a, new_b
 
 
 def join(a, b):

time: 51.9 us -> 51.3 us (0.988)
  Pallas kernels: 6.49 us -> 5.85 us
    pallas_call x6, Pallas kernels: 6.49 us -> 5.85 us  [call(): pl.pallas_call(kernel, out_shape=[jax.ShapeDtypeStruct((rows, LANES), F32...]
where the time goes in v6:
time: 51.3 us; the launch traced here: 51 us
  blocking collectives  21.4 us (42%)
  starting transfers between devices  17.6 us (34%)
  Pallas kernels  5.85 us (11%)
  waiting for transfers between devices  4.24 us (8%)
  other arithmetic  1.16 us (2%)
  between operations  0.79 us (2%)
    all_gather x5, blocking collectives, exchange(): lax.all_gather(jnp.where(odd, down, up), axis, axis_index_groups=inner)  21.4 us
    ppermute x5, starting transfers between devices, exchange(): two = lax.ppermute(jnp.where(odd, up, down), axis, outer)  17.6 us
    pallas_call x6, Pallas kernels, call(): pl.pallas_call(kernel, out_shape=[jax.ShapeDtypeStruct((rows, LANES), F32...  5.85 us
    ppermute x5, waiting for transfers between devices, exchange(): two = lax.ppermute(jnp.where(odd, up, down), axis, outer)  4.24 us
  transfers between devices with their start and end apart: 5, of which 2 were waited for; matrix products, arithmetic and copies ran while one was open for 0% of the time, Pallas kernels for 0%

profile of v6, /device:TPU:250, one launch (start us, length us, event | category | flops | bytes accessed | tf_op | source)
XLA Modules:
  0.0 51.0 jit_solution(2478729096434954199)
XLA Ops:
  0.6 1.0 %pad_maximum_fusion.fk_ref = f32[512,128]{1,0:T(8,128)S(1)} fusion(f32[256,128]{1,0:T(8,128)} %bitcast.4, f32[256,128]{1,0:T(8,128)} %bitcast.5), kind=kLoop, calls=%fused_computation | loop fusion | flops 65536 | bytes 524288 | tf_op jit(solution)/shard_map/concatenate | solution.py:440
  1.6 0.2 shard_map.41
  1.8 3.4 %collective-permute-start = (f32[128,128]{1,0:T(8,128)S(1)}, f32[128,128]{1,0:T(8,128)S(1)}, u32[]{:S(2)}, u32[]{:S(2)}) collective-permute-start(f32[128,128]{1,0:T(8,128)S(1)} %get-tuple-element.63), channel_id=1, source_target_pairs={{128,256},{256,128},{129,257},{257,129},{130,258},{258,130},{131,2... | collective-permute-start | bytes 196616 | tf_op jit(solution)/shard_map/ppermute | solution.py:431
  5.2 4.9 %all-gather = f32[256,128]{1,0:T(8,128)S(1)} all-gather(f32[128,128]{1,0:T(8,128)S(1)} %get-tuple-element.62), channel_id=2, replica_groups={{0,128},{256,384},{1,129},{257,385},{2,130},{258,386},{3,131},{259,387}..., dimensions={0}, use_global_device_ids=true | all-gather | bytes 196608 | tf_op jit(solution)/shard_map/all_gather | solution.py:432
  10.2 0.0 collective-permute-done
  10.2 0.5 shard_map.42
  10.7 5.7 %collective-permute-start.1 = (f32[168,128]{1,0:T(8,128)S(1)}, f32[168,128]{1,0:T(8,128)S(1)}, u32[]{:S(2)}, u32[]{:S(2)}) collective-permute-start(f32[168,128]{1,0:T(8,128)S(1)} %get-tuple-element.57), channel_id=1, source_target_pairs={{4,8},{12,16},{20,24},{28,32},{36,40},{44,48},{52,56},{60,64},{68,... | collective-permute-start | bytes 258056 | tf_op jit(solution)/shard_map/ppermute | solution.py:431
  16.4 6.9 %all-gather.1 = f32[336,128]{1,0:T(8,128)S(1)} all-gather(f32[168,128]{1,0:T(8,128)S(1)} %get-tuple-element.56), channel_id=3, replica_groups={{0,4},{8,12},{16,20},{24,28},{32,36},{40,44},{48,52},{56,60},{64,68},{7..., dimensions={0}, use_global_device_ids=true | all-gather | bytes 258048 | tf_op jit(solution)/shard_map/all_gather | solution.py:432
  23.3 0.0 collective-permute-done.1
  23.3 0.3 shard_map.43
  23.7 1.9 %collective-permute-start.2 = (f32[256,128]{1,0:T(8,128)S(1)}, f32[256,128]{1,0:T(8,128)S(1)}, u32[]{:S(2)}, u32[]{:S(2)}) collective-permute-start(f32[256,128]{1,0:T(8,128)S(1)} %get-tuple-element.49), channel_id=1, source_target_pairs={{1,2},{2,1},{5,6},{6,5},{9,10},{10,9},{13,14},{14,13},{17,18},{18,... | collective-permute-start | bytes 393224 | tf_op jit(solution)/shard_map/ppermute | solution.py:431
  25.6 2.0 %all-gather.2 = f32[512,128]{1,0:T(8,128)S(1)} all-gather(f32[256,128]{1,0:T(8,128)S(1)} %get-tuple-element.48), channel_id=4, replica_groups={{0,1},{2,3},{4,5},{6,7},{8,9},{10,11},{12,13},{14,15},{16,17},{18,19},{..., dimensions={0}, use_global_device_ids=true | all-gather | bytes 393216 | tf_op jit(solution)/shard_map/all_gather | solution.py:432
  27.6 2.4 %collective-permute-done.2 = f32[256,128]{1,0:T(8,128)S(1)} collective-permute-done((f32[256,128]{1,0:T(8,128)S(1)}, f32[256,128]{1,0:T(8,128)S(1)}, u32[]{:S(2)}, u32[]{:S(2)}) %collective-permute-start.2) | collective-permute-done | bytes 131104 | tf_op jit(solution)/shard_map/ppermute | solution.py:431
  30.0 2.2 %shard_map.44 = (f32[672,128]{1,0:T(8,128)S(1)}, f32[96,128]{1,0:T(8,128)S(1)}, f32[96,128]{1,0:T(8,128)S(1)}, f32[864,128]{1,0:T(8,128)S(1)}, f32[1824,128]{1,0:T(8,128)S(1)}) custom-call(f32[1344,128]{1,0:T(8,128)S(1)} %get-tuple-element.26.raw_ref, f32[1344,128]{1,0:T(8,128)S(1)} %get-tuple-element.27.refs_0_.own_ref, ...), custom_call_target="tpu_custom_call" | custom-call | tf_op jit(solution)/shard_map/pallas_call | solution.py:41
  32.2 4.6 %collective-permute-start.3 = (f32[96,128]{1,0:T(8,128)S(1)}, f32[96,128]{1,0:T(8,128)S(1)}, u32[]{:S(2)}, u32[]{:S(2)}) collective-permute-start(f32[96,128]{1,0:T(8,128)S(1)} %get-tuple-element.65), channel_id=1, source_target_pairs={{4,8},{12,16},{20,24},{28,32},{36,40},{44,48},{52,56},{60,64},{68,... | collective-permute-start | bytes 147464 | tf_op jit(solution)/shard_map/ppermute | solution.py:431
  36.8 5.7 %all-gather.3 = f32[192,128]{1,0:T(8,128)S(1)} all-gather(f32[96,128]{1,0:T(8,128)S(1)} %get-tuple-element.64), channel_id=5, replica_groups={{0,4},{8,12},{16,20},{24,28},{32,36},{40,44},{48,52},{56,60},{64,68},{7..., dimensions={0}, use_global_device_ids=true | all-gather | bytes 147456 | tf_op jit(solution)/shard_map/all_gather | solution.py:432
  42.5 0.0 collective-permute-done.3
  42.5 0.2 shard_map.45
  42.8 1.9 %collective-permute-start.4 = (f32[152,128]{1,0:T(8,128)S(1)}, f32[152,128]{1,0:T(8,128)S(1)}, u32[]{:S(2)}, u32[]{:S(2)}) collective-permute-start(f32[152,128]{1,0:T(8,128)S(1)} %get-tuple-element.59), channel_id=1, source_target_pairs={{1,2},{2,1},{5,6},{6,5},{9,10},{10,9},{13,14},{14,13},{17,18},{18,... | collective-permute-start | bytes 233480 | tf_op jit(solution)/shard_map/ppermute | solution.py:431
  44.7 1.9 %all-gather.4 = f32[304,128]{1,0:T(8,128)S(1)} all-gather(f32[152,128]{1,0:T(8,128)S(1)} %get-tuple-element.58), channel_id=6, replica_groups={{0,1},{2,3},{4,5},{6,7},{8,9},{10,11},{12,13},{14,15},{16,17},{18,19},{..., dimensions={0}, use_global_device_ids=true | all-gather | bytes 233472 | tf_op jit(solution)/shard_map/all_gather | solution.py:432
  46.6 1.9 %collective-permute-done.4 = f32[152,128]{1,0:T(8,128)S(1)} collective-permute-done((f32[152,128]{1,0:T(8,128)S(1)}, f32[152,128]{1,0:T(8,128)S(1)}, u32[]{:S(2)}, u32[]{:S(2)}) %collective-permute-start.4) | collective-permute-done | bytes 77856 | tf_op jit(solution)/shard_map/ppermute | solution.py:431
  48.5 2.5 %shard_map.46 = (f32[256,128]{1,0:T(8,128)}, f32[256,128]{1,0:T(8,128)}) custom-call(f32[512,128]{1,0:T(8,128)S(1)} %pad_maximum_fusion.fk_ref, f32[672,128]{1,0:T(8,128)S(1)} %get-tuple-element.35.refs_0_.own_ref, f32[168,128]{1,0:T(8,128)S(1)} %get-tuple-element.38.xl_ref, f32[168,128]{1,0:T(8,128)S(1)} %get-tuple-element.39.xr_ref, ...), custom_call_target="tpu_custom_call" | custom-call | tf_op jit(solution)/shard_map/pallas_call | solution.py:41
  (10 shorter events, 0.2 us)
Async XLA Ops:
  1.8 8.4 %collective-permute-start = (f32[128,128]{1,0:T(8,128)S(1)}, f32[128,128]{1,0:T(8,128)S(1)}, u32[]{:S(2)}, u32[]{:S(2)}) collective-permute-start(f32[128,128]{1,0:T(8,128)S(1)} %get-tuple-element.63), channel_id=1, source_target_pairs={{128,256},{256,128},{129,257},{257,129},{130,258},{258,130},{131,2... | collective-permute-start | bytes 196616 | tf_op jit(solution)/shard_map/ppermute | solution.py:431
  10.7 12.6 %collective-permute-start.1 = (f32[168,128]{1,0:T(8,128)S(1)}, f32[168,128]{1,0:T(8,128)S(1)}, u32[]{:S(2)}, u32[]{:S(2)}) collective-permute-start(f32[168,128]{1,0:T(8,128)S(1)} %get-tuple-element.57), channel_id=1, source_target_pairs={{4,8},{12,16},{20,24},{28,32},{36,40},{44,48},{52,56},{60,64},{68,... | collective-permute-start | bytes 258056 | tf_op jit(solution)/shard_map/ppermute | solution.py:431
  23.7 6.3 %collective-permute-start.2 = (f32[256,128]{1,0:T(8,128)S(1)}, f32[256,128]{1,0:T(8,128)S(1)}, u32[]{:S(2)}, u32[]{:S(2)}) collective-permute-start(f32[256,128]{1,0:T(8,128)S(1)} %get-tuple-element.49), channel_id=1, source_target_pairs={{1,2},{2,1},{5,6},{6,5},{9,10},{10,9},{13,14},{14,13},{17,18},{18,... | collective-permute-start | bytes 393224 | tf_op jit(solution)/shard_map/ppermute | solution.py:431
  32.2 10.3 %collective-permute-start.3 = (f32[96,128]{1,0:T(8,128)S(1)}, f32[96,128]{1,0:T(8,128)S(1)}, u32[]{:S(2)}, u32[]{:S(2)}) collective-permute-start(f32[96,128]{1,0:T(8,128)S(1)} %get-tuple-element.65), channel_id=1, source_target_pairs={{4,8},{12,16},{20,24},{28,32},{36,40},{44,48},{52,56},{60,64},{68,... | collective-permute-start | bytes 147464 | tf_op jit(solution)/shard_map/ppermute | solution.py:431
  42.8 5.7 %collective-permute-start.4 = (f32[152,128]{1,0:T(8,128)S(1)}, f32[152,128]{1,0:T(8,128)S(1)}, u32[]{:S(2)}, u32[]{:S(2)}) collective-permute-start(f32[152,128]{1,0:T(8,128)S(1)} %get-tuple-element.59), channel_id=1, source_target_pairs={{1,2},{2,1},{5,6},{6,5},{9,10},{10,9},{13,14},{14,13},{17,18},{18,... | collective-permute-start | bytes 233480 | tf_op jit(solution)/shard_map/ppermute | solution.py:431

commit v7 on v6

--- a/solution.py
+++ b/solution.py
@@ -15,16 +15,17 @@
 OWN = tuple(2 * n for n in N)
 WIDE = tuple(2 * r for r in RING)
 OBASE = (0, 512, 640)
-OROWS = 672
+CELLS = 672
+OROWS = 704
 XBASE = (0, 96, 144)
-XROWS = 168
-YROWS = (0, 152, 256)
+XROWS = 256
+YROWS = (0, 152, 264)
 PACKED = (0, 96, 168)
 LAYERS = (3, 2)
 UNROLL = 8
 GROUPS = (3, 3)
 WBASE = (0, 1056, 1504)
-WROWS = 1824
+WROWS = 2048
 SOLROWS = 18 * 48
 VMEM_LIMIT = 48 * 1024 * 1024
 
@@ -163,7 +164,7 @@
         scale = 0.125 if field == 0 else 0.125 * 0.25
         coarsen(raw_ref, 0, base, tmp, scale)
         coarsen(raw_ref, 1, base, tmp, scale)
-    for at in range(0, OROWS, 32):
+    for at in range(0, CELLS, 32):
         c = raw_ref[pl.ds(OROWS + at, 32), :]
         w = 0.8 / (14.0 * c + 1.0)
         w_ref[pl.ds(at, 32), :] = w
@@ -178,15 +179,14 @@
     for j in range(count):
         parts.append((at, 0, ((0, j),), None))
         at += X[0]
-    parts.append((at, 0, tuple((1, j) for j in range(count)), "lanes"))
-    at += X[0]
-    for j in range(count):
-        parts.append((at, 1, ((0, j), (1, j)), "turns"))
-        at += X[1]
     for j in range(0, count, 2):
         members = tuple((h, k) for k in range(j, min(j + 2, count)) for h in range(2))
         parts.append((at, 2, members, "turns"))
         at += X[2]
+    for j in range(count):
+        parts.append((at, 1, ((0, j), (1, j)), "turns"))
+        at += X[1]
+    parts.append((at, 0, tuple((1, j) for j in range(count)), "lanes"))
     return parts
 
 
@@ -216,8 +216,6 @@
 
 
 def y_faces(fields, own_ref, xl_packed, xr_packed, up_ref, down_ref, xl_ref, xr_ref, rows_ref):
-    for ref in (up_ref, down_ref):
-        ref[pl.ds(150, 2), :] = jnp.zeros((2, LANES), F32)
     for field in range(fields):
         ob, xb, yb, count = field * OROWS, field * XROWS, YROWS[field], LAYERS[field]
         unpack(xl_packed, PACKED[field], xl_ref, xb, count, HALO - count)
@@ -389,7 +387,7 @@
     loop(0, 16, resid, lambda i, new: put(r_ref, 0, i, 32, new))
     coarsen(r_ref, 0, 0, tmp, 0.125)
     coarsen(r_ref, 1, 0, tmp, 0.125)
-    for at in range(0, OROWS, 32):
+    for at in range(0, CELLS, 32):
         next_ref[pl.ds(at, 32), :] = w_ref[pl.ds(at, 32), :] * r_ref[pl.ds(at, 32), :]
     x_faces(next_ref, 0, up_ref, down_ref, 0, LAYERS[0])
 
@@ -441,7 +439,7 @@
     up, down = call(z_faces, [128, 128], [], fk)
     zl, zr = exchange(up, down, "grp")
     raw, own, w, up, down = call(
-        begin, [2 * OROWS, 2 * OROWS, OROWS, PACKED[2], PACKED[2]], [256], fk, zl, zr
+        begin, [2 * OROWS, 2 * OROWS, OROWS, PACKED[2], PACKED[2]], [264], fk, zl, zr
     )
     xl, xr = exchange(up, down, "gx")
 
@@ -449,14 +447,14 @@
         def kernel(*refs):
             y_faces(fields, *refs)
 
-        return call(kernel, [YROWS[fields]] * 2 + [fields * XROWS] * 2, [24 * 16], own, xl, xr)
+        return call(kernel, [YROWS[fields]] * 2 + [fields * XROWS] * 2, [400], own, xl, xr)
 
     up, down, xl, xr = faces(2, own, xl, xr)
     yl, yr = exchange(up, down, "gy")
     own, up, down, sol, wide_u = call(
         first_round,
         [OROWS, PACKED[1], PACKED[1], SOLROWS, WROWS],
-        [WROWS, WROWS, WROWS, 192, 480, OROWS, 256],
+        [WROWS, WROWS, WROWS, 208, 496, OROWS, 264],
         raw, own, w, xl, xr, yl, yr,
     )
     xl, xr = exchange(up, down, "gx")
@@ -465,7 +463,7 @@
     out, resid = call(
         second_round,
         [256, 256],
-        [WROWS, WROWS, WROWS, SOLROWS, 192, 480, 256, 256],
+        [WROWS, WROWS, WROWS, SOLROWS, 208, 496, 256, 256],
         fk, own, xl, xr, yl, yr, sol, wide_u,
         out_specs=[HBM, HBM], copies=3,
     )

time: 51.3 us -> 51.5 us (level)
  no operation moved by 1% of the time
where the time goes in v7:
time: 51.5 us; the launch traced here: 51.2 us
  blocking collectives  21.4 us (42%)
  starting transfers between devices  17.6 us (34%)
  Pallas kernels  6.02 us (12%)
  waiting for transfers between devices  4.28 us (8%)
  other arithmetic  1.19 us (2%)
  between operations  0.8 us (2%)
    all_gather x5, blocking collectives, exchange(): lax.all_gather(jnp.where(odd, down, up), axis, axis_index_groups=inner)  21.4 us
    ppermute x5, starting transfers between devices, exchange(): two = lax.ppermute(jnp.where(odd, up, down), axis, outer)  17.6 us
    pallas_call x6, Pallas kernels, call(): pl.pallas_call(kernel, out_shape=[jax.ShapeDtypeStruct((rows, LANES), F32...  6.02 us
    ppermute x5, waiting for transfers between devices, exchange(): two = lax.ppermute(jnp.where(odd, up, down), axis, outer)  4.28 us
  transfers between devices with their start and end apart: 5, of which 2 were waited for; matrix products, arithmetic and copies ran while one was open for 0% of the time, Pallas kernels for 0%

profile of v7, /device:TPU:250, one launch (start us, length us, event | category | flops | bytes accessed | tf_op | source)
XLA Modules:
  0.0 51.2 jit_solution(14718484481302891515)
XLA Ops:
  0.6 1.0 %pad_maximum_fusion.fk_ref = f32[512,128]{1,0:T(8,128)S(1)} fusion(f32[256,128]{1,0:T(8,128)} %bitcast.4, f32[256,128]{1,0:T(8,128)} %bitcast.5), kind=kLoop, calls=%fused_computation | loop fusion | flops 65536 | bytes 524288 | tf_op jit(solution)/shard_map/concatenate | solution.py:438
  1.6 0.2 shard_map.41
  1.8 3.4 %collective-permute-start = (f32[128,128]{1,0:T(8,128)S(1)}, f32[128,128]{1,0:T(8,128)S(1)}, u32[]{:S(2)}, u32[]{:S(2)}) collective-permute-start(f32[128,128]{1,0:T(8,128)S(1)} %get-tuple-element.63), channel_id=1, source_target_pairs={{128,256},{256,128},{129,257},{257,129},{130,258},{258,130},{131,2... | collective-permute-start | bytes 196616 | tf_op jit(solution)/shard_map/ppermute | solution.py:429
  5.2 4.9 %all-gather = f32[256,128]{1,0:T(8,128)S(1)} all-gather(f32[128,128]{1,0:T(8,128)S(1)} %get-tuple-element.62), channel_id=2, replica_groups={{0,128},{256,384},{1,129},{257,385},{2,130},{258,386},{3,131},{259,387}..., dimensions={0}, use_global_device_ids=true | all-gather | bytes 196608 | tf_op jit(solution)/shard_map/all_gather | solution.py:430
  10.2 0.0 collective-permute-done
  10.2 0.5 shard_map.42
  10.7 5.7 %collective-permute-start.1 = (f32[168,128]{1,0:T(8,128)S(1)}, f32[168,128]{1,0:T(8,128)S(1)}, u32[]{:S(2)}, u32[]{:S(2)}) collective-permute-start(f32[168,128]{1,0:T(8,128)S(1)} %get-tuple-element.57), channel_id=1, source_target_pairs={{4,8},{12,16},{20,24},{28,32},{36,40},{44,48},{52,56},{60,64},{68,... | collective-permute-start | bytes 258056 | tf_op jit(solution)/shard_map/ppermute | solution.py:429
  16.4 6.9 %all-gather.1 = f32[336,128]{1,0:T(8,128)S(1)} all-gather(f32[168,128]{1,0:T(8,128)S(1)} %get-tuple-element.56), channel_id=3, replica_groups={{0,4},{8,12},{16,20},{24,28},{32,36},{40,44},{48,52},{56,60},{64,68},{7..., dimensions={0}, use_global_device_ids=true | all-gather | bytes 258048 | tf_op jit(solution)/shard_map/all_gather | solution.py:430
  23.3 0.0 collective-permute-done.1
  23.3 0.3 shard_map.43
  23.7 1.9 %collective-permute-start.2 = (f32[264,128]{1,0:T(8,128)S(1)}, f32[264,128]{1,0:T(8,128)S(1)}, u32[]{:S(2)}, u32[]{:S(2)}) collective-permute-start(f32[264,128]{1,0:T(8,128)S(1)} %get-tuple-element.49), channel_id=1, source_target_pairs={{1,2},{2,1},{5,6},{6,5},{9,10},{10,9},{13,14},{14,13},{17,18},{18,... | collective-permute-start | bytes 405512 | tf_op jit(solution)/shard_map/ppermute | solution.py:429
  25.6 2.0 %all-gather.2 = f32[528,128]{1,0:T(8,128)S(1)} all-gather(f32[264,128]{1,0:T(8,128)S(1)} %get-tuple-element.48), channel_id=4, replica_groups={{0,1},{2,3},{4,5},{6,7},{8,9},{10,11},{12,13},{14,15},{16,17},{18,19},{..., dimensions={0}, use_global_device_ids=true | all-gather | bytes 405504 | tf_op jit(solution)/shard_map/all_gather | solution.py:430
  27.6 2.4 %collective-permute-done.2 = f32[264,128]{1,0:T(8,128)S(1)} collective-permute-done((f32[264,128]{1,0:T(8,128)S(1)}, f32[264,128]{1,0:T(8,128)S(1)}, u32[]{:S(2)}, u32[]{:S(2)}) %collective-permute-start.2) | collective-permute-done | bytes 135200 | tf_op jit(solution)/shard_map/ppermute | solution.py:429
  30.0 2.3 %shard_map.44 = (f32[704,128]{1,0:T(8,128)S(1)}, f32[96,128]{1,0:T(8,128)S(1)}, f32[96,128]{1,0:T(8,128)S(1)}, f32[864,128]{1,0:T(8,128)S(1)}, f32[2048,128]{1,0:T(8,128)S(1)}) custom-call(f32[1408,128]{1,0:T(8,128)S(1)} %get-tuple-element.26.raw_ref, f32[1408,128]{1,0:T(8,128)S(1)} %get-tuple-element.27.refs_0_.own_ref, ...), custom_call_target="tpu_custom_call" | custom-call | tf_op jit(solution)/shard_map/pallas_call | solution.py:42
  32.3 4.6 %collective-permute-start.3 = (f32[96,128]{1,0:T(8,128)S(1)}, f32[96,128]{1,0:T(8,128)S(1)}, u32[]{:S(2)}, u32[]{:S(2)}) collective-permute-start(f32[96,128]{1,0:T(8,128)S(1)} %get-tuple-element.65), channel_id=1, source_target_pairs={{4,8},{12,16},{20,24},{28,32},{36,40},{44,48},{52,56},{60,64},{68,... | collective-permute-start | bytes 147464 | tf_op jit(solution)/shard_map/ppermute | solution.py:429
  37.0 5.7 %all-gather.3 = f32[192,128]{1,0:T(8,128)S(1)} all-gather(f32[96,128]{1,0:T(8,128)S(1)} %get-tuple-element.64), channel_id=5, replica_groups={{0,4},{8,12},{16,20},{24,28},{32,36},{40,44},{48,52},{56,60},{64,68},{7..., dimensions={0}, use_global_device_ids=true | all-gather | bytes 147456 | tf_op jit(solution)/shard_map/all_gather | solution.py:430
  42.6 0.0 collective-permute-done.3
  42.6 0.2 shard_map.45
  42.9 1.9 %collective-permute-start.4 = (f32[152,128]{1,0:T(8,128)S(1)}, f32[152,128]{1,0:T(8,128)S(1)}, u32[]{:S(2)}, u32[]{:S(2)}) collective-permute-start(f32[152,128]{1,0:T(8,128)S(1)} %get-tuple-element.59), channel_id=1, source_target_pairs={{1,2},{2,1},{5,6},{6,5},{9,10},{10,9},{13,14},{14,13},{17,18},{18,... | collective-permute-start | bytes 233480 | tf_op jit(solution)/shard_map/ppermute | solution.py:429
  44.9 1.9 %all-gather.4 = f32[304,128]{1,0:T(8,128)S(1)} all-gather(f32[152,128]{1,0:T(8,128)S(1)} %get-tuple-element.58), channel_id=6, replica_groups={{0,1},{2,3},{4,5},{6,7},{8,9},{10,11},{12,13},{14,15},{16,17},{18,19},{..., dimensions={0}, use_global_device_ids=true | all-gather | bytes 233472 | tf_op jit(solution)/shard_map/all_gather | solution.py:430
  46.8 1.9 %collective-permute-done.4 = f32[152,128]{1,0:T(8,128)S(1)} collective-permute-done((f32[152,128]{1,0:T(8,128)S(1)}, f32[152,128]{1,0:T(8,128)S(1)}, u32[]{:S(2)}, u32[]{:S(2)}) %collective-permute-start.4) | collective-permute-done | bytes 77856 | tf_op jit(solution)/shard_map/ppermute | solution.py:429
  48.7 2.6 %shard_map.46 = (f32[256,128]{1,0:T(8,128)}, f32[256,128]{1,0:T(8,128)}) custom-call(f32[512,128]{1,0:T(8,128)S(1)} %pad_maximum_fusion.fk_ref, f32[704,128]{1,0:T(8,128)S(1)} %get-tuple-element.35.refs_0_.own_ref, f32[256,128]{1,0:T(8,128)S(1)} %get-tuple-element.38.xl_ref, f32[256,128]{1,0:T(8,128)S(1)} %get-tuple-element.39.xr_ref, ...), custom_call_target="tpu_custom_call" | custom-call | tf_op jit(solution)/shard_map/pallas_call | solution.py:42
  (10 shorter events, 0.2 us)
Async XLA Ops:
  1.8 8.4 %collective-permute-start = (f32[128,128]{1,0:T(8,128)S(1)}, f32[128,128]{1,0:T(8,128)S(1)}, u32[]{:S(2)}, u32[]{:S(2)}) collective-permute-start(f32[128,128]{1,0:T(8,128)S(1)} %get-tuple-element.63), channel_id=1, source_target_pairs={{128,256},{256,128},{129,257},{257,129},{130,258},{258,130},{131,2... | collective-permute-start | bytes 196616 | tf_op jit(solution)/shard_map/ppermute | solution.py:429
  10.7 12.6 %collective-permute-start.1 = (f32[168,128]{1,0:T(8,128)S(1)}, f32[168,128]{1,0:T(8,128)S(1)}, u32[]{:S(2)}, u32[]{:S(2)}) collective-permute-start(f32[168,128]{1,0:T(8,128)S(1)} %get-tuple-element.57), channel_id=1, source_target_pairs={{4,8},{12,16},{20,24},{28,32},{36,40},{44,48},{52,56},{60,64},{68,... | collective-permute-start | bytes 258056 | tf_op jit(solution)/shard_map/ppermute | solution.py:429
  23.7 6.3 %collective-permute-start.2 = (f32[264,128]{1,0:T(8,128)S(1)}, f32[264,128]{1,0:T(8,128)S(1)}, u32[]{:S(2)}, u32[]{:S(2)}) collective-permute-start(f32[264,128]{1,0:T(8,128)S(1)} %get-tuple-element.49), channel_id=1, source_target_pairs={{1,2},{2,1},{5,6},{6,5},{9,10},{10,9},{13,14},{14,13},{17,18},{18,... | collective-permute-start | bytes 405512 | tf_op jit(solution)/shard_map/ppermute | solution.py:429
  32.3 10.3 %collective-permute-start.3 = (f32[96,128]{1,0:T(8,128)S(1)}, f32[96,128]{1,0:T(8,128)S(1)}, u32[]{:S(2)}, u32[]{:S(2)}) collective-permute-start(f32[96,128]{1,0:T(8,128)S(1)} %get-tuple-element.65), channel_id=1, source_target_pairs={{4,8},{12,16},{20,24},{28,32},{36,40},{44,48},{52,56},{60,64},{68,... | collective-permute-start | bytes 147464 | tf_op jit(solution)/shard_map/ppermute | solution.py:429
  42.9 5.7 %collective-permute-start.4 = (f32[152,128]{1,0:T(8,128)S(1)}, f32[152,128]{1,0:T(8,128)S(1)}, u32[]{:S(2)}, u32[]{:S(2)}) collective-permute-start(f32[152,128]{1,0:T(8,128)S(1)} %get-tuple-element.59), channel_id=1, source_target_pairs={{1,2},{2,1},{5,6},{6,5},{9,10},{10,9},{13,14},{14,13},{17,18},{18,... | collective-permute-start | bytes 233480 | tf_op jit(solution)/shard_map/ppermute | solution.py:429

commit v8 on v7

--- a/solution.py
+++ b/solution.py
@@ -15,6 +15,8 @@
 OWN = tuple(2 * n for n in N)
 WIDE = tuple(2 * r for r in RING)
 OBASE = (0, 512, 640)
+ZWIDTH = 24
+ZROWS = 48
 CELLS = 672
 OROWS = 704
 XBASE = (0, 96, 144)
@@ -23,7 +25,7 @@
 PACKED = (0, 96, 168)
 LAYERS = (3, 2)
 UNROLL = 8
-GROUPS = (3, 3)
+GROUPS = (3, 2)
 WBASE = (0, 1056, 1504)
 WROWS = 2048
 SOLROWS = 18 * 48
@@ -51,20 +53,28 @@
 
 
 def z_faces(fk_ref, up_ref, down_ref):
-    quarter = lanes_of(16) // 32
-    for field, ref in enumerate((fk_ref.at[pl.ds(0, 256), :], fk_ref.at[pl.ds(256, 256), :])):
-        for g in range(4):
-            slabs = [ref[pl.ds(16 * (4 * g + m), 16), :] for m in range(4)]
-            up = pltpu.roll(slabs[0], 32, 1)
-            down = slabs[0]
-            for m in range(1, 4):
-                shift = 32 * (m + 1) % LANES
-                moved = pltpu.roll(slabs[m], shift, 1) if shift else slabs[m]
-                up = jnp.where(quarter == m, moved, up)
-                down = jnp.where(quarter == m, pltpu.roll(slabs[m], 32 * m, 1), down)
-            at = pl.ds(64 * field + 16 * g, 16)
-            up_ref[at, :] = up
-            down_ref[at, :] = down
+    lane = lanes_of(16)
+    for field in range(2):
+        for tile in range(3):
+            slot = (lane + LANES * tile) // ZWIDTH
+            members = range(LANES * tile // ZWIDTH, (LANES * (tile + 1) - 1) // ZWIDTH + 1)
+            for dst, begin_at in ((up_ref, LANES - ZWIDTH), (down_ref, 0)):
+                shared = None
+                for i in members:
+                    value = fk_ref[pl.ds(256 * field + 16 * i, 16), :]
+                    move = (ZWIDTH * i - begin_at) % LANES
+                    value = pltpu.roll(value, move, 1) if move else value
+                    shared = value if shared is None else jnp.where(slot == i, value, shared)
+                dst[pl.ds(ZROWS * field + 16 * tile, 16), :] = shared
+
+
+def z_slab(ref, field, i, begin_at):
+    tile, at = divmod(ZWIDTH * i, LANES)
+    value = ref[pl.ds(ZROWS * field + 16 * tile, 16), :]
+    if at + ZWIDTH > LANES:
+        value = jnp.where(lanes_of(16) >= at, value, ref[pl.ds(ZROWS * field + 16 * (tile + 1), 16), :])
+    move = (begin_at - at) % LANES
+    return pltpu.roll(value, move, 1) if move else value
 
 
 def coarsen(ref, level, base, tmp, scale):
@@ -151,16 +161,11 @@
     low = lanes_of(16) < 64
     for field, ref in enumerate((fk_ref.at[pl.ds(0, 256), :], fk_ref.at[pl.ds(256, 256), :])):
         base = field * OROWS
-        for g in range(4):
-            at = pl.ds(64 * field + 16 * g, 16)
-            left, right = zl_ref[at, :], zr_ref[at, :]
-            for m in range(4):
-                slab = 4 * g + m
-                shift_l, shift_r = (96 - 32 * m) % LANES, (-32 * m) % LANES
-                from_l = pltpu.roll(left, shift_l, 1) if shift_l else left
-                from_r = pltpu.roll(right, shift_r, 1) if shift_r else right
-                raw_ref[pl.ds(base + 32 * slab, 16), :] = ref[pl.ds(16 * slab, 16), :]
-                raw_ref[pl.ds(base + 32 * slab + 16, 16), :] = jnp.where(low, from_r, from_l)
+        for i in range(16):
+            from_l = z_slab(zl_ref, field, i, LANES - ZWIDTH)
+            from_r = z_slab(zr_ref, field, i, 0)
+            raw_ref[pl.ds(base + 32 * i, 16), :] = ref[pl.ds(16 * i, 16), :]
+            raw_ref[pl.ds(base + 32 * i + 16, 16), :] = jnp.where(low, from_r, from_l)
         scale = 0.125 if field == 0 else 0.125 * 0.25
         coarsen(raw_ref, 0, base, tmp, scale)
         coarsen(raw_ref, 1, base, tmp, scale)
@@ -296,14 +301,14 @@
     halves = []
     for h in range(2):
         t = total[h * ring : (h + 1) * ring]
-        halves.append(pltpu.roll(t, 1, 0) + pltpu.roll(t, ring - 1, 0) + (t + t))
+        halves.append((pltpu.roll(t, 1, 0) + pltpu.roll(t, ring - 1, 0)) + (t + t))
     lane = lanes_of(ring)
     a, b = halves
     ra, rb = pltpu.roll(a, step, 1), pltpu.roll(b, step, 1)
     sa, sb = pltpu.roll(a, LANES - step, 1), pltpu.roll(b, LANES - step, 1)
     low, high = lane < step, lane >= LANES - step
-    new_a = a + a + jnp.where(low, rb, ra) + jnp.where(high, sb, sa)
-    new_b = b + b + jnp.where(low, ra, rb) + jnp.where(high, sa, sb)
+    new_a = (a + a) + (jnp.where(low, rb, ra) + jnp.where(high, sb, sa))
+    new_b = (b + b) + (jnp.where(low, ra, rb) + jnp.where(high, sa, sb))
     return mid, new_a, new_b
 
 
@@ -436,7 +441,7 @@
     f = forcing.reshape(256, LANES)
     k = kappa.reshape(256, LANES)
     fk = lax.optimization_barrier(jnp.concatenate([f, k]))
-    up, down = call(z_faces, [128, 128], [], fk)
+    up, down = call(z_faces, [2 * ZROWS, 2 * ZROWS], [], fk)
     zl, zr = exchange(up, down, "grp")
     raw, own, w, up, down = call(
         begin, [2 * OROWS, 2 * OROWS, OROWS, PACKED[2], PACKED[2]], [264], fk, zl, zr

time: 51.5 us -> 51.2 us (level)
  no operation moved by 1% of the time
where the time goes in v8:
time: 51.2 us; the launch traced here: 50.9 us
  blocking collectives  21.2 us (41%)
  starting transfers between devices  17.6 us (34%)
  Pallas kernels  5.84 us (11%)
  waiting for transfers between devices  4.28 us (8%)
  other arithmetic  1.18 us (2%)
  between operations  0.8 us (2%)
    all_gather x5, blocking collectives, exchange(): lax.all_gather(jnp.where(odd, down, up), axis, axis_index_groups=inner)  21.2 us
    ppermute x5, starting transfers between devices, exchange(): two = lax.ppermute(jnp.where(odd, up, down), axis, outer)  17.6 us
    pallas_call x6, Pallas kernels, call(): pl.pallas_call(kernel, out_shape=[jax.ShapeDtypeStruct((rows, LANES), F32...  5.84 us
    ppermute x5, waiting for transfers between devices, exchange(): two = lax.ppermute(jnp.where(odd, up, down), axis, outer)  4.28 us
  transfers between devices with their start and end apart: 5, of which 2 were waited for; matrix products, arithmetic and copies ran while one was open for 0% of the time, Pallas kernels for 0%

profile of v8, /device:TPU:250, one launch (start us, length us, event | category | flops | bytes accessed | tf_op | source)
XLA Modules:
  0.0 50.9 jit_solution(7208183583454786805)
XLA Ops:
  0.6 1.0 %pad_maximum_fusion.fk_ref = f32[512,128]{1,0:T(8,128)S(1)} fusion(f32[256,128]{1,0:T(8,128)} %bitcast.4, f32[256,128]{1,0:T(8,128)} %bitcast.5), kind=kLoop, calls=%fused_computation | loop fusion | flops 65536 | bytes 524288 | tf_op jit(solution)/shard_map/concatenate | solution.py:443
  1.6 0.2 shard_map.41
  1.9 3.4 %collective-permute-start = (f32[96,128]{1,0:T(8,128)S(1)}, f32[96,128]{1,0:T(8,128)S(1)}, u32[]{:S(2)}, u32[]{:S(2)}) collective-permute-start(f32[96,128]{1,0:T(8,128)S(1)} %get-tuple-element.65), channel_id=1, source_target_pairs={{128,256},{256,128},{129,257},{257,129},{130,258},{258,130},{131,2... | collective-permute-start | bytes 147464 | tf_op jit(solution)/shard_map/ppermute | solution.py:434
  5.3 4.8 %all-gather = f32[192,128]{1,0:T(8,128)S(1)} all-gather(f32[96,128]{1,0:T(8,128)S(1)} %get-tuple-element.64), channel_id=2, replica_groups={{0,128},{256,384},{1,129},{257,385},{2,130},{258,386},{3,131},{259,387}..., dimensions={0}, use_global_device_ids=true | all-gather | bytes 147456 | tf_op jit(solution)/shard_map/all_gather | solution.py:435
  10.1 0.0 collective-permute-done
  10.1 0.5 shard_map.42
  10.6 5.7 %collective-permute-start.1 = (f32[168,128]{1,0:T(8,128)S(1)}, f32[168,128]{1,0:T(8,128)S(1)}, u32[]{:S(2)}, u32[]{:S(2)}) collective-permute-start(f32[168,128]{1,0:T(8,128)S(1)} %get-tuple-element.55), channel_id=1, source_target_pairs={{4,8},{12,16},{20,24},{28,32},{36,40},{44,48},{52,56},{60,64},{68,... | collective-permute-start | bytes 258056 | tf_op jit(solution)/shard_map/ppermute | solution.py:434
  16.3 6.9 %all-gather.1 = f32[336,128]{1,0:T(8,128)S(1)} all-gather(f32[168,128]{1,0:T(8,128)S(1)} %get-tuple-element.54), channel_id=3, replica_groups={{0,4},{8,12},{16,20},{24,28},{32,36},{40,44},{48,52},{56,60},{64,68},{7..., dimensions={0}, use_global_device_ids=true | all-gather | bytes 258048 | tf_op jit(solution)/shard_map/all_gather | solution.py:435
  23.2 0.0 collective-permute-done.1
  23.2 0.3 shard_map.43
  23.6 1.9 %collective-permute-start.2 = (f32[264,128]{1,0:T(8,128)S(1)}, f32[264,128]{1,0:T(8,128)S(1)}, u32[]{:S(2)}, u32[]{:S(2)}) collective-permute-start(f32[264,128]{1,0:T(8,128)S(1)} %get-tuple-element.49), channel_id=1, source_target_pairs={{1,2},{2,1},{5,6},{6,5},{9,10},{10,9},{13,14},{14,13},{17,18},{18,... | collective-permute-start | bytes 405512 | tf_op jit(solution)/shard_map/ppermute | solution.py:434
  25.5 2.0 %all-gather.2 = f32[528,128]{1,0:T(8,128)S(1)} all-gather(f32[264,128]{1,0:T(8,128)S(1)} %get-tuple-element.48), channel_id=4, replica_groups={{0,1},{2,3},{4,5},{6,7},{8,9},{10,11},{12,13},{14,15},{16,17},{18,19},{..., dimensions={0}, use_global_device_ids=true | all-gather | bytes 405504 | tf_op jit(solution)/shard_map/all_gather | solution.py:435
  27.5 2.4 %collective-permute-done.2 = f32[264,128]{1,0:T(8,128)S(1)} collective-permute-done((f32[264,128]{1,0:T(8,128)S(1)}, f32[264,128]{1,0:T(8,128)S(1)}, u32[]{:S(2)}, u32[]{:S(2)}) %collective-permute-start.2) | collective-permute-done | bytes 135200 | tf_op jit(solution)/shard_map/ppermute | solution.py:434
  29.9 2.1 %shard_map.44 = (f32[704,128]{1,0:T(8,128)S(1)}, f32[96,128]{1,0:T(8,128)S(1)}, f32[96,128]{1,0:T(8,128)S(1)}, f32[864,128]{1,0:T(8,128)S(1)}, f32[2048,128]{1,0:T(8,128)S(1)}) custom-call(f32[1408,128]{1,0:T(8,128)S(1)} %get-tuple-element.26.raw_ref, f32[1408,128]{1,0:T(8,128)S(1)} %get-tuple-element.27.refs_0_.own_ref, ...), custom_call_target="tpu_custom_call" | custom-call | tf_op jit(solution)/shard_map/pallas_call | solution.py:44
  32.1 4.6 %collective-permute-start.3 = (f32[96,128]{1,0:T(8,128)S(1)}, f32[96,128]{1,0:T(8,128)S(1)}, u32[]{:S(2)}, u32[]{:S(2)}) collective-permute-start(f32[96,128]{1,0:T(8,128)S(1)} %get-tuple-element.63), channel_id=1, source_target_pairs={{4,8},{12,16},{20,24},{28,32},{36,40},{44,48},{52,56},{60,64},{68,... | collective-permute-start | bytes 147464 | tf_op jit(solution)/shard_map/ppermute | solution.py:434
  36.7 5.7 %all-gather.3 = f32[192,128]{1,0:T(8,128)S(1)} all-gather(f32[96,128]{1,0:T(8,128)S(1)} %get-tuple-element.62), channel_id=5, replica_groups={{0,4},{8,12},{16,20},{24,28},{32,36},{40,44},{48,52},{56,60},{64,68},{7..., dimensions={0}, use_global_device_ids=true | all-gather | bytes 147456 | tf_op jit(solution)/shard_map/all_gather | solution.py:435
  42.4 0.0 collective-permute-done.3
  42.4 0.2 shard_map.45
  42.7 1.9 %collective-permute-start.4 = (f32[152,128]{1,0:T(8,128)S(1)}, f32[152,128]{1,0:T(8,128)S(1)}, u32[]{:S(2)}, u32[]{:S(2)}) collective-permute-start(f32[152,128]{1,0:T(8,128)S(1)} %get-tuple-element.57), channel_id=1, source_target_pairs={{1,2},{2,1},{5,6},{6,5},{9,10},{10,9},{13,14},{14,13},{17,18},{18,... | collective-permute-start | bytes 233480 | tf_op jit(solution)/shard_map/ppermute | solution.py:434
  44.6 1.9 %all-gather.4 = f32[304,128]{1,0:T(8,128)S(1)} all-gather(f32[152,128]{1,0:T(8,128)S(1)} %get-tuple-element.56), channel_id=6, replica_groups={{0,1},{2,3},{4,5},{6,7},{8,9},{10,11},{12,13},{14,15},{16,17},{18,19},{..., dimensions={0}, use_global_device_ids=true | all-gather | bytes 233472 | tf_op jit(solution)/shard_map/all_gather | solution.py:435
  46.5 1.9 %collective-permute-done.4 = f32[152,128]{1,0:T(8,128)S(1)} collective-permute-done((f32[152,128]{1,0:T(8,128)S(1)}, f32[152,128]{1,0:T(8,128)S(1)}, u32[]{:S(2)}, u32[]{:S(2)}) %collective-permute-start.4) | collective-permute-done | bytes 77856 | tf_op jit(solution)/shard_map/ppermute | solution.py:434
  48.4 2.5 %shard_map.46 = (f32[256,128]{1,0:T(8,128)}, f32[256,128]{1,0:T(8,128)}) custom-call(f32[512,128]{1,0:T(8,128)S(1)} %pad_maximum_fusion.fk_ref, f32[704,128]{1,0:T(8,128)S(1)} %get-tuple-element.35.refs_0_.own_ref, f32[256,128]{1,0:T(8,128)S(1)} %get-tuple-element.38.xl_ref, f32[256,128]{1,0:T(8,128)S(1)} %get-tuple-element.39.xr_ref, ...), custom_call_target="tpu_custom_call" | custom-call | tf_op jit(solution)/shard_map/pallas_call | solution.py:44
  (10 shorter events, 0.2 us)
Async XLA Ops:
  1.9 8.2 %collective-permute-start = (f32[96,128]{1,0:T(8,128)S(1)}, f32[96,128]{1,0:T(8,128)S(1)}, u32[]{:S(2)}, u32[]{:S(2)}) collective-permute-start(f32[96,128]{1,0:T(8,128)S(1)} %get-tuple-element.65), channel_id=1, source_target_pairs={{128,256},{256,128},{129,257},{257,129},{130,258},{258,130},{131,2... | collective-permute-start | bytes 147464 | tf_op jit(solution)/shard_map/ppermute | solution.py:434
  10.6 12.6 %collective-permute-start.1 = (f32[168,128]{1,0:T(8,128)S(1)}, f32[168,128]{1,0:T(8,128)S(1)}, u32[]{:S(2)}, u32[]{:S(2)}) collective-permute-start(f32[168,128]{1,0:T(8,128)S(1)} %get-tuple-element.55), channel_id=1, source_target_pairs={{4,8},{12,16},{20,24},{28,32},{36,40},{44,48},{52,56},{60,64},{68,... | collective-permute-start | bytes 258056 | tf_op jit(solution)/shard_map/ppermute | solution.py:434
  23.6 6.3 %collective-permute-start.2 = (f32[264,128]{1,0:T(8,128)S(1)}, f32[264,128]{1,0:T(8,128)S(1)}, u32[]{:S(2)}, u32[]{:S(2)}) collective-permute-start(f32[264,128]{1,0:T(8,128)S(1)} %get-tuple-element.49), channel_id=1, source_target_pairs={{1,2},{2,1},{5,6},{6,5},{9,10},{10,9},{13,14},{14,13},{17,18},{18,... | collective-permute-start | bytes 405512 | tf_op jit(solution)/shard_map/ppermute | solution.py:434
  32.1 10.3 %collective-permute-start.3 = (f32[96,128]{1,0:T(8,128)S(1)}, f32[96,128]{1,0:T(8,128)S(1)}, u32[]{:S(2)}, u32[]{:S(2)}) collective-permute-start(f32[96,128]{1,0:T(8,128)S(1)} %get-tuple-element.63), channel_id=1, source_target_pairs={{4,8},{12,16},{20,24},{28,32},{36,40},{44,48},{52,56},{60,64},{68,... | collective-permute-start | bytes 147464 | tf_op jit(solution)/shard_map/ppermute | solution.py:434
  42.7 5.7 %collective-permute-start.4 = (f32[152,128]{1,0:T(8,128)S(1)}, f32[152,128]{1,0:T(8,128)S(1)}, u32[]{:S(2)}, u32[]{:S(2)}) collective-permute-start(f32[152,128]{1,0:T(8,128)S(1)} %get-tuple-element.57), channel_id=1, source_target_pairs={{1,2},{2,1},{5,6},{6,5},{9,10},{10,9},{13,14},{14,13},{17,18},{18,... | collective-permute-start | bytes 233480 | tf_op jit(solution)/shard_map/ppermute | solution.py:434

commit v9 on v8

--- a/solution.py
+++ b/solution.py
@@ -21,8 +21,8 @@
 OROWS = 704
 XBASE = (0, 96, 144)
 XROWS = 256
-YROWS = (0, 152, 264)
-PACKED = (0, 96, 168)
+YROWS = (0, 144, 256)
+PACKED = (0, 88, 160)
 LAYERS = (3, 2)
 UNROLL = 8
 GROUPS = (3, 2)
@@ -89,6 +89,18 @@
         pair = tmp[pl.ds(a * rows, half, 2), :] + tmp[pl.ds(a * rows + 1, half, 2), :]
         other = jnp.where(even, pltpu.roll(pair, LANES - bit, 1), pltpu.roll(pair, bit, 1))
         ref[pl.ds(base + OBASE[level + 1] + a * half, half), :] = (pair + other) * scale
+
+
+def slots(vectors):
+    shared = vectors[0]
+    slot = (lanes_of(shared.shape[0]) + 21) // 42
+    for i in (1, 2):
+        shared = jnp.where(slot == i, pltpu.roll(vectors[i], 42 * i, 1), shared)
+    return shared
+
+
+def unslots(shared):
+    return [shared] + [pltpu.roll(shared, LANES - 42 * i, 1) for i in (1, 2)]
 
 
 def x_faces(own_ref, base, up_ref, down_ref, xbase, count):
@@ -107,11 +119,12 @@
             shared = jnp.where((lane + 16) // 32 == i, moved, shared)
         dst[pl.ds(to, 16), :] = shared
         c = [own_ref[pl.ds(at[1] + 16 * i, 16), :] for i in range(count)]
-        dst[pl.ds(to + 16, 16), :] = jnp.where(odd, c[1], c[0])
+        if count == 3:
+            dst[pl.ds(to + 16, 8), :] = jnp.where(odd[:8], c[1][:8], c[0][:8])
+            dst[pl.ds(to + 24, 8), :] = jnp.where(odd[:8], slots([v[8:] for v in c]), c[2][:8])
+        else:
+            dst[pl.ds(to + 16, 16), :] = jnp.where(odd, c[1], c[0])
         to += 32
-        if count == 3:
-            dst[pl.ds(to, 8), :] = jnp.where(odd[:8], c[2][8:], c[2][:8])
-            to += 8
         c = [own_ref[pl.ds(at[2] + 8 * i, 8), :] for i in range(count)]
         shared = c[0]
         for i in range(1, count):
@@ -140,14 +153,15 @@
         return jnp.where(mask, pltpu.roll(value, 1, 1), value), jnp.where(mask, value, pltpu.roll(value, LANES - 1, 1))
 
     first = two(src[pl.ds(at + 16, 16), :])
-    dst[pl.ds(to2, 16), :] = first[0]
-    dst[pl.ds(to2 + 16, 16), :] = first[1]
+    if count == 3:
+        for i, value in enumerate((first[0][:8], first[1][:8], first[0][8:])):
+            dst[pl.ds(to2 + 16 * i, 8), :] = value
+        for i, value in enumerate(unslots(first[1][8:])):
+            dst[pl.ds(to2 + 16 * i + 8, 8), :] = value
+    else:
+        dst[pl.ds(to2, 16), :] = first[0]
+        dst[pl.ds(to2 + 16, 16), :] = first[1]
     at += 32
-    if count == 3:
-        last = two(src[pl.ds(at, 8), :])
-        dst[pl.ds(to2 + 32, 8), :] = last[0]
-        dst[pl.ds(to2 + 40, 8), :] = last[1]
-        at += 8
     c = src[pl.ds(at, 8), :]
     moved = {d: pltpu.roll(c, d % LANES, 1) if d else c for d in range(1 - count, 4)}
     for i in range(count):
@@ -188,14 +202,20 @@
         members = tuple((h, k) for k in range(j, min(j + 2, count)) for h in range(2))
         parts.append((at, 2, members, "turns"))
         at += X[2]
-    for j in range(count):
-        parts.append((at, 1, ((0, j), (1, j)), "turns"))
+    if count == 3:
+        second = ((((0, 0), (0, 1)), "turns"), (((0, 2), (1, 0), (1, 1), (1, 2)), "slots"))
+    else:
+        second = tuple((((0, j), (1, j)), "turns") for j in range(count))
+    for members, how in second:
+        parts.append((at, 1, members, how))
         at += X[1]
     parts.append((at, 0, tuple((1, j) for j in range(count)), "lanes"))
     return parts
 
 
 def share(vectors, how):
+    if how == "slots":
+        vectors, how = [vectors[0], slots(vectors[1:])], "turns"
     shared = vectors[0]
     lane = lanes_of(shared.shape[0])
     for i in range(1, len(vectors)):
@@ -207,6 +227,9 @@
 
 
 def unshare(shared, number, how):
+    if how == "slots":
+        first, rest = unshare(shared, 2, "turns")
+        return [first] + unslots(rest)
     if how != "turns":
         return [pltpu.roll(shared, LANES - 32 * i, 1) if i else shared for i in range(number)]
     turn = lanes_of(shared.shape[0]) % number

time: 51.2 us -> 51 us (level)
  no operation moved by 1% of the time
where the time goes in v9:
time: 51 us; the launch traced here: 50.8 us
  blocking collectives  21.1 us (41%)
  starting transfers between devices  17.6 us (35%)
  Pallas kernels  5.97 us (12%)
  waiting for transfers between devices  4.2 us (8%)
  other arithmetic  1.14 us (2%)
  between operations  0.81 us (2%)
    all_gather x5, blocking collectives, exchange(): lax.all_gather(jnp.where(odd, down, up), axis, axis_index_groups=inner)  21.1 us
    ppermute x5, starting transfers between devices, exchange(): two = lax.ppermute(jnp.where(odd, up, down), axis, outer)  17.6 us
    pallas_call x6, Pallas kernels, call(): pl.pallas_call(kernel, out_shape=[jax.ShapeDtypeStruct((rows, LANES), F32...  5.97 us
    ppermute x5, waiting for transfers between devices, exchange(): two = lax.ppermute(jnp.where(odd, up, down), axis, outer)  4.2 us
  transfers between devices with their start and end apart: 5, of which 2 were waited for; matrix products, arithmetic and copies ran while one was open for 0% of the time, Pallas kernels for 0%

profile of v9, /device:TPU:250, one launch (start us, length us, event | category | flops | bytes accessed | tf_op | source)
XLA Modules:
  0.0 50.8 jit_solution(7274922483257771715)
XLA Ops:
  0.6 1.0 %pad_maximum_fusion.fk_ref = f32[512,128]{1,0:T(8,128)S(1)} fusion(f32[256,128]{1,0:T(8,128)} %bitcast.4, f32[256,128]{1,0:T(8,128)} %bitcast.5), kind=kLoop, calls=%fused_computation | loop fusion | flops 65536 | bytes 524288 | tf_op jit(solution)/shard_map/concatenate | solution.py:466
  1.6 0.2 shard_map.41
  1.9 3.4 %collective-permute-start = (f32[96,128]{1,0:T(8,128)S(1)}, f32[96,128]{1,0:T(8,128)S(1)}, u32[]{:S(2)}, u32[]{:S(2)}) collective-permute-start(f32[96,128]{1,0:T(8,128)S(1)} %get-tuple-element.63), channel_id=1, source_target_pairs={{128,256},{256,128},{129,257},{257,129},{130,258},{258,130},{131,2... | collective-permute-start | bytes 147464 | tf_op jit(solution)/shard_map/ppermute | solution.py:457
  5.3 4.8 %all-gather = f32[192,128]{1,0:T(8,128)S(1)} all-gather(f32[96,128]{1,0:T(8,128)S(1)} %get-tuple-element.62), channel_id=2, replica_groups={{0,128},{256,384},{1,129},{257,385},{2,130},{258,386},{3,131},{259,387}..., dimensions={0}, use_global_device_ids=true | all-gather | bytes 147456 | tf_op jit(solution)/shard_map/all_gather | solution.py:458
  10.1 0.0 collective-permute-done
  10.1 0.5 shard_map.42
  10.6 5.7 %collective-permute-start.1 = (f32[160,128]{1,0:T(8,128)S(1)}, f32[160,128]{1,0:T(8,128)S(1)}, u32[]{:S(2)}, u32[]{:S(2)}) collective-permute-start(f32[160,128]{1,0:T(8,128)S(1)} %get-tuple-element.55), channel_id=1, source_target_pairs={{4,8},{12,16},{20,24},{28,32},{36,40},{44,48},{52,56},{60,64},{68,... | collective-permute-start | bytes 245768 | tf_op jit(solution)/shard_map/ppermute | solution.py:457
  16.3 6.8 %all-gather.1 = f32[320,128]{1,0:T(8,128)S(1)} all-gather(f32[160,128]{1,0:T(8,128)S(1)} %get-tuple-element.54), channel_id=3, replica_groups={{0,4},{8,12},{16,20},{24,28},{32,36},{40,44},{48,52},{56,60},{64,68},{7..., dimensions={0}, use_global_device_ids=true | all-gather | bytes 245760 | tf_op jit(solution)/shard_map/all_gather | solution.py:458
  23.1 0.0 collective-permute-done.1
  23.1 0.4 shard_map.43
  23.5 1.9 %collective-permute-start.2 = (f32[256,128]{1,0:T(8,128)S(1)}, f32[256,128]{1,0:T(8,128)S(1)}, u32[]{:S(2)}, u32[]{:S(2)}) collective-permute-start(f32[256,128]{1,0:T(8,128)S(1)} %get-tuple-element.49), channel_id=1, source_target_pairs={{1,2},{2,1},{5,6},{6,5},{9,10},{10,9},{13,14},{14,13},{17,18},{18,... | collective-permute-start | bytes 393224 | tf_op jit(solution)/shard_map/ppermute | solution.py:457
  25.5 2.0 %all-gather.2 = f32[512,128]{1,0:T(8,128)S(1)} all-gather(f32[256,128]{1,0:T(8,128)S(1)} %get-tuple-element.48), channel_id=4, replica_groups={{0,1},{2,3},{4,5},{6,7},{8,9},{10,11},{12,13},{14,15},{16,17},{18,19},{..., dimensions={0}, use_global_device_ids=true | all-gather | bytes 393216 | tf_op jit(solution)/shard_map/all_gather | solution.py:458
  27.5 2.4 %collective-permute-done.2 = f32[256,128]{1,0:T(8,128)S(1)} collective-permute-done((f32[256,128]{1,0:T(8,128)S(1)}, f32[256,128]{1,0:T(8,128)S(1)}, u32[]{:S(2)}, u32[]{:S(2)}) %collective-permute-start.2) | collective-permute-done | bytes 131104 | tf_op jit(solution)/shard_map/ppermute | solution.py:457
  29.9 2.1 %shard_map.44 = (f32[704,128]{1,0:T(8,128)S(1)}, f32[88,128]{1,0:T(8,128)S(1)}, f32[88,128]{1,0:T(8,128)S(1)}, f32[864,128]{1,0:T(8,128)S(1)}, f32[2048,128]{1,0:T(8,128)S(1)}) custom-call(f32[1408,128]{1,0:T(8,128)S(1)} %get-tuple-element.26.raw_ref, f32[1408,128]{1,0:T(8,128)S(1)} %get-tuple-element.27.refs_0_.own_ref, ...), custom_call_target="tpu_custom_call" | custom-call | tf_op jit(solution)/shard_map/pallas_call | solution.py:44
  32.0 4.6 %collective-permute-start.3 = (f32[88,128]{1,0:T(8,128)S(1)}, f32[88,128]{1,0:T(8,128)S(1)}, u32[]{:S(2)}, u32[]{:S(2)}) collective-permute-start(f32[88,128]{1,0:T(8,128)S(1)} %get-tuple-element.65), channel_id=1, source_target_pairs={{4,8},{12,16},{20,24},{28,32},{36,40},{44,48},{52,56},{60,64},{68,... | collective-permute-start | bytes 135176 | tf_op jit(solution)/shard_map/ppermute | solution.py:457
  36.6 5.6 %all-gather.3 = f32[176,128]{1,0:T(8,128)S(1)} all-gather(f32[88,128]{1,0:T(8,128)S(1)} %get-tuple-element.64), channel_id=5, replica_groups={{0,4},{8,12},{16,20},{24,28},{32,36},{40,44},{48,52},{56,60},{64,68},{7..., dimensions={0}, use_global_device_ids=true | all-gather | bytes 135168 | tf_op jit(solution)/shard_map/all_gather | solution.py:458
  42.3 0.0 collective-permute-done.3
  42.3 0.3 shard_map.45
  42.6 1.9 %collective-permute-start.4 = (f32[144,128]{1,0:T(8,128)S(1)}, f32[144,128]{1,0:T(8,128)S(1)}, u32[]{:S(2)}, u32[]{:S(2)}) collective-permute-start(f32[144,128]{1,0:T(8,128)S(1)} %get-tuple-element.57), channel_id=1, source_target_pairs={{1,2},{2,1},{5,6},{6,5},{9,10},{10,9},{13,14},{14,13},{17,18},{18,... | collective-permute-start | bytes 221192 | tf_op jit(solution)/shard_map/ppermute | solution.py:457
  44.5 1.9 %all-gather.4 = f32[288,128]{1,0:T(8,128)S(1)} all-gather(f32[144,128]{1,0:T(8,128)S(1)} %get-tuple-element.56), channel_id=6, replica_groups={{0,1},{2,3},{4,5},{6,7},{8,9},{10,11},{12,13},{14,15},{16,17},{18,19},{..., dimensions={0}, use_global_device_ids=true | all-gather | bytes 221184 | tf_op jit(solution)/shard_map/all_gather | solution.py:458
  46.4 1.8 %collective-permute-done.4 = f32[144,128]{1,0:T(8,128)S(1)} collective-permute-done((f32[144,128]{1,0:T(8,128)S(1)}, f32[144,128]{1,0:T(8,128)S(1)}, u32[]{:S(2)}, u32[]{:S(2)}) %collective-permute-start.4) | collective-permute-done | bytes 73760 | tf_op jit(solution)/shard_map/ppermute | solution.py:457
  48.3 2.5 %shard_map.46 = (f32[256,128]{1,0:T(8,128)}, f32[256,128]{1,0:T(8,128)}) custom-call(f32[512,128]{1,0:T(8,128)S(1)} %pad_maximum_fusion.fk_ref, f32[704,128]{1,0:T(8,128)S(1)} %get-tuple-element.35.refs_0_.own_ref, f32[256,128]{1,0:T(8,128)S(1)} %get-tuple-element.38.xl_ref, f32[256,128]{1,0:T(8,128)S(1)} %get-tuple-element.39.xr_ref, ...), custom_call_target="tpu_custom_call" | custom-call | tf_op jit(solution)/shard_map/pallas_call | solution.py:44
  (10 shorter events, 0.2 us)
Async XLA Ops:
  1.9 8.2 %collective-permute-start = (f32[96,128]{1,0:T(8,128)S(1)}, f32[96,128]{1,0:T(8,128)S(1)}, u32[]{:S(2)}, u32[]{:S(2)}) collective-permute-start(f32[96,128]{1,0:T(8,128)S(1)} %get-tuple-element.63), channel_id=1, source_target_pairs={{128,256},{256,128},{129,257},{257,129},{130,258},{258,130},{131,2... | collective-permute-start | bytes 147464 | tf_op jit(solution)/shard_map/ppermute | solution.py:457
  10.6 12.5 %collective-permute-start.1 = (f32[160,128]{1,0:T(8,128)S(1)}, f32[160,128]{1,0:T(8,128)S(1)}, u32[]{:S(2)}, u32[]{:S(2)}) collective-permute-start(f32[160,128]{1,0:T(8,128)S(1)} %get-tuple-element.55), channel_id=1, source_target_pairs={{4,8},{12,16},{20,24},{28,32},{36,40},{44,48},{52,56},{60,64},{68,... | collective-permute-start | bytes 245768 | tf_op jit(solution)/shard_map/ppermute | solution.py:457
  23.5 6.3 %collective-permute-start.2 = (f32[256,128]{1,0:T(8,128)S(1)}, f32[256,128]{1,0:T(8,128)S(1)}, u32[]{:S(2)}, u32[]{:S(2)}) collective-permute-start(f32[256,128]{1,0:T(8,128)S(1)} %get-tuple-element.49), channel_id=1, source_target_pairs={{1,2},{2,1},{5,6},{6,5},{9,10},{10,9},{13,14},{14,13},{17,18},{18,... | collective-permute-start | bytes 393224 | tf_op jit(solution)/shard_map/ppermute | solution.py:457
  32.0 10.2 %collective-permute-start.3 = (f32[88,128]{1,0:T(8,128)S(1)}, f32[88,128]{1,0:T(8,128)S(1)}, u32[]{:S(2)}, u32[]{:S(2)}) collective-permute-start(f32[88,128]{1,0:T(8,128)S(1)} %get-tuple-element.65), channel_id=1, source_target_pairs={{4,8},{12,16},{20,24},{28,32},{36,40},{44,48},{52,56},{60,64},{68,... | collective-permute-start | bytes 135176 | tf_op jit(solution)/shard_map/ppermute | solution.py:457
  42.6 5.7 %collective-permute-start.4 = (f32[144,128]{1,0:T(8,128)S(1)}, f32[144,128]{1,0:T(8,128)S(1)}, u32[]{:S(2)}, u32[]{:S(2)}) collective-permute-start(f32[144,128]{1,0:T(8,128)S(1)} %get-tuple-element.57), channel_id=1, source_target_pairs={{1,2},{2,1},{5,6},{6,5},{9,10},{10,9},{13,14},{14,13},{17,18},{18,... | collective-permute-start | bytes 221192 | tf_op jit(solution)/shard_map/ppermute | solution.py:457

commit v10 on v9

--- a/solution.py
+++ b/solution.py
@@ -272,7 +272,7 @@
     ob, xb, yb, count = field * OROWS, field * XROWS, YROWS[field], LAYERS[field]
     for level in range(3):
         n, ring, rows = N[level], RING[level], OWN[level]
-        for i in range(X[level]):
+        for i in range(HALO - count, X[level] - HALO + count):
             if i < HALO:
                 ref, at = xl_ref, xb + XBASE[level] + i * rows
             elif i < HALO + n:

time: 51 us -> 51 us (level)
  no operation moved by 1% of the time
where the time goes in v10:
time: 51 us; the launch traced here: 50.8 us
  blocking collectives  21.1 us (41%)
  starting transfers between devices  17.6 us (35%)
  Pallas kernels  5.97 us (12%)
  waiting for transfers between devices  4.2 us (8%)
  other arithmetic  1.14 us (2%)
  between operations  0.81 us (2%)
    all_gather x5, blocking collectives, exchange(): lax.all_gather(jnp.where(odd, down, up), axis, axis_index_groups=inner)  21.1 us
    ppermute x5, starting transfers between devices, exchange(): two = lax.ppermute(jnp.where(odd, up, down), axis, outer)  17.6 us
    pallas_call x6, Pallas kernels, call(): pl.pallas_call(kernel, out_shape=[jax.ShapeDtypeStruct((rows, LANES), F32...  5.97 us
    ppermute x5, waiting for transfers between devices, exchange(): two = lax.ppermute(jnp.where(odd, up, down), axis, outer)  4.2 us
  transfers between devices with their start and end apart: 5, of which 2 were waited for; matrix products, arithmetic and copies ran while one was open for 0% of the time, Pallas kernels for 0%

profile of v10, /device:TPU:250, one launch (start us, length us, event | category | flops | bytes accessed | tf_op | source)
XLA Modules:
  0.0 50.8 jit_solution(3654122070967827998)
XLA Ops:
  0.6 1.0 %pad_maximum_fusion.fk_ref = f32[512,128]{1,0:T(8,128)S(1)} fusion(f32[256,128]{1,0:T(8,128)} %bitcast.4, f32[256,128]{1,0:T(8,128)} %bitcast.5), kind=kLoop, calls=%fused_computation | loop fusion | flops 65536 | bytes 524288 | tf_op jit(solution)/shard_map/concatenate | solution.py:466
  1.6 0.2 shard_map.41
  1.9 3.4 %collective-permute-start = (f32[96,128]{1,0:T(8,128)S(1)}, f32[96,128]{1,0:T(8,128)S(1)}, u32[]{:S(2)}, u32[]{:S(2)}) collective-permute-start(f32[96,128]{1,0:T(8,128)S(1)} %get-tuple-element.63), channel_id=1, source_target_pairs={{128,256},{256,128},{129,257},{257,129},{130,258},{258,130},{131,2... | collective-permute-start | bytes 147464 | tf_op jit(solution)/shard_map/ppermute | solution.py:457
  5.3 4.8 %all-gather = f32[192,128]{1,0:T(8,128)S(1)} all-gather(f32[96,128]{1,0:T(8,128)S(1)} %get-tuple-element.62), channel_id=2, replica_groups={{0,128},{256,384},{1,129},{257,385},{2,130},{258,386},{3,131},{259,387}..., dimensions={0}, use_global_device_ids=true | all-gather | bytes 147456 | tf_op jit(solution)/shard_map/all_gather | solution.py:458
  10.1 0.0 collective-permute-done
  10.1 0.5 shard_map.42
  10.6 5.7 %collective-permute-start.1 = (f32[160,128]{1,0:T(8,128)S(1)}, f32[160,128]{1,0:T(8,128)S(1)}, u32[]{:S(2)}, u32[]{:S(2)}) collective-permute-start(f32[160,128]{1,0:T(8,128)S(1)} %get-tuple-element.55), channel_id=1, source_target_pairs={{4,8},{12,16},{20,24},{28,32},{36,40},{44,48},{52,56},{60,64},{68,... | collective-permute-start | bytes 245768 | tf_op jit(solution)/shard_map/ppermute | solution.py:457
  16.3 6.8 %all-gather.1 = f32[320,128]{1,0:T(8,128)S(1)} all-gather(f32[160,128]{1,0:T(8,128)S(1)} %get-tuple-element.54), channel_id=3, replica_groups={{0,4},{8,12},{16,20},{24,28},{32,36},{40,44},{48,52},{56,60},{64,68},{7..., dimensions={0}, use_global_device_ids=true | all-gather | bytes 245760 | tf_op jit(solution)/shard_map/all_gather | solution.py:458
  23.1 0.0 collective-permute-done.1
  23.1 0.4 shard_map.43
  23.5 1.9 %collective-permute-start.2 = (f32[256,128]{1,0:T(8,128)S(1)}, f32[256,128]{1,0:T(8,128)S(1)}, u32[]{:S(2)}, u32[]{:S(2)}) collective-permute-start(f32[256,128]{1,0:T(8,128)S(1)} %get-tuple-element.49), channel_id=1, source_target_pairs={{1,2},{2,1},{5,6},{6,5},{9,10},{10,9},{13,14},{14,13},{17,18},{18,... | collective-permute-start | bytes 393224 | tf_op jit(solution)/shard_map/ppermute | solution.py:457
  25.5 2.0 %all-gather.2 = f32[512,128]{1,0:T(8,128)S(1)} all-gather(f32[256,128]{1,0:T(8,128)S(1)} %get-tuple-element.48), channel_id=4, replica_groups={{0,1},{2,3},{4,5},{6,7},{8,9},{10,11},{12,13},{14,15},{16,17},{18,19},{..., dimensions={0}, use_global_device_ids=true | all-gather | bytes 393216 | tf_op jit(solution)/shard_map/all_gather | solution.py:458
  27.5 2.4 %collective-permute-done.2 = f32[256,128]{1,0:T(8,128)S(1)} collective-permute-done((f32[256,128]{1,0:T(8,128)S(1)}, f32[256,128]{1,0:T(8,128)S(1)}, u32[]{:S(2)}, u32[]{:S(2)}) %collective-permute-start.2) | collective-permute-done | bytes 131104 | tf_op jit(solution)/shard_map/ppermute | solution.py:457
  29.9 2.1 %shard_map.44 = (f32[704,128]{1,0:T(8,128)S(1)}, f32[88,128]{1,0:T(8,128)S(1)}, f32[88,128]{1,0:T(8,128)S(1)}, f32[864,128]{1,0:T(8,128)S(1)}, f32[2048,128]{1,0:T(8,128)S(1)}) custom-call(f32[1408,128]{1,0:T(8,128)S(1)} %get-tuple-element.26.raw_ref, f32[1408,128]{1,0:T(8,128)S(1)} %get-tuple-element.27.refs_0_.own_ref, ...), custom_call_target="tpu_custom_call" | custom-call | tf_op jit(solution)/shard_map/pallas_call | solution.py:44
  32.0 4.6 %collective-permute-start.3 = (f32[88,128]{1,0:T(8,128)S(1)}, f32[88,128]{1,0:T(8,128)S(1)}, u32[]{:S(2)}, u32[]{:S(2)}) collective-permute-start(f32[88,128]{1,0:T(8,128)S(1)} %get-tuple-element.65), channel_id=1, source_target_pairs={{4,8},{12,16},{20,24},{28,32},{36,40},{44,48},{52,56},{60,64},{68,... | collective-permute-start | bytes 135176 | tf_op jit(solution)/shard_map/ppermute | solution.py:457
  36.6 5.6 %all-gather.3 = f32[176,128]{1,0:T(8,128)S(1)} all-gather(f32[88,128]{1,0:T(8,128)S(1)} %get-tuple-element.64), channel_id=5, replica_groups={{0,4},{8,12},{16,20},{24,28},{32,36},{40,44},{48,52},{56,60},{64,68},{7..., dimensions={0}, use_global_device_ids=true | all-gather | bytes 135168 | tf_op jit(solution)/shard_map/all_gather | solution.py:458
  42.3 0.0 collective-permute-done.3
  42.3 0.3 shard_map.45
  42.6 1.9 %collective-permute-start.4 = (f32[144,128]{1,0:T(8,128)S(1)}, f32[144,128]{1,0:T(8,128)S(1)}, u32[]{:S(2)}, u32[]{:S(2)}) collective-permute-start(f32[144,128]{1,0:T(8,128)S(1)} %get-tuple-element.57), channel_id=1, source_target_pairs={{1,2},{2,1},{5,6},{6,5},{9,10},{10,9},{13,14},{14,13},{17,18},{18,... | collective-permute-start | bytes 221192 | tf_op jit(solution)/shard_map/ppermute | solution.py:457
  44.5 1.9 %all-gather.4 = f32[288,128]{1,0:T(8,128)S(1)} all-gather(f32[144,128]{1,0:T(8,128)S(1)} %get-tuple-element.56), channel_id=6, replica_groups={{0,1},{2,3},{4,5},{6,7},{8,9},{10,11},{12,13},{14,15},{16,17},{18,19},{..., dimensions={0}, use_global_device_ids=true | all-gather | bytes 221184 | tf_op jit(solution)/shard_map/all_gather | solution.py:458
  46.4 1.8 %collective-permute-done.4 = f32[144,128]{1,0:T(8,128)S(1)} collective-permute-done((f32[144,128]{1,0:T(8,128)S(1)}, f32[144,128]{1,0:T(8,128)S(1)}, u32[]{:S(2)}, u32[]{:S(2)}) %collective-permute-start.4) | collective-permute-done | bytes 73760 | tf_op jit(solution)/shard_map/ppermute | solution.py:457
  48.3 2.5 %shard_map.46 = (f32[256,128]{1,0:T(8,128)}, f32[256,128]{1,0:T(8,128)}) custom-call(f32[512,128]{1,0:T(8,128)S(1)} %pad_maximum_fusion.fk_ref, f32[704,128]{1,0:T(8,128)S(1)} %get-tuple-element.35.refs_0_.own_ref, f32[256,128]{1,0:T(8,128)S(1)} %get-tuple-element.38.xl_ref, f32[256,128]{1,0:T(8,128)S(1)} %get-tuple-element.39.xr_ref, ...), custom_call_target="tpu_custom_call" | custom-call | tf_op jit(solution)/shard_map/pallas_call | solution.py:44
  (10 shorter events, 0.2 us)
Async XLA Ops:
  1.9 8.2 %collective-permute-start = (f32[96,128]{1,0:T(8,128)S(1)}, f32[96,128]{1,0:T(8,128)S(1)}, u32[]{:S(2)}, u32[]{:S(2)}) collective-permute-start(f32[96,128]{1,0:T(8,128)S(1)} %get-tuple-element.63), channel_id=1, source_target_pairs={{128,256},{256,128},{129,257},{257,129},{130,258},{258,130},{131,2... | collective-permute-start | bytes 147464 | tf_op jit(solution)/shard_map/ppermute | solution.py:457
  10.6 12.5 %collective-permute-start.1 = (f32[160,128]{1,0:T(8,128)S(1)}, f32[160,128]{1,0:T(8,128)S(1)}, u32[]{:S(2)}, u32[]{:S(2)}) collective-permute-start(f32[160,128]{1,0:T(8,128)S(1)} %get-tuple-element.55), channel_id=1, source_target_pairs={{4,8},{12,16},{20,24},{28,32},{36,40},{44,48},{52,56},{60,64},{68,... | collective-permute-start | bytes 245768 | tf_op jit(solution)/shard_map/ppermute | solution.py:457
  23.5 6.3 %collective-permute-start.2 = (f32[256,128]{1,0:T(8,128)S(1)}, f32[256,128]{1,0:T(8,128)S(1)}, u32[]{:S(2)}, u32[]{:S(2)}) collective-permute-start(f32[256,128]{1,0:T(8,128)S(1)} %get-tuple-element.49), channel_id=1, source_target_pairs={{1,2},{2,1},{5,6},{6,5},{9,10},{10,9},{13,14},{14,13},{17,18},{18,... | collective-permute-start | bytes 393224 | tf_op jit(solution)/shard_map/ppermute | solution.py:457
  32.0 10.2 %collective-permute-start.3 = (f32[88,128]{1,0:T(8,128)S(1)}, f32[88,128]{1,0:T(8,128)S(1)}, u32[]{:S(2)}, u32[]{:S(2)}) collective-permute-start(f32[88,128]{1,0:T(8,128)S(1)} %get-tuple-element.65), channel_id=1, source_target_pairs={{4,8},{12,16},{20,24},{28,32},{36,40},{44,48},{52,56},{60,64},{68,... | collective-permute-start | bytes 135176 | tf_op jit(solution)/shard_map/ppermute | solution.py:457
  42.6 5.7 %collective-permute-start.4 = (f32[144,128]{1,0:T(8,128)S(1)}, f32[144,128]{1,0:T(8,128)S(1)}, u32[]{:S(2)}, u32[]{:S(2)}) collective-permute-start(f32[144,128]{1,0:T(8,128)S(1)} %get-tuple-element.57), channel_id=1, source_target_pairs={{1,2},{2,1},{5,6},{6,5},{9,10},{10,9},{13,14},{14,13},{17,18},{18,... | collective-permute-start | bytes 221192 | tf_op jit(solution)/shard_map/ppermute | solution.py:457

commit v11 on v9

--- a/solution.py
+++ b/solution.py
@@ -244,17 +244,18 @@
 
 
 def y_faces(fields, own_ref, xl_packed, xr_packed, up_ref, down_ref, xl_ref, xr_ref, rows_ref):
+    spare = 0
     for field in range(fields):
         ob, xb, yb, count = field * OROWS, field * XROWS, YROWS[field], LAYERS[field]
         unpack(xl_packed, PACKED[field], xl_ref, xb, count, HALO - count)
         unpack(xr_packed, PACKED[field], xr_ref, xb, count, 0)
-        for side, (dst, first) in enumerate(((up_ref, False), (down_ref, True))):
+        for dst, first in ((up_ref, False), (down_ref, True)):
             for at, level, members, how in y_parts(count):
                 n, rows, size = N[level], OWN[level], X[level]
                 vectors = []
-                for m, (h, j) in enumerate(members):
+                for h, j in members:
                     row = h * n + (j if first else n - count + j)
-                    to = 24 * (m + 4 * (side + 2 * field))
+                    to, spare = spare, spare + 24
                     if len(members) == 1:
                         ref, to = dst, yb + at
                     else:
@@ -475,7 +476,7 @@
         def kernel(*refs):
             y_faces(fields, *refs)
 
-        return call(kernel, [YROWS[fields]] * 2 + [fields * XROWS] * 2, [400], own, xl, xr)
+        return call(kernel, [YROWS[fields]] * 2 + [fields * XROWS] * 2, [72 * 24], own, xl, xr)
 
     up, down, xl, xr = faces(2, own, xl, xr)
     yl, yr = exchange(up, down, "gy")

time: 51 us -> 50.9 us (level)
  no operation moved by 1% of the time
where the time goes in v11:
time: 50.9 us; the launch traced here: 50.7 us
  blocking collectives  21.1 us (41%)
  starting transfers between devices  17.6 us (35%)
  Pallas kernels  5.87 us (12%)
  waiting for transfers between devices  4.2 us (8%)
  other arithmetic  1.14 us (2%)
  between operations  0.8 us (2%)
    all_gather x5, blocking collectives, exchange(): lax.all_gather(jnp.where(odd, down, up), axis, axis_index_groups=inner)  21.1 us
    ppermute x5, starting transfers between devices, exchange(): two = lax.ppermute(jnp.where(odd, up, down), axis, outer)  17.6 us
    pallas_call x6, Pallas kernels, call(): pl.pallas_call(kernel, out_shape=[jax.ShapeDtypeStruct((rows, LANES), F32...  5.87 us
    ppermute x5, waiting for transfers between devices, exchange(): two = lax.ppermute(jnp.where(odd, up, down), axis, outer)  4.2 us
  transfers between devices with their start and end apart: 5, of which 2 were waited for; matrix products, arithmetic and copies ran while one was open for 0% of the time, Pallas kernels for 0%

profile of v11, /device:TPU:250, one launch (start us, length us, event | category | flops | bytes accessed | tf_op | source)
XLA Modules:
  0.0 50.7 jit_solution(12878772910048591094)
XLA Ops:
  0.6 1.0 %pad_maximum_fusion.fk_ref = f32[512,128]{1,0:T(8,128)S(1)} fusion(f32[256,128]{1,0:T(8,128)} %bitcast.4, f32[256,128]{1,0:T(8,128)} %bitcast.5), kind=kLoop, calls=%fused_computation | loop fusion | flops 65536 | bytes 524288 | tf_op jit(solution)/shard_map/concatenate | solution.py:467
  1.6 0.2 shard_map.41
  1.9 3.4 %collective-permute-start = (f32[96,128]{1,0:T(8,128)S(1)}, f32[96,128]{1,0:T(8,128)S(1)}, u32[]{:S(2)}, u32[]{:S(2)}) collective-permute-start(f32[96,128]{1,0:T(8,128)S(1)} %get-tuple-element.63), channel_id=1, source_target_pairs={{128,256},{256,128},{129,257},{257,129},{130,258},{258,130},{131,2... | collective-permute-start | bytes 147464 | tf_op jit(solution)/shard_map/ppermute | solution.py:458
  5.3 4.8 %all-gather = f32[192,128]{1,0:T(8,128)S(1)} all-gather(f32[96,128]{1,0:T(8,128)S(1)} %get-tuple-element.62), channel_id=2, replica_groups={{0,128},{256,384},{1,129},{257,385},{2,130},{258,386},{3,131},{259,387}..., dimensions={0}, use_global_device_ids=true | all-gather | bytes 147456 | tf_op jit(solution)/shard_map/all_gather | solution.py:459
  10.1 0.0 collective-permute-done
  10.1 0.5 shard_map.42
  10.6 5.7 %collective-permute-start.1 = (f32[160,128]{1,0:T(8,128)S(1)}, f32[160,128]{1,0:T(8,128)S(1)}, u32[]{:S(2)}, u32[]{:S(2)}) collective-permute-start(f32[160,128]{1,0:T(8,128)S(1)} %get-tuple-element.55), channel_id=1, source_target_pairs={{4,8},{12,16},{20,24},{28,32},{36,40},{44,48},{52,56},{60,64},{68,... | collective-permute-start | bytes 245768 | tf_op jit(solution)/shard_map/ppermute | solution.py:458
  16.3 6.8 %all-gather.1 = f32[320,128]{1,0:T(8,128)S(1)} all-gather(f32[160,128]{1,0:T(8,128)S(1)} %get-tuple-element.54), channel_id=3, replica_groups={{0,4},{8,12},{16,20},{24,28},{32,36},{40,44},{48,52},{56,60},{64,68},{7..., dimensions={0}, use_global_device_ids=true | all-gather | bytes 245760 | tf_op jit(solution)/shard_map/all_gather | solution.py:459
  23.1 0.0 collective-permute-done.1
  23.1 0.3 shard_map.43
  23.5 1.9 %collective-permute-start.2 = (f32[256,128]{1,0:T(8,128)S(1)}, f32[256,128]{1,0:T(8,128)S(1)}, u32[]{:S(2)}, u32[]{:S(2)}) collective-permute-start(f32[256,128]{1,0:T(8,128)S(1)} %get-tuple-element.49), channel_id=1, source_target_pairs={{1,2},{2,1},{5,6},{6,5},{9,10},{10,9},{13,14},{14,13},{17,18},{18,... | collective-permute-start | bytes 393224 | tf_op jit(solution)/shard_map/ppermute | solution.py:458
  25.4 2.0 %all-gather.2 = f32[512,128]{1,0:T(8,128)S(1)} all-gather(f32[256,128]{1,0:T(8,128)S(1)} %get-tuple-element.48), channel_id=4, replica_groups={{0,1},{2,3},{4,5},{6,7},{8,9},{10,11},{12,13},{14,15},{16,17},{18,19},{..., dimensions={0}, use_global_device_ids=true | all-gather | bytes 393216 | tf_op jit(solution)/shard_map/all_gather | solution.py:459
  27.4 2.4 %collective-permute-done.2 = f32[256,128]{1,0:T(8,128)S(1)} collective-permute-done((f32[256,128]{1,0:T(8,128)S(1)}, f32[256,128]{1,0:T(8,128)S(1)}, u32[]{:S(2)}, u32[]{:S(2)}) %collective-permute-start.2) | collective-permute-done | bytes 131104 | tf_op jit(solution)/shard_map/ppermute | solution.py:458
  29.8 2.1 %shard_map.44 = (f32[704,128]{1,0:T(8,128)S(1)}, f32[88,128]{1,0:T(8,128)S(1)}, f32[88,128]{1,0:T(8,128)S(1)}, f32[864,128]{1,0:T(8,128)S(1)}, f32[2048,128]{1,0:T(8,128)S(1)}) custom-call(f32[1408,128]{1,0:T(8,128)S(1)} %get-tuple-element.26.raw_ref, f32[1408,128]{1,0:T(8,128)S(1)} %get-tuple-element.27.refs_0_.own_ref, ...), custom_call_target="tpu_custom_call" | custom-call | tf_op jit(solution)/shard_map/pallas_call | solution.py:44
  31.9 4.6 %collective-permute-start.3 = (f32[88,128]{1,0:T(8,128)S(1)}, f32[88,128]{1,0:T(8,128)S(1)}, u32[]{:S(2)}, u32[]{:S(2)}) collective-permute-start(f32[88,128]{1,0:T(8,128)S(1)} %get-tuple-element.65), channel_id=1, source_target_pairs={{4,8},{12,16},{20,24},{28,32},{36,40},{44,48},{52,56},{60,64},{68,... | collective-permute-start | bytes 135176 | tf_op jit(solution)/shard_map/ppermute | solution.py:458
  36.5 5.6 %all-gather.3 = f32[176,128]{1,0:T(8,128)S(1)} all-gather(f32[88,128]{1,0:T(8,128)S(1)} %get-tuple-element.64), channel_id=5, replica_groups={{0,4},{8,12},{16,20},{24,28},{32,36},{40,44},{48,52},{56,60},{64,68},{7..., dimensions={0}, use_global_device_ids=true | all-gather | bytes 135168 | tf_op jit(solution)/shard_map/all_gather | solution.py:459
  42.2 0.0 collective-permute-done.3
  42.2 0.3 shard_map.45
  42.5 1.9 %collective-permute-start.4 = (f32[144,128]{1,0:T(8,128)S(1)}, f32[144,128]{1,0:T(8,128)S(1)}, u32[]{:S(2)}, u32[]{:S(2)}) collective-permute-start(f32[144,128]{1,0:T(8,128)S(1)} %get-tuple-element.57), channel_id=1, source_target_pairs={{1,2},{2,1},{5,6},{6,5},{9,10},{10,9},{13,14},{14,13},{17,18},{18,... | collective-permute-start | bytes 221192 | tf_op jit(solution)/shard_map/ppermute | solution.py:458
  44.4 1.9 %all-gather.4 = f32[288,128]{1,0:T(8,128)S(1)} all-gather(f32[144,128]{1,0:T(8,128)S(1)} %get-tuple-element.56), channel_id=6, replica_groups={{0,1},{2,3},{4,5},{6,7},{8,9},{10,11},{12,13},{14,15},{16,17},{18,19},{..., dimensions={0}, use_global_device_ids=true | all-gather | bytes 221184 | tf_op jit(solution)/shard_map/all_gather | solution.py:459
  46.3 1.8 %collective-permute-done.4 = f32[144,128]{1,0:T(8,128)S(1)} collective-permute-done((f32[144,128]{1,0:T(8,128)S(1)}, f32[144,128]{1,0:T(8,128)S(1)}, u32[]{:S(2)}, u32[]{:S(2)}) %collective-permute-start.4) | collective-permute-done | bytes 73760 | tf_op jit(solution)/shard_map/ppermute | solution.py:458
  48.2 2.5 %shard_map.46 = (f32[256,128]{1,0:T(8,128)}, f32[256,128]{1,0:T(8,128)}) custom-call(f32[512,128]{1,0:T(8,128)S(1)} %pad_maximum_fusion.fk_ref, f32[704,128]{1,0:T(8,128)S(1)} %get-tuple-element.35.refs_0_.own_ref, f32[256,128]{1,0:T(8,128)S(1)} %get-tuple-element.38.xl_ref, f32[256,128]{1,0:T(8,128)S(1)} %get-tuple-element.39.xr_ref, ...), custom_call_target="tpu_custom_call" | custom-call | tf_op jit(solution)/shard_map/pallas_call | solution.py:44
  (10 shorter events, 0.2 us)
Async XLA Ops:
  1.9 8.2 %collective-permute-start = (f32[96,128]{1,0:T(8,128)S(1)}, f32[96,128]{1,0:T(8,128)S(1)}, u32[]{:S(2)}, u32[]{:S(2)}) collective-permute-start(f32[96,128]{1,0:T(8,128)S(1)} %get-tuple-element.63), channel_id=1, source_target_pairs={{128,256},{256,128},{129,257},{257,129},{130,258},{258,130},{131,2... | collective-permute-start | bytes 147464 | tf_op jit(solution)/shard_map/ppermute | solution.py:458
  10.6 12.5 %collective-permute-start.1 = (f32[160,128]{1,0:T(8,128)S(1)}, f32[160,128]{1,0:T(8,128)S(1)}, u32[]{:S(2)}, u32[]{:S(2)}) collective-permute-start(f32[160,128]{1,0:T(8,128)S(1)} %get-tuple-element.55), channel_id=1, source_target_pairs={{4,8},{12,16},{20,24},{28,32},{36,40},{44,48},{52,56},{60,64},{68,... | collective-permute-start | bytes 245768 | tf_op jit(solution)/shard_map/ppermute | solution.py:458
  23.5 6.3 %collective-permute-start.2 = (f32[256,128]{1,0:T(8,128)S(1)}, f32[256,128]{1,0:T(8,128)S(1)}, u32[]{:S(2)}, u32[]{:S(2)}) collective-permute-start(f32[256,128]{1,0:T(8,128)S(1)} %get-tuple-element.49), channel_id=1, source_target_pairs={{1,2},{2,1},{5,6},{6,5},{9,10},{10,9},{13,14},{14,13},{17,18},{18,... | collective-permute-start | bytes 393224 | tf_op jit(solution)/shard_map/ppermute | solution.py:458
  31.9 10.2 %collective-permute-start.3 = (f32[88,128]{1,0:T(8,128)S(1)}, f32[88,128]{1,0:T(8,128)S(1)}, u32[]{:S(2)}, u32[]{:S(2)}) collective-permute-start(f32[88,128]{1,0:T(8,128)S(1)} %get-tuple-element.65), channel_id=1, source_target_pairs={{4,8},{12,16},{20,24},{28,32},{36,40},{44,48},{52,56},{60,64},{68,... | collective-permute-start | bytes 135176 | tf_op jit(solution)/shard_map/ppermute | solution.py:458
  42.5 5.7 %collective-permute-start.4 = (f32[144,128]{1,0:T(8,128)S(1)}, f32[144,128]{1,0:T(8,128)S(1)}, u32[]{:S(2)}, u32[]{:S(2)}) collective-permute-start(f32[144,128]{1,0:T(8,128)S(1)} %get-tuple-element.57), channel_id=1, source_target_pairs={{1,2},{2,1},{5,6},{6,5},{9,10},{10,9},{13,14},{14,13},{17,18},{18,... | collective-permute-start | bytes 221192 | tf_op jit(solution)/shard_map/ppermute | solution.py:458
